TPU v7x, 32 devices: a whole 2x2x4 slice. The times are simulated.
32 devices in a mesh: side: 2 (over core), grp: 16 (over z, y, x).
Axes of the slice: x: 2, y: 2, z: 4, core: 2. Of those that a mesh axis runs over, the one named last changes fastest.
Arguments:
- query_heads: bfloat16 [256, 8192], P('grp'), may hold values from -160 to 160
- key_cache: bfloat16 [256, 128, 512], P('grp'), may hold values from -4 to 4
- value_cache: bfloat16 [256, 128, 512], P('grp'), may hold values from -6 to 6
- cache_lengths: int32 [256], P('grp'), may hold values from 2 to 128, as said below
- out_weight: bfloat16 [8192, 4096], P(None, 'grp'), may hold values from -0.0625 to 0.0625
- residual: bfloat16 [256, 4096], P('grp'), may hold values from -4 to 4
- norm_gain: float32 [4096], replicated, may hold values from 0.5 to 1.5
- expert_ids: int32 [256, 8], P('grp'), may hold values from 0 to 15, all different within a row; in each aligned block of 16 rows (0 to 15, 16 to 31, ...) at most 16 rows name the same one
- route_weights: float32 [256, 8], P('grp'), may hold values from 0.05 to 0.25
- gate_up: bfloat16 [16, 4096, 1536], P('grp'), may hold values from -0.09375 to 0.09375
- down_weight: bfloat16 [16, 768, 4096], P('grp'), may hold values from -0.21875 to 0.21875
Outputs:
- layer_out: bfloat16 [256, 4096], P('grp', 'side')
Inputs may be any that keep to these rules, and one draw needn't show every extreme that they name: `cache_lengths`: at least one session has 128 live positions. `expert_ids`: each row names 8 different experts; among the 16 sessions of one index of grp (aligned blocks of rows) no expert is named by more than 16 rows, a bound that some block reaches.
All inputs are finite; a program needn't handle non-finite values.
Results may differ from a plain program's by a relative error of at most 0.0055.
Values may be sent and summed in bfloat16 or wider, within the bound.
No kernel may reach another device: no remote copies, remote signals or barrier semaphores. Data moves between devices by JAX's collectives and lax.ppermute only.
A program may use at most 128 MiB of HBM per device.

v0:
```python
import jax
import jax.numpy as jnp
from jax import lax
from jax.sharding import PartitionSpec as P

HQ = 64
KVH = 4
HD = 128
HID = 768
TOPK = 8
CTX = 128


def from_behind(value, axis, steps):
    count = lax.axis_size(axis)
    leading, last = (max(0, -steps), min(count, count - steps))
    return lax.ppermute(value, axis, [(source, source + steps) for source in range(leading, last)])


def partner(block, axis, apart):
    count = lax.axis_size(axis)
    route = []
    for low in range(count):
        high = low | 1 << apart
        if high != low and high < count:
            route += [(low, high), (high, low)]
    return lax.ppermute(block, axis, route)


def slots_of(expert_block, groups):
    flat_ids = expert_block.reshape(-1)
    onehot = (flat_ids[:, None] == jnp.arange(groups, dtype=jnp.int32)[None, :]).astype(jnp.int32)
    running = jnp.cumsum(onehot, axis=0)
    return jnp.sum(onehot * running, axis=1) - 1


def attend(query_heads, key_cache, value_cache, cache_lengths):
    session_count = query_heads.shape[0]
    group_size = HQ // KVH
    queries = query_heads.reshape(session_count, KVH, group_size, HD)
    key_heads = key_cache.reshape(session_count, CTX, KVH, HD)
    value_heads = value_cache.reshape(session_count, CTX, KVH, HD)
    scores = jnp.einsum(
        "skgd,stkd->skgt", queries, key_heads, preferred_element_type=jnp.float32
    ) * HD ** (-0.5)
    visible = jnp.arange(CTX, dtype=jnp.int32)[None, :] < cache_lengths[:, None]
    scores = jnp.where(visible[:, None, None, :], scores, -1e30)
    row_max = jnp.max(scores, axis=-1, keepdims=True)
    lifted = jnp.exp(scores - row_max)
    softmax_weights = (lifted / jnp.sum(lifted, axis=-1, keepdims=True)).astype(jnp.bfloat16)
    attended = jnp.einsum(
        "skgt,stkd->skgd", softmax_weights, value_heads, preferred_element_type=jnp.float32
    )
    return attended.astype(jnp.bfloat16).reshape(session_count, HQ * HD)


def expert_rows(token_rows, expert_gate_up, expert_down):
    both_halves = jnp.dot(token_rows, expert_gate_up, preferred_element_type=jnp.float32)
    activated = (jax.nn.silu(both_halves[:, :HID]) * both_halves[:, HID:]).astype(jnp.bfloat16)
    return jnp.dot(activated, expert_down, preferred_element_type=jnp.float32).astype(jnp.bfloat16)


def body(
    query_heads,
    key_cache,
    value_cache,
    cache_lengths,
    out_weight,
    residual,
    norm_gain,
    expert_ids,
    route_weights,
    gate_up,
    down_weight,
):
    side_index = lax.axis_index("side")
    on_attention = side_index == 0
    groups = lax.axis_size("grp")
    session_count = query_heads.shape[0]
    model_width = residual.shape[1]
    capacity = max(2, 2 * session_count * TOPK // groups)
    total_slots = groups * capacity
    attn_out = lax.cond(
        on_attention,
        attend,
        lambda *operands: jnp.zeros((session_count, HQ * HD), jnp.bfloat16),
        query_heads,
        key_cache,
        value_cache,
        cache_lengths,
    )
    columns = jnp.dot(
        lax.all_gather(attn_out, "grp", axis=0, tiled=True),
        out_weight,
        preferred_element_type=jnp.float32,
    )
    attn_proj = lax.all_to_all(columns, "grp", split_axis=0, concat_axis=1, tiled=True)
    hidden = residual.astype(jnp.float32) + attn_proj
    scaling = lax.rsqrt(jnp.mean(hidden * hidden, axis=-1, keepdims=True) + 1e-06)
    normed = (hidden * scaling * norm_gain).astype(jnp.bfloat16)
    slot_index = slots_of(expert_ids, groups)
    position = expert_ids.reshape(-1) * capacity + slot_index
    placing = jnp.arange(total_slots, dtype=jnp.int32)[:, None] == position[None, :]
    dispatch = jnp.sum(
        placing.reshape(total_slots, session_count, TOPK).astype(jnp.bfloat16), axis=2
    )
    outgoing_rows = jnp.dot(dispatch, normed, preferred_element_type=jnp.float32).astype(
        jnp.bfloat16
    )
    outgoing_rows = outgoing_rows.reshape(groups, capacity, model_width)
    expert_gate_up = gate_up[0]
    expert_down = down_weight[0]

    def compute(token_slots):
        flat_rows = token_slots.reshape(-1, model_width)
        return expert_rows(flat_rows, expert_gate_up, expert_down).reshape(token_slots.shape)

    crossed = from_behind(outgoing_rows, "side", 1)
    results = lax.cond(
        on_attention,
        lambda operands: jnp.zeros_like(operands),
        compute,
        lax.all_to_all(crossed, "grp", split_axis=0, concat_axis=0, tiled=True),
    )
    returned = lax.all_to_all(results, "grp", split_axis=0, concat_axis=0, tiled=True)
    weighting = (position[:, None] == jnp.arange(total_slots, dtype=jnp.int32)[None, :]).astype(
        jnp.float32
    )
    weighting = weighting * route_weights.reshape(-1)[:, None]
    weighting = jnp.sum(weighting.reshape(session_count, TOPK, total_slots), axis=1)
    mixture = jnp.dot(
        weighting,
        returned.reshape(total_slots, model_width).astype(jnp.float32),
        precision=lax.Precision.HIGHEST,
    )
    half_width = model_width // 2
    outgoing = jnp.where(on_attention, hidden[:, half_width:], mixture[:, :half_width])
    incoming = partner(outgoing, "side", 0)
    combined = jnp.where(
        on_attention, hidden[:, :half_width] + incoming, incoming + mixture[:, half_width:]
    )
    return combined.astype(jnp.bfloat16)


def solution(mesh):
    return jax.shard_map(
        body,
        mesh=mesh,
        in_specs=(
            P("grp", None),
            P("grp", None, None),
            P("grp", None, None),
            P("grp"),
            P(None, "grp"),
            P("grp", None),
            P(),
            P("grp", None),
            P("grp", None),
            P("grp", None, None),
            P("grp", None, None),
        ),
        out_specs=P("grp", "side"),
        check_vma=False,
    )
```

profile of v0, /device:TPU:0, one launch (start us, length us, event | category | flops | bytes accessed | tf_op | source)
XLA Modules:
  0.0 233.6 jit_solution(11014379530624704253)
XLA Ops:
  6.5 0.0 all-gather.2.cloned.1.call-start
  6.5 0.0 copy-start.4
  6.5 7.1 %conditional.2 = (bf16[16,8192]{1,0:T(8,128)(2,1)S(1)}) conditional(s32[]{:T(128)} %convert_element_type.39, () %tuple.17, (s32[16]{0:T(128)}, bf16[16,8192]{1,0:T(8,128)(2,1)}, bf16[16,128,512]{2,1,0:T(8,128)(2,1)}, bf16[16,128,512]{2,1,0:T(8,128)(2,1)}) %tuple.18), branch_computations={%region_0.0_spmd, %region_1.4_spmd} | conditional | flops 68160768 | bytes 15741028 | solution.py:83
  6.5 1.1 copy.38
  7.7 0.7 iota_compare_fusion
  8.4 2.8 %fusion.12 = f32[16,4,16,128]{3,2,1,0:T(8,128)S(1)} fusion(bf16[16,4,16,128]{3,2,1,0:T(8,128)(2,1)S(1)} %bitcast.57, pred[16,128]{1,0:T(8,128)(4,1)S(1)} %iota_compare_fusion, bf16[16,128,512]{2,1,0:T(8,128)(2,1)} %get-tuple-element.40), kind=kOutput, calls=%fused_computation.10 | convolution fusion | flops 33816576 | bytes 2885632 | tf_op jit(solution)/shard_map/cond/branch_1_fun/skgd,stkd->skgt/dot_general | solution.py:43
  11.2 0.4 fusion.38
  11.6 0.0 copy-done.7
  11.6 1.8 fusion.15
  13.5 0.2 copy.56
  13.6 0.0 copy-start.1
  13.7 0.7 copy-done.1
  14.3 0.0 all-gather.2.cloned.1.call-update
  14.4 0.0 copy-done.4
  14.4 0.1 copy.33
  14.4 0.1 eq.47
  14.5 0.1 fusion.37
  14.6 0.2 reduce_window_sum.11
  14.8 0.2 select_reduce_fusion.1
  15.0 0.0 copy-start.2
  15.0 0.0 copy-start.3
  15.0 78.3 %all-gather.2.cloned.1.call-done = bf16[256,8192]{1,0:T(8,128)(2,1)} async-done(((bf16[16,8192]{1,0:T(8,128)(2,1)}), bf16[256,8192]{1,0:T(8,128)(2,1)}) %all-gather.2.cloned.1.call-update) | async-done | bytes 4194320 | tf_op jit(solution)/shard_map/all_gather | solution.py:93
  93.3 5.4 %fusion.39 = f32[256,256]{1,0:T(8,128)} fusion(bf16[256,8192]{1,0:T(8,128)(2,1)} %all-gather.2.cloned.1.call-done, bf16[8192,256]{1,0:T(8,128)(2,1)} %param.19), kind=kOutput, calls=%fused_computation.49 | convolution fusion | flops 1073741824 | bytes 8650752 | tf_op jit(solution)/shard_map/dot_general | solution.py:92
  98.7 4.2 %all-to-all-start = ((f32[16,16,256]{2,1,0:T(8,128)}), f32[16,16,256]{2,1,0:T(8,128)S(1)}, u32[]{:S(2)}, u32[]{:S(2)}) async-start(f32[16,16,256]{2,1,0:T(8,128)} %bitcast.4), calls=%async_computation | async-start | bytes 524288 | tf_op jit(solution)/shard_map/all_to_all | solution.py:97
  102.9 0.1 sub.15
  103.0 0.1 fusion.36
  103.2 9.6 %all-to-all-done = f32[16,16,256]{2,1,0:T(8,128)S(1)} async-done(((f32[16,16,256]{2,1,0:T(8,128)}), f32[16,16,256]{2,1,0:T(8,128)S(1)}, u32[]{:S(2)}, u32[]{:S(2)}) %all-to-all-start) | async-done | bytes 262176 | tf_op jit(solution)/shard_map/all_to_all | solution.py:97
  112.8 0.0 copy-done.2
  112.8 0.2 multiply_reduce_fusion
  113.0 0.0 copy-done.3
  113.0 0.8 convolution_convert_fusion
  113.8 2.6 %collective-permute-start = (bf16[16,16,4096]{2,1,0:T(8,128)(2,1)S(1)}, bf16[16,16,4096]{2,1,0:T(8,128)(2,1)}, u32[]{:S(2)}, u32[]{:S(2)}) collective-permute-start(bf16[16,16,4096]{2,1,0:T(8,128)(2,1)S(1)} %bitcast.55), channel_id=1, source_target_pairs={{0,16},{1,17},{2,18},{3,19},{4,20},{5,21},{6,22},{7,23},{8,24},{9,... | collective-permute-start | bytes 6291464 | tf_op jit(solution)/shard_map/ppermute | solution.py:17
  116.4 2.6 %collective-permute-done = bf16[16,16,4096]{2,1,0:T(8,128)(2,1)} collective-permute-done((bf16[16,16,4096]{2,1,0:T(8,128)(2,1)S(1)}, bf16[16,16,4096]{2,1,0:T(8,128)(2,1)}, u32[]{:S(2)}, u32[]{:S(2)}) %collective-permute-start) | collective-permute-done | bytes 2097184 | tf_op jit(solution)/shard_map/ppermute | solution.py:17
  119.0 3.7 %all-to-all-start.1 = ((bf16[16,16,4096]{2,1,0:T(8,128)(2,1)}), bf16[16,16,4096]{2,1,0:T(8,128)(2,1)S(1)}, u32[]{:S(2)}, u32[]{:S(2)}) async-start(bf16[16,16,4096]{2,1,0:T(8,128)(2,1)} %collective-permute-done), calls=%async_computation.1 | async-start | bytes 4194304 | tf_op jit(solution)/shard_map/all_to_all | solution.py:123
  122.7 43.0 %all-to-all-done.1 = bf16[16,16,4096]{2,1,0:T(8,128)(2,1)S(1)} async-done(((bf16[16,16,4096]{2,1,0:T(8,128)(2,1)}), bf16[16,16,4096]{2,1,0:T(8,128)(2,1)S(1)}, u32[]{:S(2)}, u32[]{:S(2)}) %all-to-all-start.1) | async-done | bytes 2097184 | tf_op jit(solution)/shard_map/all_to_all | solution.py:123
  165.7 0.2 conditional.3
  165.7 0.2 broadcast.75
  165.9 0.0 copy-start
  165.9 1.3 copy-done
  167.3 11.6 %all-to-all-start.2 = ((bf16[16,16,4096]{2,1,0:T(8,128)(2,1)}), bf16[16,16,4096]{2,1,0:T(8,128)(2,1)S(1)}, u32[]{:S(2)}, u32[]{:S(2)}) async-start(bf16[16,16,4096]{2,1,0:T(8,128)(2,1)} %copy-done), calls=%async_computation.2 | async-start | bytes 4194304 | tf_op jit(solution)/shard_map/all_to_all | solution.py:125
  178.9 0.0 copy-done.5
  178.9 0.1 copy.35
  179.0 0.1 select_reduce_fusion
  179.1 40.8 %all-to-all-done.2 = bf16[16,16,4096]{2,1,0:T(8,128)(2,1)S(1)} async-done(((bf16[16,16,4096]{2,1,0:T(8,128)(2,1)}), bf16[16,16,4096]{2,1,0:T(8,128)(2,1)S(1)}, u32[]{:S(2)}, u32[]{:S(2)}) %all-to-all-start.2) | async-done | bytes 2097184 | tf_op jit(solution)/shard_map/all_to_all | solution.py:125
  219.9 0.9 fusion.40
  220.8 4.3 %collective-permute-start.1 = (f32[16,2048]{1,0:T(8,128)S(1)}, f32[16,2048]{1,0:T(8,128)S(1)}, u32[]{:S(2)}, u32[]{:S(2)}) collective-permute-start(f32[16,2048]{1,0:T(8,128)S(1)} %slice_select_fusion), channel_id=1, source_target_pairs={{0,16},{16,0},{1,17},{17,1},{2,18},{18,2},{3,19},{19,3},{4,20},{20... | collective-permute-start | bytes 393224 | tf_op jit(solution)/shard_map/ppermute | solution.py:27
  225.1 1.0 collective-permute-done.1
  226.1 0.7 fusion.32
  (7 shorter events, 0.1 us)
Async XLA Ops:
  6.5 86.8 %all-gather.2.cloned.1.call-start = ((), (), s32[]{:S(2)}) async-start(), calls=%async_computation.3 | async-start | bytes 4456448 | tf_op jit(solution)/shard_map/all_gather | solution.py:93
  6.5 7.8 %copy-start.4 = (s32[16,8]{0,1:T(8,128)S(1)}, s32[16,8]{0,1:T(8,128)}, u32[]{:S(2)}) copy-start(s32[16,8]{0,1:T(8,128)} %param.22) | copy-start | bytes 1540
  6.5 5.1 %copy-start.7 = (bf16[16,128,512]{2,1,0:T(8,128)(2,1)S(1)}, bf16[16,128,512]{2,1,0:T(8,128)(2,1)}, u32[]{:S(2)}) copy-start(bf16[16,128,512]{2,1,0:T(8,128)(2,1)} %get-tuple-element.41) | copy-start | bytes 6291460 | tf_op jit(solution)/shard_map/cond
  13.6 0.7 copy-start.1
  15.0 97.9 %copy-start.2 = (bf16[16,4096]{1,0:T(8,128)(2,1)S(1)}, bf16[16,4096]{1,0:T(8,128)(2,1)}, u32[]{:S(2)}) copy-start(bf16[16,4096]{1,0:T(8,128)(2,1)} %param.20) | copy-start | bytes 393220
  15.0 98.0 %copy-start.3 = (f32[4096]{0:T(1024)S(1)}, f32[4096]{0:T(1024)}, u32[]{:S(2)}) copy-start(f32[4096]{0:T(1024)} %param.21) | copy-start | bytes 49156
  98.7 14.1 %all-to-all-start = ((f32[16,16,256]{2,1,0:T(8,128)}), f32[16,16,256]{2,1,0:T(8,128)S(1)}, u32[]{:S(2)}, u32[]{:S(2)}) async-start(f32[16,16,256]{2,1,0:T(8,128)} %bitcast.4), calls=%async_computation | async-start | bytes 524288 | tf_op jit(solution)/shard_map/all_to_all | solution.py:97
  113.8 5.2 %collective-permute-start = (bf16[16,16,4096]{2,1,0:T(8,128)(2,1)S(1)}, bf16[16,16,4096]{2,1,0:T(8,128)(2,1)}, u32[]{:S(2)}, u32[]{:S(2)}) collective-permute-start(bf16[16,16,4096]{2,1,0:T(8,128)(2,1)S(1)} %bitcast.55), channel_id=1, source_target_pairs={{0,16},{1,17},{2,18},{3,19},{4,20},{5,21},{6,22},{7,23},{8,24},{9,... | collective-permute-start | bytes 6291464 | tf_op jit(solution)/shard_map/ppermute | solution.py:17
  119.0 46.7 %all-to-all-start.1 = ((bf16[16,16,4096]{2,1,0:T(8,128)(2,1)}), bf16[16,16,4096]{2,1,0:T(8,128)(2,1)S(1)}, u32[]{:S(2)}, u32[]{:S(2)}) async-start(bf16[16,16,4096]{2,1,0:T(8,128)(2,1)} %collective-permute-done), calls=%async_computation.1 | async-start | bytes 4194304 | tf_op jit(solution)/shard_map/all_to_all | solution.py:123
  165.9 1.4 copy-start
  167.3 11.6 %copy-start.5 = (f32[16,8]{0,1:T(8,128)S(1)}, f32[16,8]{0,1:T(8,128)}, u32[]{:S(2)}) copy-start(f32[16,8]{0,1:T(8,128)} %param.23) | copy-start | bytes 1540
  167.3 52.6 %all-to-all-start.2 = ((bf16[16,16,4096]{2,1,0:T(8,128)(2,1)}), bf16[16,16,4096]{2,1,0:T(8,128)(2,1)S(1)}, u32[]{:S(2)}, u32[]{:S(2)}) async-start(bf16[16,16,4096]{2,1,0:T(8,128)(2,1)} %copy-done), calls=%async_computation.2 | async-start | bytes 4194304 | tf_op jit(solution)/shard_map/all_to_all | solution.py:125
  220.8 5.2 %collective-permute-start.1 = (f32[16,2048]{1,0:T(8,128)S(1)}, f32[16,2048]{1,0:T(8,128)S(1)}, u32[]{:S(2)}, u32[]{:S(2)}) collective-permute-start(f32[16,2048]{1,0:T(8,128)S(1)} %slice_select_fusion), channel_id=1, source_target_pairs={{0,16},{16,0},{1,17},{17,1},{2,18},{18,2},{3,19},{19,3},{4,20},{20... | collective-permute-start | bytes 393224 | tf_op jit(solution)/shard_map/ppermute | solution.py:27
Sparse Core Ops, SparseCore 0:
  14.5 78.7 all-gather.1
where the time goes:
time: 238 us; the launch traced here: 234 us
  waiting for transfers between devices  175 us (74%)
  starting transfers between devices  26.4 us (11%)
  between operations  13.5 us (6%)
  matrix products  11.7 us (5%)
  local copies, waits for them, and re-layouts  3.93 us (2%)
  other arithmetic  2.68 us (1%)
    all_gather x1, waiting for transfers between devices, body(): lax.all_gather(attn_out, 'grp', axis=0, tiled=True)  78.3 us
    all_to_all x1, waiting for transfers between devices, body(): lax.all_to_all(crossed, 'grp', split_axis=0, concat_axis=0, tiled=True)  43 us
    all_to_all x1, waiting for transfers between devices, body(): lax.all_to_all(results, 'grp', split_axis=0, concat_axis=0, tiled=True)  40.8 us
    all_to_all x1, starting transfers between devices, body(): lax.all_to_all(results, 'grp', split_axis=0, concat_axis=0, tiled=True)  11.6 us
    all_to_all x1, waiting for transfers between devices, body(): lax.all_to_all(columns, 'grp', split_axis=0, concat_axis=1, tiled=True)  9.65 us
    dot_general x1, matrix products, body(): jnp.dot(lax.all_gather(attn_out, 'grp', axis=0, tiled=True), out_weight,...  5.4 us
  transfers between devices with their start and end apart: 6, of which 6 were waited for; matrix products, arithmetic and copies ran while one was open for 0% of the time, Pallas kernels for 0%

commit v1 on v0

v1 whole, which is shorter than its diff:
```python
import functools

import jax
import jax.numpy as jnp
from jax import lax
from jax.experimental import pallas as pl
from jax.experimental.pallas import tpu as pltpu
from jax.sharding import PartitionSpec as P

HQ = 64
KVH = 4
HD = 128
HID = 768
TOPK = 8
CTX = 128
GROUP = HQ // KVH
EPS = 1e-06
CHUNK = 256
LANES = 128
MIB = 1 << 20


CHIPS = 16
PLANES = 4
PAIRS = ((0, 1), (2, 3))
BACK_PAIRS = ((0, 3), (1, 2))
ROUTING = LANES


def exchange(value, bits):
    return lax.ppermute(value, "grp", [(g, g ^ bits) for g in range(CHIPS)])


def piece_order(place, groups):
    if groups != CHIPS:
        return list(range(groups))
    return [place ^ n for n in range(CHIPS)]


def pair_order(place, groups, pairs):
    if groups != CHIPS:
        return list(range(groups))
    return [place ^ (4 * k + f) for pair in pairs for f in range(4) for k in pair]


def after(value, *done):
    return lax.optimization_barrier((value, *done))[0]


def gather(planes):
    own = planes[0]
    z1, z2 = (exchange(planes[k], 4 * k) for k in (1, 2))
    x0, y0 = (exchange(own, f) for f in (1, 2))
    z3 = exchange(after(planes[3], z2), 12)
    x1 = exchange(x0, 4)
    c0 = exchange(y0, 1)
    y1 = exchange(after(z1, y0), 2)
    x2, y2 = (exchange(after(z2, x0, y0, z1), f) for f in (1, 2))
    c1 = exchange(c0, 4)
    c2 = exchange(after(y2, y1, x2, z3), 1)
    d3, x3, y3 = (exchange(after(z3, x1, y1, x2), f) for f in (3, 1, 2))
    return [own, x0, y0, c0, z1, x1, y1, c1, z2, x2, y2, c2, z3, x3, y3, d3]


BY_NEXT_PLANE = (5, 7)


def gather_pairs(piece):
    column = [piece] + [exchange(piece, 4 * k) for k in range(1, PLANES)]
    near, far = (jnp.stack([column[k] for k in pair]) for pair in PAIRS)
    far = after(far, near)
    nears = [exchange(near, f) if f else near for f in range(4)]
    fars = [exchange(far, f) if f else far for f in range(4)]
    return nears, fars


def add(*terms):
    return sum(t.astype(jnp.float32) for t in terms).astype(jnp.bfloat16)


def scatter_sum(first, second):
    first = add(first[0], *[exchange(first[f], f) for f in (3, 1, 2)])
    second = add(second[0], *[exchange(second[f], f) for f in (3, 1, 2)])
    terms = [first[0], exchange(first[1], 12), exchange(second[0], 4), exchange(second[1], 8)]
    return sum(t.astype(jnp.float32) for t in terms)


def attend_kernel(
    planes, ids_hbm, route_hbm, len_hbm, g_hbm, r_hbm, q_hbm, k_hbm, v_hbm, *refs
):
    o_refs = refs[: max(1, planes)]
    gain_ref = refs[max(1, planes)]
    o_ref = o_refs[0]
    len_ref, ids_ref, route_ref, tail_ref, r_ref, q_ref, k_ref, v_ref, sems = refs[-9:]
    side = lax.axis_index("side")
    half = k_ref.shape[0]
    rows = GROUP * half
    depth = HQ * HD // 2
    mine = [side * half + s for s in range(half)]
    small = [
        pltpu.make_async_copy(ids_hbm, ids_ref, sems.at[2 * half + 3]),
        pltpu.make_async_copy(route_hbm, route_ref, sems.at[2 * half + 4]),
    ]
    copies = [
        pltpu.make_async_copy(len_hbm, len_ref, sems.at[2 * half + 1]),
        pltpu.make_async_copy(q_hbm, q_ref, sems.at[2 * half]),
    ]
    copies += [
        pltpu.make_async_copy(k_hbm.at[mine[s]], k_ref.at[s], sems.at[s]) for s in range(half)
    ]
    late = [
        pltpu.make_async_copy(v_hbm.at[mine[s]], v_ref.at[s], sems.at[half + s])
        for s in range(half)
    ]
    late.append(pltpu.make_async_copy(r_hbm, r_ref, sems.at[2 * half + 2]))
    gain = g_hbm.at[lax.axis_index("grp")]
    late.append(pltpu.make_async_copy(gain, gain_ref, sems.at[2 * half + 5]))
    for copy in small + copies + late:
        copy.start()
    session = lax.broadcasted_iota(jnp.int32, (rows, CTX), 0) % half
    place = lax.broadcasted_iota(jnp.int32, (rows, CTX), 1)
    for copy in small:
        copy.wait()
    terms, rest = [], route_ref[...]
    for _ in range(3):
        terms.append(rest.astype(jnp.bfloat16).astype(jnp.float32))
        rest = rest - terms[-1]
    count = 2 * half
    tail_ref[...] = jnp.zeros_like(tail_ref)
    tail_ref[:, :count] = jnp.concatenate(terms[1:], axis=0)
    second = pltpu.roll(tail_ref[...], LANES // 2, axis=1)
    tail_ref[:, :count] = jnp.concatenate([ids_ref[...].astype(jnp.float32), terms[0]], axis=0)
    tail = jnp.where(
        lax.broadcasted_iota(jnp.int32, second.shape, 1) < LANES // 2, tail_ref[...], second
    ).astype(jnp.bfloat16)
    for ref in o_refs:
        ref[:, depth : depth + ROUTING] = tail

    for copy in copies:
        copy.wait()
    lives = [(session == s) & (place < len_ref[mine[s]]) for s in range(half)]
    spreads = []
    for kv in range(KVH):
        parts = []
        for h in range(kv * GROUP, (kv + 1) * GROUP):
            both = q_ref[:, h * HD : (h + 1) * HD].astype(jnp.float32)
            parts.append(jnp.where(side == 0, both[:half], both[half:]))
        queries = jnp.concatenate(parts, axis=0).astype(jnp.bfloat16)
        keys = k_ref[:, :, kv * HD : (kv + 1) * HD].reshape(half * CTX, HD)
        every = lax.dot_general(
            queries, keys, (((1,), (1,)), ((), ())), preferred_element_type=jnp.float32
        )
        scores = jnp.full((rows, CTX), -1e30, jnp.float32)
        for s in range(half):
            part = every[:, s * CTX : (s + 1) * CTX] * HD ** (-0.5)
            scores = jnp.where(lives[s], part, scores)
        lifted = jnp.exp(scores - jnp.max(scores, axis=-1, keepdims=True))
        weights = lifted / jnp.sum(lifted, axis=-1, keepdims=True)
        spreads.append(
            jnp.concatenate(
                [jnp.where(session == s, weights, 0.0).astype(jnp.bfloat16) for s in range(half)],
                axis=1,
            )
        )
    for copy in late:
        copy.wait()
    outs = []
    for kv in range(KVH):
        values = v_ref[:, :, kv * HD : (kv + 1) * HD].reshape(half * CTX, HD)
        outs.append(jnp.dot(spreads[kv], values, preferred_element_type=jnp.float32))
    later = KVH // 2
    for kv in range(later):
        for h in range(GROUP):
            pair = [out[h * half : (h + 1) * half] for out in (outs[kv], outs[kv + later])]
            both = jnp.concatenate(pair, axis=0).astype(jnp.bfloat16)
            for ref in o_refs:
                ref[:, (kv * GROUP + h) * HD : (kv * GROUP + h + 1) * HD] = both
    here = lax.axis_index("grp") // 4
    for k in range(planes):
        wide = r_ref.shape[1] // planes // 2
        parts = []
        for part in range(2):
            start = pl.multiple_of(((here ^ k) * 2 + part) * wide, wide)
            both = r_ref[:, pl.ds(start, wide)].astype(jnp.float32)
            parts.append(jnp.where(side == 0, both[:half], both[half:]))
        tail = jnp.concatenate(parts, axis=0).astype(jnp.bfloat16)
        o_refs[k][:, depth + ROUTING : depth + ROUTING + wide] = tail
        if k == 1:
            o_ref[:, depth + ROUTING + wide :] = tail


def attend(
    groups,
    planes,
    query_heads,
    key_cache,
    value_cache,
    cache_lengths,
    expert_ids,
    route_weights,
    norm_gain,
    residual,
):
    sessions, width = residual.shape
    half = sessions // 2
    columns = width // groups
    hbm_spec = pl.BlockSpec(memory_space=pltpu.HBM)
    vmem_spec = pl.BlockSpec(memory_space=pltpu.VMEM)
    in_hbm = functools.partial(pltpu.with_memory_space_constraint, memory_space=pltpu.HBM)
    outs = max(1, planes)
    tail = width // planes // 2 if planes else 0
    carried = [HQ * HD // 2 + ROUTING + tail * (2 if k == 0 else 1) for k in range(outs)]
    return pl.pallas_call(
        functools.partial(attend_kernel, planes),
        in_specs=[hbm_spec] * 8,
        out_specs=[vmem_spec] * (outs + 1),
        out_shape=[jax.ShapeDtypeStruct((sessions, n), jnp.bfloat16) for n in carried]
        + [jax.ShapeDtypeStruct((1, columns), jnp.float32)],
        scratch_shapes=[
            pltpu.SMEM((sessions,), jnp.int32),
            pltpu.VMEM((TOPK, sessions), jnp.int32),
            pltpu.VMEM((TOPK, sessions), jnp.float32),
            pltpu.VMEM((sessions, ROUTING), jnp.float32),
            pltpu.VMEM((sessions, width), jnp.bfloat16),
            pltpu.VMEM((sessions, HQ * HD), jnp.bfloat16),
            pltpu.VMEM((half, CTX, KVH * HD), jnp.bfloat16),
            pltpu.VMEM((half, CTX, KVH * HD), jnp.bfloat16),
            pltpu.SemaphoreType.DMA((2 * half + 6,)),
        ],
        compiler_params=pltpu.CompilerParams(vmem_limit_bytes=8 * MIB),
        name="attend",
    )(
        in_hbm(expert_ids.T),
        in_hbm(route_weights.T),
        in_hbm(cache_lengths),
        in_hbm(norm_gain.reshape(groups, 1, columns)),
        in_hbm(residual),
        in_hbm(query_heads),
        in_hbm(key_cache),
        in_hbm(value_cache),
    )


def project_kernel(count, waits, *refs):
    refs = refs[waits:]
    pieces = refs[:count]
    *rest, w_ref, g_ref, y_ref, mix_ref, plain = refs[count:]
    blocks, sessions, _ = pieces[0].shape
    depth = w_ref.shape[0] // 2
    half = sessions // 2
    columns = w_ref.shape[1]
    groups = count * blocks
    side, place = lax.axis_index("side"), lax.axis_index("grp")
    order = piece_order(place, groups)
    total = None
    for part in range(2):
        chunk = depth // 4
        for j in range(4):
            a = jnp.concatenate(
                [
                    piece[:, :, j * chunk : (j + 1) * chunk].reshape(blocks * sessions, chunk)
                    for piece in pieces
                ],
                axis=0,
            )
            start = part * depth + j * chunk
            term = jnp.dot(a, w_ref[start : start + chunk], preferred_element_type=jnp.float32)
            got = term if j == 0 else got + term
        got = got.reshape(groups, 2, half, columns)[:, part]
        total = got if total is None else total + got
    own = lax.broadcasted_iota(jnp.int32, (half, LANES), 1) == side * half + (
        lax.broadcasted_iota(jnp.int32, (half, LANES), 0)
    )
    for n in range(count):
        for b in range(blocks):
            span = pl.ds(pl.multiple_of(order[n * blocks + b] * half, half), half)
            value = total[n * blocks + b]
            if not rest:
                start = depth + ROUTING + (2 * columns if n in BY_NEXT_PLANE else 0)
                tail = pieces[n][b, :, start : start + 2 * columns].astype(jnp.float32)
                spot = place % 4
                tail = jnp.where(spot // 2 == 0, tail[:half], tail[half:])
                value = value + jnp.where(spot % 2 == 0, tail[:, :columns], tail[:, columns:])
            plain[span, :] = value
            first = pieces[n][b, :, depth : depth + ROUTING].astype(jnp.float32)
            second = pltpu.roll(first, LANES // 2, axis=1)
            weights = first[half:] + (second[:half] + second[half:])
            chosen = jnp.where(first[:half] == place.astype(jnp.float32), weights, 0.0)
            chosen = jnp.sum(chosen, axis=0, keepdims=True)
            mix_ref[span, :] = jnp.sum(jnp.where(own, chosen, 0.0), axis=1, keepdims=True)
    hidden = plain[...]
    if rest:
        hidden = hidden + rest[0][...].astype(jnp.float32)
    y_ref[...] = (hidden * g_ref[...]).astype(jnp.bfloat16)


def project(pieces, out_weight, gain_columns, residual_columns=None, waits=()):
    count = len(pieces)
    columns = out_weight.shape[1]
    rows = sum(p.shape[0] for p in pieces) * pieces[0].shape[1] // 2
    rest = [] if residual_columns is None else [residual_columns]
    vmem_spec = pl.BlockSpec(memory_space=pltpu.VMEM)
    return pl.pallas_call(
        functools.partial(project_kernel, count, len(waits)),
        in_specs=[pl.BlockSpec(memory_space=pl.ANY)] * len(waits)
        + [vmem_spec] * (count + len(rest) + 2),
        out_specs=[vmem_spec] * 2,
        out_shape=[
            jax.ShapeDtypeStruct((rows, columns), jnp.bfloat16),
            jax.ShapeDtypeStruct((rows, 1), jnp.float32),
        ],
        scratch_shapes=[pltpu.VMEM((rows, columns), jnp.float32)],
        compiler_params=pltpu.CompilerParams(vmem_limit_bytes=8 * MIB),
        name="project",
    )(
        *waits,
        *pieces,
        *rest,
        pltpu.with_memory_space_constraint(out_weight, pltpu.VMEM),
        gain_columns,
    )


def take_chunk(store, g_ref, plain, hid_ref, chunk, chunks):
    side, place = lax.axis_index("side"), lax.axis_index("grp")
    value = store.astype(jnp.float32) * (1.0 / g_ref[chunk])
    plain[...] = value
    local, late = chunk % (chunks // 2), chunk // (chunks // 2)
    rows = pl.ds(pl.multiple_of(8 * ((side + late) % 2), 8), 8)
    columns = pl.ds(pl.multiple_of(local * CHUNK, CHUNK), CHUNK)
    hid_ref[rows, columns] = plain[pl.ds(pl.multiple_of(place * 8, 8), 8), :]
    squares = value * value
    return squares[:, :LANES] + squares[:, LANES:]


def weight_copies(gu_hbm, dst, sems, first):
    return [
        pltpu.make_async_copy(
            gu_hbm.at[0, pl.ds(pl.multiple_of((first + j) * CHUNK, CHUNK), CHUNK)],
            dst.at[pl.ds(j * CHUNK, CHUNK)],
            sems.at[j],
        )
        for j in range(dst.shape[0] // CHUNK)
    ]


def stage_kernel(_, gu_hbm, weights, done, sems):
    own = weights.shape[0] // CHUNK
    copies = weight_copies(
        gu_hbm, weights, sems, (lax.axis_index("grp") // (CHIPS // 2)) * own
    )
    for copy in copies:
        copy.start()
    done[...] = jnp.zeros_like(done)
    for copy in copies:
        copy.wait()


def stage(gate_up, arrived):
    half = gate_up.shape[1] // 2
    hbm_spec = pl.BlockSpec(memory_space=pltpu.HBM)
    vmem_spec = pl.BlockSpec(memory_space=pltpu.VMEM)
    return pl.pallas_call(
        stage_kernel,
        in_specs=[pl.BlockSpec(memory_space=pl.ANY), hbm_spec],
        out_specs=[vmem_spec] * 2,
        out_shape=[
            jax.ShapeDtypeStruct((half, 2 * HID), jnp.bfloat16),
            jax.ShapeDtypeStruct((8, LANES), jnp.float32),
        ],
        scratch_shapes=[pltpu.SemaphoreType.DMA((half // CHUNK,))],
        compiler_params=pltpu.CompilerParams(vmem_limit_bytes=2 * MIB),
        cost_estimate=pl.CostEstimate(
            flops=0, bytes_accessed=half * 4 * HID, transcendentals=0
        ),
        name="stage",
    )(arrived, pltpu.with_memory_space_constraint(gate_up, pltpu.HBM))


def near_kernel(count, *refs):
    pieces = refs[:count]
    weights, gu_hbm, g_ref, acc, sq_ref, hid_ref, kept, store, plain, sems = refs[count:]
    place = lax.axis_index("grp")
    chunks = g_ref.shape[0]
    own = chunks // 2
    first = (place // (CHIPS // 2)) * own
    copies = weight_copies(gu_hbm, kept, sems, own - first)
    for copy in copies:
        copy.start()
    order = pair_order(place, CHIPS, PAIRS)[:own]
    squares = jnp.zeros(sq_ref.shape, jnp.float32)
    for n in range(count):
        for b in range(2):
            chunk = order[2 * n + b]
            piece = pieces[n][b]
            store[chunk - first] = piece
            squares += take_chunk(piece, g_ref, plain, hid_ref, chunk, chunks)
    sq_ref[...] = squares
    y = jnp.concatenate([store[j] for j in range(own)], axis=1)
    for n in range(2 * HID // CHUNK):
        cols = slice(n * CHUNK, (n + 1) * CHUNK)
        acc[:, cols] = jnp.dot(y, weights[:, cols], preferred_element_type=jnp.float32)
    for copy in copies:
        copy.wait()


def near(pieces, staged, gate_up, norm_gain):
    rows = pieces[0].shape[1]
    width = gate_up.shape[1]
    chunks = width // CHUNK
    vmem_spec = pl.BlockSpec(memory_space=pltpu.VMEM)
    hbm_spec = pl.BlockSpec(memory_space=pltpu.HBM)
    count = len(pieces)
    return pl.pallas_call(
        functools.partial(near_kernel, count),
        in_specs=[vmem_spec] * (count + 1) + [hbm_spec, vmem_spec],
        out_specs=[vmem_spec] * 4,
        out_shape=[
            jax.ShapeDtypeStruct((rows, 2 * HID), jnp.float32),
            jax.ShapeDtypeStruct((rows, LANES), jnp.float32),
            jax.ShapeDtypeStruct((16, width // 2), jnp.float32),
            jax.ShapeDtypeStruct((width // 2, 2 * HID), jnp.bfloat16),
        ],
        scratch_shapes=[
            pltpu.VMEM((chunks // 2, rows, CHUNK), jnp.bfloat16),
            pltpu.VMEM((rows, CHUNK), jnp.float32),
            pltpu.SemaphoreType.DMA((chunks // 2,)),
        ],
        compiler_params=pltpu.CompilerParams(vmem_limit_bytes=6 * MIB),
        cost_estimate=pl.CostEstimate(
            flops=2 * rows * width * HID, bytes_accessed=width * 4 * HID, transcendentals=0
        ),
        name="near",
    )(
        *pieces,
        pltpu.with_memory_space_constraint(staged, pltpu.VMEM),
        pltpu.with_memory_space_constraint(gate_up, pltpu.HBM),
        norm_gain.reshape(chunks, 1, CHUNK),
    )


def expert_kernel(count, outs, resumed, *refs):
    pieces = refs[:count]
    gu_ref, dn_ref, g_ref, mix_ref = refs[count : count + 4]
    rest = refs[count + 4 :]
    if resumed:
        acc_ref, sq_ref, old_ref = rest[:3]
        rest = rest[3:]
    o_refs, (hid_ref, store, plain, first, second) = rest[:outs], rest[outs:]
    side, place = lax.axis_index("side"), lax.axis_index("grp")
    own, rows, _ = store.shape
    chunks = g_ref.shape[0]
    width = chunks * CHUNK
    groups = rows // 8
    blocks = groups // outs
    spans = pieces[0].shape[0]
    back = pair_order(place, groups, BACK_PAIRS)
    if resumed:
        order = pair_order(place, groups, PAIRS)[own:]
        base = own - (place // (CHIPS // 2)) * own
        squares = sq_ref[...]
        hid_ref[...] = old_ref[...]
    else:
        order, base = list(range(chunks)), 0
        squares = jnp.zeros((rows, LANES), jnp.float32)
    for n in range(count):
        for b in range(spans):
            chunk = order[n * spans + b]
            piece = pieces[n][b]
            store[chunk - base] = piece
            squares += take_chunk(piece, g_ref, plain, hid_ref, chunk, chunks)
    mean = jnp.sum(squares, axis=-1, keepdims=True) * (1.0 / width)
    scaling = lax.rsqrt(mean + EPS)
    y = jnp.concatenate([store[j] for j in range(own)], axis=1)
    activated = []
    for n in range(HID // CHUNK):
        halves = []
        for start in (0, HID):
            cols = slice(start + n * CHUNK, start + (n + 1) * CHUNK)
            value = jnp.dot(y, gu_ref[:, cols], preferred_element_type=jnp.float32)
            if resumed:
                value = value + acc_ref[:, cols]
            halves.append(value * scaling)
        gate, up = halves
        activated.append((gate / (1.0 + jnp.exp(-gate)) * up).astype(jnp.bfloat16))
    activated = jnp.concatenate(activated, axis=1)
    mix = mix_ref[...]
    wide = width // 8
    for j in range(4):
        results = [
            jnp.dot(
                activated,
                dn_ref[0, :, start + j * wide : start + (j + 1) * wide],
                preferred_element_type=jnp.float32,
            )
            * mix
            for start in (0, width // 2)
        ]
        first[...] = jnp.where(side == 0, results[0], results[1])
        second[...] = jnp.where(side == 0, results[1], results[0])
        for n in range(outs):
            for b in range(blocks):
                span = pl.ds(pl.multiple_of(back[n * blocks + b] * 8, 8), 8)
                o_refs[n][b, :, j * wide : (j + 1) * wide] = jnp.concatenate(
                    [first[span, :], second[span, :]], axis=0
                ).astype(jnp.bfloat16)


def experts(pieces, gate_up, down_weight, norm_gain, mix, outs, begun=()):
    rows = mix.shape[0]
    width = down_weight.shape[2]
    chunks = width // CHUNK
    groups = rows // 8
    vmem_spec = pl.BlockSpec(memory_space=pltpu.VMEM)
    count = len(pieces)
    in_vmem = functools.partial(pltpu.with_memory_space_constraint, memory_space=pltpu.VMEM)
    return pl.pallas_call(
        functools.partial(expert_kernel, count, outs, bool(begun)),
        in_specs=[vmem_spec] * (count + 4 + len(begun)),
        out_specs=[vmem_spec] * (outs + 1),
        out_shape=[jax.ShapeDtypeStruct((groups // outs, 16, width // 2), jnp.bfloat16)] * outs
        + [jax.ShapeDtypeStruct((16, width // 2), jnp.float32)],
        scratch_shapes=[
            pltpu.VMEM((gate_up.shape[0] // CHUNK, rows, CHUNK), jnp.bfloat16),
            pltpu.VMEM((rows, CHUNK), jnp.float32),
            pltpu.VMEM((rows, width // 8), jnp.float32),
            pltpu.VMEM((rows, width // 8), jnp.float32),
        ],
        compiler_params=pltpu.CompilerParams(vmem_limit_bytes=(8 if rows <= 128 else 24) * MIB),
        name="experts",
    )(
        *pieces,
        in_vmem(gate_up),
        in_vmem(down_weight),
        norm_gain.reshape(chunks, 1, CHUNK),
        mix,
        *begun,
    )


def body(
    query_heads,
    key_cache,
    value_cache,
    cache_lengths,
    out_weight,
    residual,
    norm_gain,
    expert_ids,
    route_weights,
    gate_up,
    down_weight,
):
    side = lax.axis_index("side")
    groups = lax.axis_size("grp")
    sessions, width = residual.shape
    half = sessions // 2
    rows = groups * half
    columns = width // groups
    arrays = (
        query_heads,
        key_cache,
        value_cache,
        cache_lengths,
        expert_ids,
        route_weights,
        norm_gain,
        residual,
    )
    if groups == CHIPS:
        *carried, gain = attend(groups, PLANES, *arrays)
        pieces = gather(carried)
        staged, done = stage(gate_up, pieces[11])
        y, mix = project([p[None] for p in pieces], out_weight, gain, waits=(done,))
        nears, fars = gather_pairs(y)
        *begun, kept = near(nears, staged, gate_up, norm_gain)
        *sums, hidden = experts(fars, kept, down_weight, norm_gain, mix, 8, begun)
        mixture = scatter_sum(sums[:4], sums[4:])
    else:
        own_residual = lax.dynamic_slice_in_dim(residual, side * half, half, axis=0)
        residual_columns = lax.all_to_all(
            own_residual.reshape(half, groups, columns).transpose(1, 0, 2),
            "grp",
            split_axis=0,
            concat_axis=0,
            tiled=True,
        ).reshape(rows, columns)
        attn_out, gain = attend(groups, 0, *arrays)
        pieces = lax.all_gather(attn_out, "grp", axis=0)
        y, mix = project([pieces], out_weight, gain, residual_columns)
        y_all = lax.all_gather(y, "grp", axis=0).transpose(1, 0, 2)
        y_chunks = y_all.reshape(rows, width // CHUNK, CHUNK).transpose(1, 0, 2)
        *sums, hidden = experts([y_chunks], gate_up[0], down_weight, norm_gain, mix, 1)
        sent = lax.all_to_all(sums[0], "grp", split_axis=0, concat_axis=0, tiled=True)
        mixture = jnp.sum(sent.astype(jnp.float32), axis=0)
    ready = (hidden + mixture).astype(jnp.bfloat16)
    mine, other = ready[:half], ready[half:]
    other = lax.ppermute(other, "side", [(0, 1), (1, 0)])
    return jnp.where(
        side == 0, jnp.concatenate([mine, other]), jnp.concatenate([other, mine])
    )


def solution(mesh):
    return jax.shard_map(
        body,
        mesh=mesh,
        in_specs=(
            P("grp", None),
            P("grp", None, None),
            P("grp", None, None),
            P("grp"),
            P(None, "grp"),
            P("grp", None),
            P(),
            P("grp", None),
            P("grp", None),
            P("grp", None, None),
            P("grp", None, None),
        ),
        out_specs=P("grp", "side"),
        check_vma=False,
    )
```

time: 238 us -> 81.5 us (0.34); the launches traced: 234 us -> 81.3 us
  waiting for transfers between devices: 175 us -> 20.2 us
  starting transfers between devices: 26.4 us -> 47.3 us
  between operations: 13.5 us -> 0.21 us
  Pallas kernels: 0 us -> 12.7 us
  matrix products: 11.7 us -> 0 us
  local copies, waits for them, and re-layouts: 3.93 us -> 0.04 us
    all_to_all x3 -> x0, waiting for transfers between devices: 93.4 us -> none  [the longest x1 43 us: body(): lax.all_to_all(crossed, 'grp', split_axis=0, concat_axis=0, tiled=True)]
    all_gather x1 -> x0, waiting for transfers between devices: 78.3 us -> none  [body(): lax.all_gather(attn_out, 'grp', axis=0, tiled=True)]
    ppermute x2 -> x34, starting transfers between devices: 6.91 us -> 47.3 us  [the longest x33 47.2 us: exchange(): return lax.ppermute(value, 'grp', [(g, g ^ bits) for g in range(CHIPS)])]
    all_to_all x3 -> x0, starting transfers between devices: 19.5 us -> none  [the longest x1 11.6 us: body(): lax.all_to_all(results, 'grp', split_axis=0, concat_axis=0, tiled=True)]
    ppermute x2 -> x34, waiting for transfers between devices: 3.54 us -> 20.2 us  [the longest x33 19 us: exchange(): return lax.ppermute(value, 'grp', [(g, g ^ bits) for g in range(CHIPS)])]
    pallas_call x0 -> x5, Pallas kernels: none -> 12.7 us  [the longest x1 3.79 us: near(): pl.pallas_call(functools.partial(near_kernel, count), in_specs=[vmem_spec...]
    dot_general x5 -> x0, matrix products: 11.7 us -> none  [the longest x1 5.4 us: body(): jnp.dot(lax.all_gather(attn_out, 'grp', axis=0, tiled=True), out_weight,...]
  transfers between devices with their start and end apart: 6 -> 34, of which waited for: 6 -> 17; matrix products, arithmetic and copies ran while one was open for 0% -> 0% of each run, Pallas kernels for 0% -> 8%
where the time goes in v1:
time: 81.5 us; the launch traced here: 81.3 us
  starting transfers between devices  47.3 us (58%)
  waiting for transfers between devices  20.2 us (25%)
  Pallas kernels  12.7 us (16%)
  other arithmetic  0.86 us (1%)
    ppermute x33, starting transfers between devices, exchange(): return lax.ppermute(value, 'grp', [(g, g ^ bits) for g in range(CHIPS)])  47.2 us
    ppermute x33, waiting for transfers between devices, exchange(): return lax.ppermute(value, 'grp', [(g, g ^ bits) for g in range(CHIPS)])  19 us
    pallas_call x1, Pallas kernels, near(): pl.pallas_call(functools.partial(near_kernel, count), in_specs=[vmem_spec...  3.79 us
    pallas_call x1, Pallas kernels, stage(): pl.pallas_call(stage_kernel, in_specs=[pl.BlockSpec(memory_space=pl.ANY),...  2.86 us
    pallas_call x1, Pallas kernels, attend(): pl.pallas_call(functools.partial(attend_kernel, planes), in_specs=[hbm_sp...  2.62 us
    pallas_call x1, Pallas kernels, experts(): pl.pallas_call(functools.partial(expert_kernel, count, outs, bool(begun))...  2.2 us
  transfers between devices with their start and end apart: 34, of which 17 were waited for; matrix products, arithmetic and copies ran while one was open for 0% of the time, Pallas kernels for 8%

profile of v1, /device:TPU:0, one launch (start us, length us, event | category | flops | bytes accessed | tf_op | source)
XLA Modules:
  0.0 81.3 jit_solution(13712124448437992809)
XLA Ops:
  0.0 2.6 %attend.1 = (bf16[16,5248]{1,0:T(8,128)(2,1)S(1)}, bf16[16,4736]{1,0:T(8,128)(2,1)S(1)}, bf16[16,4736]{1,0:T(8,128)(2,1)S(1)}, bf16[16,4736]{1,0:T(8,128)(2,1)S(1)}, f32[1,256]{1,0:T(1,128)S(1)}) custom-call(s32[8,16]{1,0:T(8,128)} %bitcast.59, f32[8,16]{1,0:T(8,128)} %bitcast.60, s32[16]{0:T(128)} %len_hbm.1, f32[16,1,256]{2,1,0:T(1,128)} %bitcast.52, ...), custom_call_target="tpu_custom_call" | custom-call | tf_op jit(solution)/shard_map/attend/pallas_call | solution.py:213
  2.6 4.1 %collective-permute-start = (bf16[16,4736]{1,0:T(8,128)(2,1)S(1)}, bf16[16,4736]{1,0:T(8,128)(2,1)S(1)}, u32[]{:S(2)}, u32[]{:S(2)}) collective-permute-start(bf16[16,4736]{1,0:T(8,128)(2,1)S(1)} %get-tuple-element.33), channel_id=1, source_target_pairs={{0,8},{1,9},{2,10},{3,11},{4,12},{5,13},{6,14},{7,15},{8,0},{9,1},... | collective-permute-start | bytes 454664 | tf_op jit(solution)/shard_map/ppermute | solution.py:31
  6.7 1.5 %collective-permute-start.2 = (bf16[16,5248]{1,0:T(8,128)(2,1)S(1)}, bf16[16,5248]{1,0:T(8,128)(2,1)S(1)}, u32[]{:S(2)}, u32[]{:S(2)}) collective-permute-start(bf16[16,5248]{1,0:T(8,128)(2,1)S(1)} %get-tuple-element.34), channel_id=1, source_target_pairs={{0,2},{1,3},{2,0},{3,1},{4,6},{5,7},{6,4},{7,5},{8,10},{9,11},{10,... | collective-permute-start | bytes 503816 | tf_op jit(solution)/shard_map/ppermute | solution.py:31
  8.3 1.5 %collective-permute-start.1 = (bf16[16,5248]{1,0:T(8,128)(2,1)S(1)}, bf16[16,5248]{1,0:T(8,128)(2,1)S(1)}, u32[]{:S(2)}, u32[]{:S(2)}) collective-permute-start(bf16[16,5248]{1,0:T(8,128)(2,1)S(1)} %get-tuple-element.34), channel_id=1, source_target_pairs={{0,1},{1,0},{2,3},{3,2},{4,5},{5,4},{6,7},{7,6},{8,9},{9,8},{10,11... | collective-permute-start | bytes 503816 | tf_op jit(solution)/shard_map/ppermute | solution.py:31
  9.7 1.6 %collective-permute-start.3 = (bf16[16,4736]{1,0:T(8,128)(2,1)S(1)}, bf16[16,4736]{1,0:T(8,128)(2,1)S(1)}, u32[]{:S(2)}, u32[]{:S(2)}) collective-permute-start(bf16[16,4736]{1,0:T(8,128)(2,1)S(1)} %get-tuple-element.35), channel_id=1, source_target_pairs={{0,4},{1,5},{2,6},{3,7},{4,0},{5,1},{6,2},{7,3},{8,12},{9,13},{10,... | collective-permute-start | bytes 454664 | tf_op jit(solution)/shard_map/ppermute | solution.py:31
  11.3 2.7 %collective-permute-done = bf16[16,4736]{1,0:T(8,128)(2,1)S(1)} collective-permute-done((bf16[16,4736]{1,0:T(8,128)(2,1)S(1)}, bf16[16,4736]{1,0:T(8,128)(2,1)S(1)}, u32[]{:S(2)}, u32[]{:S(2)}) %collective-permute-start) | collective-permute-done | bytes 151584 | tf_op jit(solution)/shard_map/ppermute | solution.py:31
  14.0 3.5 %collective-permute-start.7 = (bf16[16,4736]{1,0:T(8,128)(2,1)S(1)}, bf16[16,4736]{1,0:T(8,128)(2,1)S(1)}, u32[]{:S(2)}, u32[]{:S(2)}) collective-permute-start(bf16[16,4736]{1,0:T(8,128)(2,1)S(1)} %get-tuple-element.39), channel_id=1, source_target_pairs={{0,12},{1,13},{2,14},{3,15},{4,8},{5,9},{6,10},{7,11},{8,4},{9,5},... | collective-permute-start | bytes 454664 | tf_op jit(solution)/shard_map/ppermute | solution.py:31
  17.6 1.5 %collective-permute-start.9 = (bf16[16,5248]{1,0:T(8,128)(2,1)S(1)}, bf16[16,5248]{1,0:T(8,128)(2,1)S(1)}, u32[]{:S(2)}, u32[]{:S(2)}) collective-permute-start(bf16[16,5248]{1,0:T(8,128)(2,1)S(1)} %collective-permute-done.2), channel_id=1, source_target_pairs={{0,1},{1,0},{2,3},{3,2},{4,5},{5,4},{6,7},{7,6},{8,9},{9,8},{10,11... | collective-permute-start | bytes 503816 | tf_op jit(solution)/shard_map/ppermute | solution.py:31
  19.1 0.6 collective-permute-start.6
  19.7 1.5 %collective-permute-start.4 = (bf16[16,4736]{1,0:T(8,128)(2,1)S(1)}, bf16[16,4736]{1,0:T(8,128)(2,1)S(1)}, u32[]{:S(2)}, u32[]{:S(2)}) collective-permute-start(bf16[16,4736]{1,0:T(8,128)(2,1)S(1)} %collective-permute-done), channel_id=1, source_target_pairs={{0,2},{1,3},{2,0},{3,1},{4,6},{5,7},{6,4},{7,5},{8,10},{9,11},{10,... | collective-permute-start | bytes 454664 | tf_op jit(solution)/shard_map/ppermute | solution.py:31
  21.2 1.4 %collective-permute-done.7 = bf16[16,4736]{1,0:T(8,128)(2,1)S(1)} collective-permute-done((bf16[16,4736]{1,0:T(8,128)(2,1)S(1)}, bf16[16,4736]{1,0:T(8,128)(2,1)S(1)}, u32[]{:S(2)}, u32[]{:S(2)}) %collective-permute-start.7) | collective-permute-done | bytes 151584 | tf_op jit(solution)/shard_map/ppermute | solution.py:31
  22.6 1.6 %collective-permute-start.5 = (bf16[16,4736]{1,0:T(8,128)(2,1)S(1)}, bf16[16,4736]{1,0:T(8,128)(2,1)S(1)}, u32[]{:S(2)}, u32[]{:S(2)}) collective-permute-start(bf16[16,4736]{1,0:T(8,128)(2,1)S(1)} %collective-permute-done.3), channel_id=1, source_target_pairs={{0,2},{1,3},{2,0},{3,1},{4,6},{5,7},{6,4},{7,5},{8,10},{9,11},{10,... | collective-permute-start | bytes 454664 | tf_op jit(solution)/shard_map/ppermute | solution.py:31
  25.3 1.4 %collective-permute-done.6 = bf16[16,4736]{1,0:T(8,128)(2,1)S(1)} collective-permute-done((bf16[16,4736]{1,0:T(8,128)(2,1)S(1)}, bf16[16,4736]{1,0:T(8,128)(2,1)S(1)}, u32[]{:S(2)}, u32[]{:S(2)}) %collective-permute-start.6) | collective-permute-done | bytes 151584 | tf_op jit(solution)/shard_map/ppermute | solution.py:31
  26.7 1.4 %collective-permute-done.5 = bf16[16,4736]{1,0:T(8,128)(2,1)S(1)} collective-permute-done((bf16[16,4736]{1,0:T(8,128)(2,1)S(1)}, bf16[16,4736]{1,0:T(8,128)(2,1)S(1)}, u32[]{:S(2)}, u32[]{:S(2)}) %collective-permute-start.5) | collective-permute-done | bytes 151584 | tf_op jit(solution)/shard_map/ppermute | solution.py:31
  28.1 1.5 %collective-permute-start.8 = (bf16[16,4736]{1,0:T(8,128)(2,1)S(1)}, bf16[16,4736]{1,0:T(8,128)(2,1)S(1)}, u32[]{:S(2)}, u32[]{:S(2)}) collective-permute-start(bf16[16,4736]{1,0:T(8,128)(2,1)S(1)} %collective-permute-done.4), channel_id=1, source_target_pairs={{0,1},{1,0},{2,3},{3,2},{4,5},{5,4},{6,7},{7,6},{8,9},{9,8},{10,11... | collective-permute-start | bytes 454664 | tf_op jit(solution)/shard_map/ppermute | solution.py:31
  30.1 1.5 %collective-permute-start.13 = (bf16[16,4736]{1,0:T(8,128)(2,1)S(1)}, bf16[16,4736]{1,0:T(8,128)(2,1)S(1)}, u32[]{:S(2)}, u32[]{:S(2)}) collective-permute-start(bf16[16,4736]{1,0:T(8,128)(2,1)S(1)} %collective-permute-done.7), channel_id=1, source_target_pairs={{0,2},{1,3},{2,0},{3,1},{4,6},{5,7},{6,4},{7,5},{8,10},{9,11},{10,... | collective-permute-start | bytes 454664 | tf_op jit(solution)/shard_map/ppermute | solution.py:31
  31.7 1.4 %collective-permute-start.14 = (bf16[16,4736]{1,0:T(8,128)(2,1)S(1)}, bf16[16,4736]{1,0:T(8,128)(2,1)S(1)}, u32[]{:S(2)}, u32[]{:S(2)}) collective-permute-start(bf16[16,4736]{1,0:T(8,128)(2,1)S(1)} %collective-permute-done.7), channel_id=1, source_target_pairs={{0,3},{1,2},{2,1},{3,0},{4,7},{5,6},{6,5},{7,4},{8,11},{9,10},{10,... | collective-permute-start | bytes 454664 | tf_op jit(solution)/shard_map/ppermute | solution.py:31
  33.1 1.9 %collective-permute-done.8._ = bf16[16,4736]{1,0:T(8,128)(2,1)S(1)} collective-permute-done((bf16[16,4736]{1,0:T(8,128)(2,1)S(1)}, bf16[16,4736]{1,0:T(8,128)(2,1)S(1)}, u32[]{:S(2)}, u32[]{:S(2)}) %collective-permute-start.8) | collective-permute-done | bytes 151584 | tf_op jit(solution)/shard_map/ppermute | solution.py:31
  35.0 2.9 %stage.1 = (bf16[2048,1536]{1,0:T(8,128)(2,1)S(1)}, f32[8,128]{1,0:T(8,128)S(1)}) custom-call(bf16[16,4736]{1,0:T(8,128)(2,1)S(1)} %collective-permute-done.8._, bf16[1,4096,1536]{2,1,0:T(8,128)(2,1)} %refs_5_.2), custom_call_target="tpu_custom_call" | custom-call | bytes 6291456 | tf_op jit(solution)/shard_map/stage/pallas_call | solution.py:363
  37.9 2.1 %collective-permute-done.14 = bf16[16,4736]{1,0:T(8,128)(2,1)S(1)} collective-permute-done((bf16[16,4736]{1,0:T(8,128)(2,1)S(1)}, bf16[16,4736]{1,0:T(8,128)(2,1)S(1)}, u32[]{:S(2)}, u32[]{:S(2)}) %collective-permute-start.14) | collective-permute-done | bytes 151584 | tf_op jit(solution)/shard_map/ppermute | solution.py:31
  40.0 1.3 %project.1 = (bf16[128,256]{1,0:T(8,128)(2,1)S(1)}, f32[128,1]{1,0:T(8,128)S(1)}) custom-call(f32[8,128]{1,0:T(8,128)S(1)} %get-tuple-element.41.refs_0_, bf16[1,16,5248]{2,1,0:T(8,128)(2,1)S(1)} %bitcast.37, bf16[1,16,5248]{2,1,0:T(8,128)(2,1)S(1)} %bitcast.39, bf16[1,16,5248]{2,1,0:T(8,128)(2,1)S(1)} %bitcast.38, bf16[1,16,5248]{2,1,0:T(8,128)(2,1)S(1)} %bitcast.40, ...), custom_call_target="tpu_custom_call" | custom-call | tf_op jit(solution)/shard_map/project/pallas_call | solution.py:303
  41.3 1.8 %collective-permute-start.17 = (bf16[128,256]{1,0:T(8,128)(2,1)S(1)}, bf16[128,256]{1,0:T(8,128)(2,1)S(1)}, u32[]{:S(2)}, u32[]{:S(2)}) collective-permute-start(bf16[128,256]{1,0:T(8,128)(2,1)S(1)} %get-tuple-element.44), channel_id=1, source_target_pairs={{0,4},{1,5},{2,6},{3,7},{4,0},{5,1},{6,2},{7,3},{8,12},{9,13},{10,... | collective-permute-start | bytes 196616 | tf_op jit(solution)/shard_map/ppermute | solution.py:31
  43.1 0.7 collective-permute-start.15
  43.8 1.9 %collective-permute-start.16 = (bf16[128,256]{1,0:T(8,128)(2,1)S(1)}, bf16[128,256]{1,0:T(8,128)(2,1)S(1)}, u32[]{:S(2)}, u32[]{:S(2)}) collective-permute-start(bf16[128,256]{1,0:T(8,128)(2,1)S(1)} %get-tuple-element.44), channel_id=1, source_target_pairs={{0,12},{1,13},{2,14},{3,15},{4,8},{5,9},{6,10},{7,11},{8,4},{9,5},... | collective-permute-start | bytes 196616 | tf_op jit(solution)/shard_map/ppermute | solution.py:31
  46.2 1.5 %collective-permute-start.21 = (bf16[2,128,256]{2,1,0:T(8,128)(2,1)S(1)}, bf16[2,128,256]{2,1,0:T(8,128)(2,1)S(1)}, u32[]{:S(2)}, u32[]{:S(2)}) collective-permute-start(bf16[2,128,256]{2,1,0:T(8,128)(2,1)S(1)} %pad_maximum_fusion.1.refs_0_), channel_id=1, source_target_pairs={{0,1},{1,0},{2,3},{3,2},{4,5},{5,4},{6,7},{7,6},{8,9},{9,8},{10,11... | collective-permute-start | bytes 393224 | tf_op jit(solution)/shard_map/ppermute | solution.py:31
  47.7 0.6 collective-permute-start.22
  48.3 1.5 %collective-permute-start.23 = (bf16[2,128,256]{2,1,0:T(8,128)(2,1)S(1)}, bf16[2,128,256]{2,1,0:T(8,128)(2,1)S(1)}, u32[]{:S(2)}, u32[]{:S(2)}) collective-permute-start(bf16[2,128,256]{2,1,0:T(8,128)(2,1)S(1)} %pad_maximum_fusion.1.refs_0_), channel_id=1, source_target_pairs={{0,3},{1,2},{2,1},{3,0},{4,7},{5,6},{6,5},{7,4},{8,11},{9,10},{10,... | collective-permute-start | bytes 393224 | tf_op jit(solution)/shard_map/ppermute | solution.py:31
  50.0 1.3 %collective-permute-start.18 = (bf16[2,128,256]{2,1,0:T(8,128)(2,1)S(1)}, bf16[2,128,256]{2,1,0:T(8,128)(2,1)S(1)}, u32[]{:S(2)}, u32[]{:S(2)}) collective-permute-start(bf16[2,128,256]{2,1,0:T(8,128)(2,1)S(1)} %pad_maximum_fusion.refs_0_), channel_id=1, source_target_pairs={{0,1},{1,0},{2,3},{3,2},{4,5},{5,4},{6,7},{7,6},{8,9},{9,8},{10,11... | collective-permute-start | bytes 393224 | tf_op jit(solution)/shard_map/ppermute | solution.py:31
  51.3 0.6 collective-permute-start.19
  51.9 0.6 collective-permute-done.21.refs_1_
  52.5 1.6 %collective-permute-start.20 = (bf16[2,128,256]{2,1,0:T(8,128)(2,1)S(1)}, bf16[2,128,256]{2,1,0:T(8,128)(2,1)S(1)}, u32[]{:S(2)}, u32[]{:S(2)}) collective-permute-start(bf16[2,128,256]{2,1,0:T(8,128)(2,1)S(1)} %pad_maximum_fusion.refs_0_), channel_id=1, source_target_pairs={{0,3},{1,2},{2,1},{3,0},{4,7},{5,6},{6,5},{7,4},{8,11},{9,10},{10,... | collective-permute-start | bytes 393224 | tf_op jit(solution)/shard_map/ppermute | solution.py:31
  54.0 1.1 %collective-permute-done.22.refs_2_ = bf16[2,128,256]{2,1,0:T(8,128)(2,1)S(1)} collective-permute-done((bf16[2,128,256]{2,1,0:T(8,128)(2,1)S(1)}, bf16[2,128,256]{2,1,0:T(8,128)(2,1)S(1)}, u32[]{:S(2)}, u32[]{:S(2)}) %collective-permute-start.22) | collective-permute-done | bytes 131104 | tf_op jit(solution)/shard_map/ppermute | solution.py:31
  55.2 3.8 %near.1 = (f32[128,1536]{1,0:T(8,128)S(1)}, f32[128,128]{1,0:T(8,128)S(1)}, f32[16,2048]{1,0:T(8,128)S(1)}, bf16[2048,1536]{1,0:T(8,128)(2,1)S(1)}) custom-call(bf16[2,128,256]{2,1,0:T(8,128)(2,1)S(1)} %pad_maximum_fusion.1.refs_0_, bf16[2,128,256]{2,1,0:T(8,128)(2,1)S(1)} %collective-permute-done.21.refs_1_, ...), custom_call_target="tpu_custom_call" | custom-call | flops 805306368 | bytes 12582912 | tf_op jit(solution)/shard_map/near/pallas_call | solution.py:414
  59.0 2.2 %experts.1 = (bf16[2,16,2048]{2,1,0:T(8,128)(2,1)S(1)}, bf16[2,16,2048]{2,1,0:T(8,128)(2,1)S(1)}, bf16[2,16,2048]{2,1,0:T(8,128)(2,1)S(1)}, bf16[2,16,2048]{2,1,...) custom-call(bf16[2,128,256]{2,1,0:T(8,128)(2,1)S(1)} %pad_maximum_fu, ...), custom_call_target="tpu_custom_call" | custom-call | tf_op jit(solution)/shard_map/experts/pallas_call | solution.py:517
  61.2 1.1 %collective-permute-start.24 = (bf16[2,16,2048]{2,1,0:T(8,128)(2,1)S(1)}, bf16[2,16,2048]{2,1,0:T(8,128)(2,1)S(1)}, u32[]{:S(2)}, u32[]{:S(2)}) collective-permute-start(bf16[2,16,2048]{2,1,0:T(8,128)(2,1)S(1)} %get-tuple-element.54), channel_id=1, source_target_pairs={{0,3},{1,2},{2,1},{3,0},{4,7},{5,6},{6,5},{7,4},{8,11},{9,10},{10,... | collective-permute-start | bytes 393224 | tf_op jit(solution)/shard_map/ppermute | solution.py:31
  62.4 1.3 %collective-permute-start.25 = (bf16[2,16,2048]{2,1,0:T(8,128)(2,1)S(1)}, bf16[2,16,2048]{2,1,0:T(8,128)(2,1)S(1)}, u32[]{:S(2)}, u32[]{:S(2)}) collective-permute-start(bf16[2,16,2048]{2,1,0:T(8,128)(2,1)S(1)} %get-tuple-element.55), channel_id=1, source_target_pairs={{0,1},{1,0},{2,3},{3,2},{4,5},{5,4},{6,7},{7,6},{8,9},{9,8},{10,11... | collective-permute-start | bytes 393224 | tf_op jit(solution)/shard_map/ppermute | solution.py:31
  63.7 1.1 %collective-permute-start.26 = (bf16[2,16,2048]{2,1,0:T(8,128)(2,1)S(1)}, bf16[2,16,2048]{2,1,0:T(8,128)(2,1)S(1)}, u32[]{:S(2)}, u32[]{:S(2)}) collective-permute-start(bf16[2,16,2048]{2,1,0:T(8,128)(2,1)S(1)} %get-tuple-element.56), channel_id=1, source_target_pairs={{0,2},{1,3},{2,0},{3,1},{4,6},{5,7},{6,4},{7,5},{8,10},{9,11},{10,... | collective-permute-start | bytes 393224 | tf_op jit(solution)/shard_map/ppermute | solution.py:31
  64.8 1.1 %collective-permute-start.28 = (bf16[2,16,2048]{2,1,0:T(8,128)(2,1)S(1)}, bf16[2,16,2048]{2,1,0:T(8,128)(2,1)S(1)}, u32[]{:S(2)}, u32[]{:S(2)}) collective-permute-start(bf16[2,16,2048]{2,1,0:T(8,128)(2,1)S(1)} %get-tuple-element.58), channel_id=1, source_target_pairs={{0,3},{1,2},{2,1},{3,0},{4,7},{5,6},{6,5},{7,4},{8,11},{9,10},{10,... | collective-permute-start | bytes 393224 | tf_op jit(solution)/shard_map/ppermute | solution.py:31
  65.9 1.3 %collective-permute-start.29 = (bf16[2,16,2048]{2,1,0:T(8,128)(2,1)S(1)}, bf16[2,16,2048]{2,1,0:T(8,128)(2,1)S(1)}, u32[]{:S(2)}, u32[]{:S(2)}) collective-permute-start(bf16[2,16,2048]{2,1,0:T(8,128)(2,1)S(1)} %get-tuple-element.59), channel_id=1, source_target_pairs={{0,1},{1,0},{2,3},{3,2},{4,5},{5,4},{6,7},{7,6},{8,9},{9,8},{10,11... | collective-permute-start | bytes 393224 | tf_op jit(solution)/shard_map/ppermute | solution.py:31
  67.2 1.1 %collective-permute-start.30 = (bf16[2,16,2048]{2,1,0:T(8,128)(2,1)S(1)}, bf16[2,16,2048]{2,1,0:T(8,128)(2,1)S(1)}, u32[]{:S(2)}, u32[]{:S(2)}) collective-permute-start(bf16[2,16,2048]{2,1,0:T(8,128)(2,1)S(1)} %get-tuple-element.60), channel_id=1, source_target_pairs={{0,2},{1,3},{2,0},{3,1},{4,6},{5,7},{6,4},{7,5},{8,10},{9,11},{10,... | collective-permute-start | bytes 393224 | tf_op jit(solution)/shard_map/ppermute | solution.py:31
  68.7 2.6 %collective-permute-start.27 = (bf16[16,2048]{1,0:T(8,128)(2,1)S(1)}, bf16[16,2048]{1,0:T(8,128)(2,1)S(1)}, u32[]{:S(2)}, u32[]{:S(2)}) collective-permute-start(bf16[16,2048]{1,0:T(8,128)(2,1)S(1)} %slice_bitcast_fusion.2), channel_id=1, source_target_pairs={{0,12},{1,13},{2,14},{3,15},{4,8},{5,9},{6,10},{7,11},{8,4},{9,5},... | collective-permute-start | bytes 196616 | tf_op jit(solution)/shard_map/ppermute | solution.py:31
  71.5 0.6 collective-permute-done.30
  72.2 1.3 %collective-permute-start.31 = (bf16[16,2048]{1,0:T(8,128)(2,1)S(1)}, bf16[16,2048]{1,0:T(8,128)(2,1)S(1)}, u32[]{:S(2)}, u32[]{:S(2)}) collective-permute-start(bf16[16,2048]{1,0:T(8,128)(2,1)S(1)} %get-tuple-element.61), channel_id=1, source_target_pairs={{0,4},{1,5},{2,6},{3,7},{4,0},{5,1},{6,2},{7,3},{8,12},{9,13},{10,... | collective-permute-start | bytes 196616 | tf_op jit(solution)/shard_map/ppermute | solution.py:31
  73.5 2.0 %collective-permute-start.32 = (bf16[16,2048]{1,0:T(8,128)(2,1)S(1)}, bf16[16,2048]{1,0:T(8,128)(2,1)S(1)}, u32[]{:S(2)}, u32[]{:S(2)}) collective-permute-start(bf16[16,2048]{1,0:T(8,128)(2,1)S(1)} %get-tuple-element.62), channel_id=1, source_target_pairs={{0,8},{1,9},{2,10},{3,11},{4,12},{5,13},{6,14},{7,15},{8,0},{9,1},... | collective-permute-start | bytes 196616 | tf_op jit(solution)/shard_map/ppermute | solution.py:31
  75.5 1.1 %collective-permute-done.31 = bf16[16,2048]{1,0:T(8,128)(2,1)S(1)} collective-permute-done((bf16[16,2048]{1,0:T(8,128)(2,1)S(1)}, bf16[16,2048]{1,0:T(8,128)(2,1)S(1)}, u32[]{:S(2)}, u32[]{:S(2)}) %collective-permute-start.31) | collective-permute-done | bytes 65568 | tf_op jit(solution)/shard_map/ppermute | solution.py:31
  76.6 2.8 %collective-permute-done.32 = bf16[16,2048]{1,0:T(8,128)(2,1)S(1)} collective-permute-done((bf16[16,2048]{1,0:T(8,128)(2,1)S(1)}, bf16[16,2048]{1,0:T(8,128)(2,1)S(1)}, u32[]{:S(2)}, u32[]{:S(2)}) %collective-permute-start.32) | collective-permute-done | bytes 65568 | tf_op jit(solution)/shard_map/ppermute | solution.py:31
  79.5 1.2 %collective-permute-done.33 = bf16[8,2048]{1,0:T(8,128)(2,1)S(1)} collective-permute-done((bf16[8,2048]{1,0:T(8,128)(2,1)S(1)}, bf16[8,2048]{1,0:T(8,128)(2,1)S(1)}, u32[]{:S(2)}, u32[]{:S(2)}) %collective-permute-start.33) | collective-permute-done | bytes 32800 | tf_op jit(solution)/shard_map/ppermute | solution.py:598
  80.7 0.6 maximum_select_fusion
  (43 shorter events, 3.2 us)
Async XLA Ops:
  2.6 11.4 %collective-permute-start = (bf16[16,4736]{1,0:T(8,128)(2,1)S(1)}, bf16[16,4736]{1,0:T(8,128)(2,1)S(1)}, u32[]{:S(2)}, u32[]{:S(2)}) collective-permute-start(bf16[16,4736]{1,0:T(8,128)(2,1)S(1)} %get-tuple-element.33), channel_id=1, source_target_pairs={{0,8},{1,9},{2,10},{3,11},{4,12},{5,13},{6,14},{7,15},{8,0},{9,1},... | collective-permute-start | bytes 454664 | tf_op jit(solution)/shard_map/ppermute | solution.py:31
  6.7 10.8 %collective-permute-start.2 = (bf16[16,5248]{1,0:T(8,128)(2,1)S(1)}, bf16[16,5248]{1,0:T(8,128)(2,1)S(1)}, u32[]{:S(2)}, u32[]{:S(2)}) collective-permute-start(bf16[16,5248]{1,0:T(8,128)(2,1)S(1)} %get-tuple-element.34), channel_id=1, source_target_pairs={{0,2},{1,3},{2,0},{3,1},{4,6},{5,7},{6,4},{7,5},{8,10},{9,11},{10,... | collective-permute-start | bytes 503816 | tf_op jit(solution)/shard_map/ppermute | solution.py:31
  8.3 10.8 %collective-permute-start.1 = (bf16[16,5248]{1,0:T(8,128)(2,1)S(1)}, bf16[16,5248]{1,0:T(8,128)(2,1)S(1)}, u32[]{:S(2)}, u32[]{:S(2)}) collective-permute-start(bf16[16,5248]{1,0:T(8,128)(2,1)S(1)} %get-tuple-element.34), channel_id=1, source_target_pairs={{0,1},{1,0},{2,3},{3,2},{4,5},{5,4},{6,7},{7,6},{8,9},{9,8},{10,11... | collective-permute-start | bytes 503816 | tf_op jit(solution)/shard_map/ppermute | solution.py:31
  9.7 9.3 %collective-permute-start.3 = (bf16[16,4736]{1,0:T(8,128)(2,1)S(1)}, bf16[16,4736]{1,0:T(8,128)(2,1)S(1)}, u32[]{:S(2)}, u32[]{:S(2)}) collective-permute-start(bf16[16,4736]{1,0:T(8,128)(2,1)S(1)} %get-tuple-element.35), channel_id=1, source_target_pairs={{0,4},{1,5},{2,6},{3,7},{4,0},{5,1},{6,2},{7,3},{8,12},{9,13},{10,... | collective-permute-start | bytes 454664 | tf_op jit(solution)/shard_map/ppermute | solution.py:31
  14.0 26.0 %copy-start = (bf16[8192,256]{1,0:T(8,128)(2,1)S(1)}, bf16[8192,256]{1,0:T(8,128)(2,1)}, u32[]{:S(2)}) copy-start(bf16[8192,256]{1,0:T(8,128)(2,1)} %refs_17_.1) | copy-start | bytes 12582916
  14.0 8.6 %collective-permute-start.7 = (bf16[16,4736]{1,0:T(8,128)(2,1)S(1)}, bf16[16,4736]{1,0:T(8,128)(2,1)S(1)}, u32[]{:S(2)}, u32[]{:S(2)}) collective-permute-start(bf16[16,4736]{1,0:T(8,128)(2,1)S(1)} %get-tuple-element.39), channel_id=1, source_target_pairs={{0,12},{1,13},{2,14},{3,15},{4,8},{5,9},{6,10},{7,11},{8,4},{9,5},... | collective-permute-start | bytes 454664 | tf_op jit(solution)/shard_map/ppermute | solution.py:31
  17.6 7.2 %collective-permute-start.9 = (bf16[16,5248]{1,0:T(8,128)(2,1)S(1)}, bf16[16,5248]{1,0:T(8,128)(2,1)S(1)}, u32[]{:S(2)}, u32[]{:S(2)}) collective-permute-start(bf16[16,5248]{1,0:T(8,128)(2,1)S(1)} %collective-permute-done.2), channel_id=1, source_target_pairs={{0,1},{1,0},{2,3},{3,2},{4,5},{5,4},{6,7},{7,6},{8,9},{9,8},{10,11... | collective-permute-start | bytes 503816 | tf_op jit(solution)/shard_map/ppermute | solution.py:31
  19.1 10.5 %collective-permute-start.10 = (bf16[16,5248]{1,0:T(8,128)(2,1)S(1)}, bf16[16,5248]{1,0:T(8,128)(2,1)S(1)}, u32[]{:S(2)}, u32[]{:S(2)}) collective-permute-start(bf16[16,5248]{1,0:T(8,128)(2,1)S(1)} %collective-permute-done.1), channel_id=1, source_target_pairs={{0,4},{1,5},{2,6},{3,7},{4,0},{5,1},{6,2},{7,3},{8,12},{9,13},{10,... | collective-permute-start | bytes 503816 | tf_op jit(solution)/shard_map/ppermute | solution.py:31
  19.1 7.6 %collective-permute-start.6 = (bf16[16,4736]{1,0:T(8,128)(2,1)S(1)}, bf16[16,4736]{1,0:T(8,128)(2,1)S(1)}, u32[]{:S(2)}, u32[]{:S(2)}) collective-permute-start(bf16[16,4736]{1,0:T(8,128)(2,1)S(1)} %collective-permute-done), channel_id=1, source_target_pairs={{0,1},{1,0},{2,3},{3,2},{4,5},{5,4},{6,7},{7,6},{8,9},{9,8},{10,11... | collective-permute-start | bytes 454664 | tf_op jit(solution)/shard_map/ppermute | solution.py:31
  19.7 7.0 %collective-permute-start.4 = (bf16[16,4736]{1,0:T(8,128)(2,1)S(1)}, bf16[16,4736]{1,0:T(8,128)(2,1)S(1)}, u32[]{:S(2)}, u32[]{:S(2)}) collective-permute-start(bf16[16,4736]{1,0:T(8,128)(2,1)S(1)} %collective-permute-done), channel_id=1, source_target_pairs={{0,2},{1,3},{2,0},{3,1},{4,6},{5,7},{6,4},{7,5},{8,10},{9,11},{10,... | collective-permute-start | bytes 454664 | tf_op jit(solution)/shard_map/ppermute | solution.py:31
  22.6 5.5 %collective-permute-start.5 = (bf16[16,4736]{1,0:T(8,128)(2,1)S(1)}, bf16[16,4736]{1,0:T(8,128)(2,1)S(1)}, u32[]{:S(2)}, u32[]{:S(2)}) collective-permute-start(bf16[16,4736]{1,0:T(8,128)(2,1)S(1)} %collective-permute-done.3), channel_id=1, source_target_pairs={{0,2},{1,3},{2,0},{3,1},{4,6},{5,7},{6,4},{7,5},{8,10},{9,11},{10,... | collective-permute-start | bytes 454664 | tf_op jit(solution)/shard_map/ppermute | solution.py:31
  24.8 15.2 %collective-permute-start.11 = (bf16[16,5248]{1,0:T(8,128)(2,1)S(1)}, bf16[16,5248]{1,0:T(8,128)(2,1)S(1)}, u32[]{:S(2)}, u32[]{:S(2)}) collective-permute-start(bf16[16,5248]{1,0:T(8,128)(2,1)S(1)} %collective-permute-done.9), channel_id=1, source_target_pairs={{0,4},{1,5},{2,6},{3,7},{4,0},{5,1},{6,2},{7,3},{8,12},{9,13},{10,... | collective-permute-start | bytes 503816 | tf_op jit(solution)/shard_map/ppermute | solution.py:31
  28.1 6.9 %collective-permute-start.8 = (bf16[16,4736]{1,0:T(8,128)(2,1)S(1)}, bf16[16,4736]{1,0:T(8,128)(2,1)S(1)}, u32[]{:S(2)}, u32[]{:S(2)}) collective-permute-start(bf16[16,4736]{1,0:T(8,128)(2,1)S(1)} %collective-permute-done.4), channel_id=1, source_target_pairs={{0,1},{1,0},{2,3},{3,2},{4,5},{5,4},{6,7},{7,6},{8,9},{9,8},{10,11... | collective-permute-start | bytes 454664 | tf_op jit(solution)/shard_map/ppermute | solution.py:31
  29.6 8.3 %collective-permute-start.12 = (bf16[16,4736]{1,0:T(8,128)(2,1)S(1)}, bf16[16,4736]{1,0:T(8,128)(2,1)S(1)}, u32[]{:S(2)}, u32[]{:S(2)}) collective-permute-start(bf16[16,4736]{1,0:T(8,128)(2,1)S(1)} %collective-permute-done.7), channel_id=1, source_target_pairs={{0,1},{1,0},{2,3},{3,2},{4,5},{5,4},{6,7},{7,6},{8,9},{9,8},{10,11... | collective-permute-start | bytes 454664 | tf_op jit(solution)/shard_map/ppermute | solution.py:31
  30.1 7.7 %collective-permute-start.13 = (bf16[16,4736]{1,0:T(8,128)(2,1)S(1)}, bf16[16,4736]{1,0:T(8,128)(2,1)S(1)}, u32[]{:S(2)}, u32[]{:S(2)}) collective-permute-start(bf16[16,4736]{1,0:T(8,128)(2,1)S(1)} %collective-permute-done.7), channel_id=1, source_target_pairs={{0,2},{1,3},{2,0},{3,1},{4,6},{5,7},{6,4},{7,5},{8,10},{9,11},{10,... | collective-permute-start | bytes 454664 | tf_op jit(solution)/shard_map/ppermute | solution.py:31
  31.7 8.3 %collective-permute-start.14 = (bf16[16,4736]{1,0:T(8,128)(2,1)S(1)}, bf16[16,4736]{1,0:T(8,128)(2,1)S(1)}, u32[]{:S(2)}, u32[]{:S(2)}) collective-permute-start(bf16[16,4736]{1,0:T(8,128)(2,1)S(1)} %collective-permute-done.7), channel_id=1, source_target_pairs={{0,3},{1,2},{2,1},{3,0},{4,7},{5,6},{6,5},{7,4},{8,11},{9,10},{10,... | collective-permute-start | bytes 454664 | tf_op jit(solution)/shard_map/ppermute | solution.py:31
  37.8 17.3 %copy-start.1 = (f32[4096]{0:T(1024)S(1)}, f32[4096]{0:T(1024)}, u32[]{:S(2)}) copy-start(f32[4096]{0:T(1024)} %param.17) | copy-start | bytes 49156
  41.3 4.9 %collective-permute-start.17 = (bf16[128,256]{1,0:T(8,128)(2,1)S(1)}, bf16[128,256]{1,0:T(8,128)(2,1)S(1)}, u32[]{:S(2)}, u32[]{:S(2)}) collective-permute-start(bf16[128,256]{1,0:T(8,128)(2,1)S(1)} %get-tuple-element.44), channel_id=1, source_target_pairs={{0,4},{1,5},{2,6},{3,7},{4,0},{5,1},{6,2},{7,3},{8,12},{9,13},{10,... | collective-permute-start | bytes 196616 | tf_op jit(solution)/shard_map/ppermute | solution.py:31
  43.1 6.7 %collective-permute-start.15 = (bf16[128,256]{1,0:T(8,128)(2,1)S(1)}, bf16[128,256]{1,0:T(8,128)(2,1)S(1)}, u32[]{:S(2)}, u32[]{:S(2)}) collective-permute-start(bf16[128,256]{1,0:T(8,128)(2,1)S(1)} %get-tuple-element.44), channel_id=1, source_target_pairs={{0,8},{1,9},{2,10},{3,11},{4,12},{5,13},{6,14},{7,15},{8,0},{9,1},... | collective-permute-start | bytes 196616 | tf_op jit(solution)/shard_map/ppermute | solution.py:31
  43.8 6.2 %collective-permute-start.16 = (bf16[128,256]{1,0:T(8,128)(2,1)S(1)}, bf16[128,256]{1,0:T(8,128)(2,1)S(1)}, u32[]{:S(2)}, u32[]{:S(2)}) collective-permute-start(bf16[128,256]{1,0:T(8,128)(2,1)S(1)} %get-tuple-element.44), channel_id=1, source_target_pairs={{0,12},{1,13},{2,14},{3,15},{4,8},{5,9},{6,10},{7,11},{8,4},{9,5},... | collective-permute-start | bytes 196616 | tf_op jit(solution)/shard_map/ppermute | solution.py:31
  46.2 12.8 %slice-start = ((s8[6291456]{0:T(1024)(128)(4,1)}), s8[4194304]{0:T(1024)(128)(4,1)S(1)}, s32[]{:S(2)}) async-start(s8[6291456]{0:T(1024)(128)(4,1)} %bitcast.34), calls=%async_computation | async-start | bytes 8388608
  46.2 6.2 %collective-permute-start.21 = (bf16[2,128,256]{2,1,0:T(8,128)(2,1)S(1)}, bf16[2,128,256]{2,1,0:T(8,128)(2,1)S(1)}, u32[]{:S(2)}, u32[]{:S(2)}) collective-permute-start(bf16[2,128,256]{2,1,0:T(8,128)(2,1)S(1)} %pad_maximum_fusion.1.refs_0_), channel_id=1, source_target_pairs={{0,1},{1,0},{2,3},{3,2},{4,5},{5,4},{6,7},{7,6},{8,9},{9,8},{10,11... | collective-permute-start | bytes 393224 | tf_op jit(solution)/shard_map/ppermute | solution.py:31
  47.7 7.4 %collective-permute-start.22 = (bf16[2,128,256]{2,1,0:T(8,128)(2,1)S(1)}, bf16[2,128,256]{2,1,0:T(8,128)(2,1)S(1)}, u32[]{:S(2)}, u32[]{:S(2)}) collective-permute-start(bf16[2,128,256]{2,1,0:T(8,128)(2,1)S(1)} %pad_maximum_fusion.1.refs_0_), channel_id=1, source_target_pairs={{0,2},{1,3},{2,0},{3,1},{4,6},{5,7},{6,4},{7,5},{8,10},{9,11},{10,... | collective-permute-start | bytes 393224 | tf_op jit(solution)/shard_map/ppermute | solution.py:31
  48.3 6.9 %collective-permute-start.23 = (bf16[2,128,256]{2,1,0:T(8,128)(2,1)S(1)}, bf16[2,128,256]{2,1,0:T(8,128)(2,1)S(1)}, u32[]{:S(2)}, u32[]{:S(2)}) collective-permute-start(bf16[2,128,256]{2,1,0:T(8,128)(2,1)S(1)} %pad_maximum_fusion.1.refs_0_), channel_id=1, source_target_pairs={{0,3},{1,2},{2,1},{3,0},{4,7},{5,6},{6,5},{7,4},{8,11},{9,10},{10,... | collective-permute-start | bytes 393224 | tf_op jit(solution)/shard_map/ppermute | solution.py:31
  50.0 9.0 %collective-permute-start.18 = (bf16[2,128,256]{2,1,0:T(8,128)(2,1)S(1)}, bf16[2,128,256]{2,1,0:T(8,128)(2,1)S(1)}, u32[]{:S(2)}, u32[]{:S(2)}) collective-permute-start(bf16[2,128,256]{2,1,0:T(8,128)(2,1)S(1)} %pad_maximum_fusion.refs_0_), channel_id=1, source_target_pairs={{0,1},{1,0},{2,3},{3,2},{4,5},{5,4},{6,7},{7,6},{8,9},{9,8},{10,11... | collective-permute-start | bytes 393224 | tf_op jit(solution)/shard_map/ppermute | solution.py:31
  51.3 7.7 %collective-permute-start.19 = (bf16[2,128,256]{2,1,0:T(8,128)(2,1)S(1)}, bf16[2,128,256]{2,1,0:T(8,128)(2,1)S(1)}, u32[]{:S(2)}, u32[]{:S(2)}) collective-permute-start(bf16[2,128,256]{2,1,0:T(8,128)(2,1)S(1)} %pad_maximum_fusion.refs_0_), channel_id=1, source_target_pairs={{0,2},{1,3},{2,0},{3,1},{4,6},{5,7},{6,4},{7,5},{8,10},{9,11},{10,... | collective-permute-start | bytes 393224 | tf_op jit(solution)/shard_map/ppermute | solution.py:31
  52.5 6.5 %collective-permute-start.20 = (bf16[2,128,256]{2,1,0:T(8,128)(2,1)S(1)}, bf16[2,128,256]{2,1,0:T(8,128)(2,1)S(1)}, u32[]{:S(2)}, u32[]{:S(2)}) collective-permute-start(bf16[2,128,256]{2,1,0:T(8,128)(2,1)S(1)} %pad_maximum_fusion.refs_0_), channel_id=1, source_target_pairs={{0,3},{1,2},{2,1},{3,0},{4,7},{5,6},{6,5},{7,4},{8,11},{9,10},{10,... | collective-permute-start | bytes 393224 | tf_op jit(solution)/shard_map/ppermute | solution.py:31
  55.2 3.8 %slice-start.1 = ((s8[6291456]{0:T(1024)(128)(4,1)}), s8[2097152]{0:T(1024)(128)(4,1)S(1)}, s32[]{:S(2)}) async-start(s8[6291456]{0:T(1024)(128)(4,1)} %bitcast.34), calls=%async_computation.1 | async-start | bytes 4194304
  61.2 5.9 %collective-permute-start.24 = (bf16[2,16,2048]{2,1,0:T(8,128)(2,1)S(1)}, bf16[2,16,2048]{2,1,0:T(8,128)(2,1)S(1)}, u32[]{:S(2)}, u32[]{:S(2)}) collective-permute-start(bf16[2,16,2048]{2,1,0:T(8,128)(2,1)S(1)} %get-tuple-element.54), channel_id=1, source_target_pairs={{0,3},{1,2},{2,1},{3,0},{4,7},{5,6},{6,5},{7,4},{8,11},{9,10},{10,... | collective-permute-start | bytes 393224 | tf_op jit(solution)/shard_map/ppermute | solution.py:31
  62.4 5.9 %collective-permute-start.25 = (bf16[2,16,2048]{2,1,0:T(8,128)(2,1)S(1)}, bf16[2,16,2048]{2,1,0:T(8,128)(2,1)S(1)}, u32[]{:S(2)}, u32[]{:S(2)}) collective-permute-start(bf16[2,16,2048]{2,1,0:T(8,128)(2,1)S(1)} %get-tuple-element.55), channel_id=1, source_target_pairs={{0,1},{1,0},{2,3},{3,2},{4,5},{5,4},{6,7},{7,6},{8,9},{9,8},{10,11... | collective-permute-start | bytes 393224 | tf_op jit(solution)/shard_map/ppermute | solution.py:31
  63.7 5.0 %collective-permute-start.26 = (bf16[2,16,2048]{2,1,0:T(8,128)(2,1)S(1)}, bf16[2,16,2048]{2,1,0:T(8,128)(2,1)S(1)}, u32[]{:S(2)}, u32[]{:S(2)}) collective-permute-start(bf16[2,16,2048]{2,1,0:T(8,128)(2,1)S(1)} %get-tuple-element.56), channel_id=1, source_target_pairs={{0,2},{1,3},{2,0},{3,1},{4,6},{5,7},{6,4},{7,5},{8,10},{9,11},{10,... | collective-permute-start | bytes 393224 | tf_op jit(solution)/shard_map/ppermute | solution.py:31
  64.8 6.5 %collective-permute-start.28 = (bf16[2,16,2048]{2,1,0:T(8,128)(2,1)S(1)}, bf16[2,16,2048]{2,1,0:T(8,128)(2,1)S(1)}, u32[]{:S(2)}, u32[]{:S(2)}) collective-permute-start(bf16[2,16,2048]{2,1,0:T(8,128)(2,1)S(1)} %get-tuple-element.58), channel_id=1, source_target_pairs={{0,3},{1,2},{2,1},{3,0},{4,7},{5,6},{6,5},{7,4},{8,11},{9,10},{10,... | collective-permute-start | bytes 393224 | tf_op jit(solution)/shard_map/ppermute | solution.py:31
  65.9 5.6 %collective-permute-start.29 = (bf16[2,16,2048]{2,1,0:T(8,128)(2,1)S(1)}, bf16[2,16,2048]{2,1,0:T(8,128)(2,1)S(1)}, u32[]{:S(2)}, u32[]{:S(2)}) collective-permute-start(bf16[2,16,2048]{2,1,0:T(8,128)(2,1)S(1)} %get-tuple-element.59), channel_id=1, source_target_pairs={{0,1},{1,0},{2,3},{3,2},{4,5},{5,4},{6,7},{7,6},{8,9},{9,8},{10,11... | collective-permute-start | bytes 393224 | tf_op jit(solution)/shard_map/ppermute | solution.py:31
  67.2 5.0 %collective-permute-start.30 = (bf16[2,16,2048]{2,1,0:T(8,128)(2,1)S(1)}, bf16[2,16,2048]{2,1,0:T(8,128)(2,1)S(1)}, u32[]{:S(2)}, u32[]{:S(2)}) collective-permute-start(bf16[2,16,2048]{2,1,0:T(8,128)(2,1)S(1)} %get-tuple-element.60), channel_id=1, source_target_pairs={{0,2},{1,3},{2,0},{3,1},{4,6},{5,7},{6,4},{7,5},{8,10},{9,11},{10,... | collective-permute-start | bytes 393224 | tf_op jit(solution)/shard_map/ppermute | solution.py:31
  68.7 6.7 %collective-permute-start.27 = (bf16[16,2048]{1,0:T(8,128)(2,1)S(1)}, bf16[16,2048]{1,0:T(8,128)(2,1)S(1)}, u32[]{:S(2)}, u32[]{:S(2)}) collective-permute-start(bf16[16,2048]{1,0:T(8,128)(2,1)S(1)} %slice_bitcast_fusion.2), channel_id=1, source_target_pairs={{0,12},{1,13},{2,14},{3,15},{4,8},{5,9},{6,10},{7,11},{8,4},{9,5},... | collective-permute-start | bytes 196616 | tf_op jit(solution)/shard_map/ppermute | solution.py:31
  72.2 4.3 %collective-permute-start.31 = (bf16[16,2048]{1,0:T(8,128)(2,1)S(1)}, bf16[16,2048]{1,0:T(8,128)(2,1)S(1)}, u32[]{:S(2)}, u32[]{:S(2)}) collective-permute-start(bf16[16,2048]{1,0:T(8,128)(2,1)S(1)} %get-tuple-element.61), channel_id=1, source_target_pairs={{0,4},{1,5},{2,6},{3,7},{4,0},{5,1},{6,2},{7,3},{8,12},{9,13},{10,... | collective-permute-start | bytes 196616 | tf_op jit(solution)/shard_map/ppermute | solution.py:31
  73.5 5.9 %collective-permute-start.32 = (bf16[16,2048]{1,0:T(8,128)(2,1)S(1)}, bf16[16,2048]{1,0:T(8,128)(2,1)S(1)}, u32[]{:S(2)}, u32[]{:S(2)}) collective-permute-start(bf16[16,2048]{1,0:T(8,128)(2,1)S(1)} %get-tuple-element.62), channel_id=1, source_target_pairs={{0,8},{1,9},{2,10},{3,11},{4,12},{5,13},{6,14},{7,15},{8,0},{9,1},... | collective-permute-start | bytes 196616 | tf_op jit(solution)/shard_map/ppermute | solution.py:31
  79.4 1.3 %collective-permute-start.33 = (bf16[8,2048]{1,0:T(8,128)(2,1)S(1)}, bf16[8,2048]{1,0:T(8,128)(2,1)S(1)}, u32[]{:S(2)}, u32[]{:S(2)}) collective-permute-start(bf16[8,2048]{1,0:T(8,128)(2,1)S(1)} %get-tuple-element.64), channel_id=1, source_target_pairs={{0,16},{16,0},{1,17},{17,1},{2,18},{18,2},{3,19},{19,3},{4,20},{20... | collective-permute-start | bytes 98312 | tf_op jit(solution)/shard_map/ppermute | solution.py:598

commit v2 on v1

--- a/solution.py
+++ b/solution.py
@@ -23,7 +23,7 @@
 CHIPS = 16
 PLANES = 4
 PAIRS = ((0, 1), (2, 3))
-BACK_PAIRS = ((0, 3), (1, 2))
+BACK_PAIRS = ((2, 3), (0, 1))
 ROUTING = LANES
 
 
@@ -51,13 +51,13 @@
     own = planes[0]
     z1, z2 = (exchange(planes[k], 4 * k) for k in (1, 2))
     x0, y0 = (exchange(own, f) for f in (1, 2))
-    z3 = exchange(after(planes[3], z2), 12)
+    z3 = exchange(after(planes[3], z1), 12)
     x1 = exchange(x0, 4)
     c0 = exchange(y0, 1)
     y1 = exchange(after(z1, y0), 2)
-    x2, y2 = (exchange(after(z2, x0, y0, z1), f) for f in (1, 2))
+    x2, y2 = (exchange(z2, f) for f in (1, 2))
     c1 = exchange(c0, 4)
-    c2 = exchange(after(y2, y1, x2, z3), 1)
+    c2 = exchange(after(y2, y1), 1)
     d3, x3, y3 = (exchange(after(z3, x1, y1, x2), f) for f in (3, 1, 2))
     return [own, x0, y0, c0, z1, x1, y1, c1, z2, x2, y2, c2, z3, x3, y3, d3]
 
@@ -78,11 +78,12 @@
     return sum(t.astype(jnp.float32) for t in terms).astype(jnp.bfloat16)
 
 
-def scatter_sum(first, second):
-    first = add(first[0], *[exchange(first[f], f) for f in (3, 1, 2)])
-    second = add(second[0], *[exchange(second[f], f) for f in (3, 1, 2)])
-    terms = [first[0], exchange(first[1], 12), exchange(second[0], 4), exchange(second[1], 8)]
-    return sum(t.astype(jnp.float32) for t in terms)
+def scatter_sum(far, near):
+    far = add(far[0], *[exchange(far[f], f) for f in (3, 1, 2)])
+    near = add(near[0], *[exchange(near[f], f) for f in (3, 1, 2)])
+    late = exchange(far[0], 8).astype(jnp.float32) + exchange(far[1], 12).astype(jnp.float32)
+    late = lax.optimization_barrier(late)
+    return near[0].astype(jnp.float32) + exchange(near[1], 4).astype(jnp.float32) + late
 
 
 def attend_kernel(
@@ -333,22 +334,13 @@
     return squares[:, :LANES] + squares[:, LANES:]
 
 
-def weight_copies(gu_hbm, dst, sems, first):
-    return [
+def stage_kernel(_, gu_hbm, weights, done, sems):
+    copies = [
         pltpu.make_async_copy(
-            gu_hbm.at[0, pl.ds(pl.multiple_of((first + j) * CHUNK, CHUNK), CHUNK)],
-            dst.at[pl.ds(j * CHUNK, CHUNK)],
-            sems.at[j],
+            gu_hbm.at[0, pl.ds(j * CHUNK, CHUNK)], weights.at[pl.ds(j * CHUNK, CHUNK)], sems.at[j]
         )
-        for j in range(dst.shape[0] // CHUNK)
+        for j in range(weights.shape[0] // CHUNK)
     ]
-
-
-def stage_kernel(_, gu_hbm, weights, done, sems):
-    own = weights.shape[0] // CHUNK
-    copies = weight_copies(
-        gu_hbm, weights, sems, (lax.axis_index("grp") // (CHIPS // 2)) * own
-    )
     for copy in copies:
         copy.start()
     done[...] = jnp.zeros_like(done)
@@ -357,7 +349,7 @@
 
 
 def stage(gate_up, arrived):
-    half = gate_up.shape[1] // 2
+    depth = gate_up.shape[1]
     hbm_spec = pl.BlockSpec(memory_space=pltpu.HBM)
     vmem_spec = pl.BlockSpec(memory_space=pltpu.VMEM)
     return pl.pallas_call(
@@ -365,13 +357,13 @@
         in_specs=[pl.BlockSpec(memory_space=pl.ANY), hbm_spec],
         out_specs=[vmem_spec] * 2,
         out_shape=[
-            jax.ShapeDtypeStruct((half, 2 * HID), jnp.bfloat16),
+            jax.ShapeDtypeStruct((depth, 2 * HID), jnp.bfloat16),
             jax.ShapeDtypeStruct((8, LANES), jnp.float32),
         ],
-        scratch_shapes=[pltpu.SemaphoreType.DMA((half // CHUNK,))],
+        scratch_shapes=[pltpu.SemaphoreType.DMA((depth // CHUNK,))],
         compiler_params=pltpu.CompilerParams(vmem_limit_bytes=2 * MIB),
         cost_estimate=pl.CostEstimate(
-            flops=0, bytes_accessed=half * 4 * HID, transcendentals=0
+            flops=0, bytes_accessed=depth * 4 * HID, transcendentals=0
         ),
         name="stage",
     )(arrived, pltpu.with_memory_space_constraint(gate_up, pltpu.HBM))
@@ -379,15 +371,13 @@
 
 def near_kernel(count, *refs):
     pieces = refs[:count]
-    weights, gu_hbm, g_ref, acc, sq_ref, hid_ref, kept, store, plain, sems = refs[count:]
+    weights, g_ref, acc, sq_ref, hid_ref, store, plain = refs[count:]
     place = lax.axis_index("grp")
     chunks = g_ref.shape[0]
     own = chunks // 2
     first = (place // (CHIPS // 2)) * own
-    copies = weight_copies(gu_hbm, kept, sems, own - first)
-    for copy in copies:
-        copy.start()
     order = pair_order(place, CHIPS, PAIRS)[:own]
+    mine = weights.at[pl.ds(pl.multiple_of(first * CHUNK, CHUNK), own * CHUNK)]
     squares = jnp.zeros(sq_ref.shape, jnp.float32)
     for n in range(count):
         for b in range(2):
@@ -399,32 +389,27 @@
     y = jnp.concatenate([store[j] for j in range(own)], axis=1)
     for n in range(2 * HID // CHUNK):
         cols = slice(n * CHUNK, (n + 1) * CHUNK)
-        acc[:, cols] = jnp.dot(y, weights[:, cols], preferred_element_type=jnp.float32)
-    for copy in copies:
-        copy.wait()
-
-
-def near(pieces, staged, gate_up, norm_gain):
+        acc[:, cols] = jnp.dot(y, mine[:, cols], preferred_element_type=jnp.float32)
+
+
+def near(pieces, staged, norm_gain):
     rows = pieces[0].shape[1]
-    width = gate_up.shape[1]
+    width = staged.shape[0]
     chunks = width // CHUNK
     vmem_spec = pl.BlockSpec(memory_space=pltpu.VMEM)
-    hbm_spec = pl.BlockSpec(memory_space=pltpu.HBM)
     count = len(pieces)
     return pl.pallas_call(
         functools.partial(near_kernel, count),
-        in_specs=[vmem_spec] * (count + 1) + [hbm_spec, vmem_spec],
-        out_specs=[vmem_spec] * 4,
+        in_specs=[vmem_spec] * (count + 2),
+        out_specs=[vmem_spec] * 3,
         out_shape=[
             jax.ShapeDtypeStruct((rows, 2 * HID), jnp.float32),
             jax.ShapeDtypeStruct((rows, LANES), jnp.float32),
             jax.ShapeDtypeStruct((16, width // 2), jnp.float32),
-            jax.ShapeDtypeStruct((width // 2, 2 * HID), jnp.bfloat16),
         ],
         scratch_shapes=[
             pltpu.VMEM((chunks // 2, rows, CHUNK), jnp.bfloat16),
             pltpu.VMEM((rows, CHUNK), jnp.float32),
-            pltpu.SemaphoreType.DMA((chunks // 2,)),
         ],
         compiler_params=pltpu.CompilerParams(vmem_limit_bytes=6 * MIB),
         cost_estimate=pl.CostEstimate(
@@ -434,7 +419,6 @@
     )(
         *pieces,
         pltpu.with_memory_space_constraint(staged, pltpu.VMEM),
-        pltpu.with_memory_space_constraint(gate_up, pltpu.HBM),
         norm_gain.reshape(chunks, 1, CHUNK),
     )
 
@@ -458,6 +442,7 @@
     if resumed:
         order = pair_order(place, groups, PAIRS)[own:]
         base = own - (place // (CHIPS // 2)) * own
+        gu_ref = gu_ref.at[pl.ds(pl.multiple_of(base * CHUNK, CHUNK), own * CHUNK)]
         squares = sq_ref[...]
         hid_ref[...] = old_ref[...]
     else:
@@ -521,7 +506,7 @@
         out_shape=[jax.ShapeDtypeStruct((groups // outs, 16, width // 2), jnp.bfloat16)] * outs
         + [jax.ShapeDtypeStruct((16, width // 2), jnp.float32)],
         scratch_shapes=[
-            pltpu.VMEM((gate_up.shape[0] // CHUNK, rows, CHUNK), jnp.bfloat16),
+            pltpu.VMEM((chunks // (2 if begun else 1), rows, CHUNK), jnp.bfloat16),
             pltpu.VMEM((rows, CHUNK), jnp.float32),
             pltpu.VMEM((rows, width // 8), jnp.float32),
             pltpu.VMEM((rows, width // 8), jnp.float32),
@@ -573,8 +558,8 @@
         staged, done = stage(gate_up, pieces[11])
         y, mix = project([p[None] for p in pieces], out_weight, gain, waits=(done,))
         nears, fars = gather_pairs(y)
-        *begun, kept = near(nears, staged, gate_up, norm_gain)
-        *sums, hidden = experts(fars, kept, down_weight, norm_gain, mix, 8, begun)
+        begun = near(nears, staged, norm_gain)
+        *sums, hidden = experts(fars, staged, down_weight, norm_gain, mix, 8, begun)
         mixture = scatter_sum(sums[:4], sums[4:])
     else:
         own_residual = lax.dynamic_slice_in_dim(residual, side * half, half, axis=0)

time: 81.5 us -> 78 us (0.957)
  starting transfers between devices: 47.3 us -> 43.7 us
  waiting for transfers between devices: 20.2 us -> 21.2 us
    ppermute x33, starting transfers between devices: 47.2 us -> 43.6 us  [exchange(): return lax.ppermute(value, 'grp', [(g, g ^ bits) for g in range(CHIPS)])]
    pallas_call x1, Pallas kernels: 3.79 us -> 1.09 us  [near(): pl.pallas_call(functools.partial(near_kernel, count), in_specs=[vmem_spec...]
    pallas_call x1, Pallas kernels: 2.86 us -> 4.72 us  [stage(): pl.pallas_call(stage_kernel, in_specs=[pl.BlockSpec(memory_space=pl.ANY),...]
    ppermute x33, waiting for transfers between devices: 19 us -> 20 us  [exchange(): return lax.ppermute(value, 'grp', [(g, g ^ bits) for g in range(CHIPS)])]
  transfers between devices with their start and end apart: 34 -> 34, of which waited for: 17 -> 13; matrix products, arithmetic and copies ran while one was open for 0% -> 0% of each run, Pallas kernels for 8% -> 7%
where the time goes in v2:
time: 78 us; the launch traced here: 77.8 us
  starting transfers between devices  43.7 us (56%)
  waiting for transfers between devices  21.2 us (27%)
  Pallas kernels  11.9 us (15%)
  other arithmetic  0.86 us (1%)
    ppermute x33, starting transfers between devices, exchange(): return lax.ppermute(value, 'grp', [(g, g ^ bits) for g in range(CHIPS)])  43.6 us
    ppermute x33, waiting for transfers between devices, exchange(): return lax.ppermute(value, 'grp', [(g, g ^ bits) for g in range(CHIPS)])  20 us
    pallas_call x1, Pallas kernels, stage(): pl.pallas_call(stage_kernel, in_specs=[pl.BlockSpec(memory_space=pl.ANY),...  4.72 us
    pallas_call x1, Pallas kernels, attend(): pl.pallas_call(functools.partial(attend_kernel, planes), in_specs=[hbm_sp...  2.62 us
    pallas_call x1, Pallas kernels, experts(): pl.pallas_call(functools.partial(expert_kernel, count, outs, bool(begun))...  2.14 us
  transfers between devices with their start and end apart: 34, of which 13 were waited for; matrix products, arithmetic and copies ran while one was open for 0% of the time, Pallas kernels for 7%

profile of v2, /device:TPU:0, one launch (start us, length us, event | category | flops | bytes accessed | tf_op | source)
XLA Modules:
  0.0 77.8 jit_solution(261114207031711668)
XLA Ops:
  0.0 2.6 %attend.1 = (bf16[16,5248]{1,0:T(8,128)(2,1)S(1)}, bf16[16,4736]{1,0:T(8,128)(2,1)S(1)}, bf16[16,4736]{1,0:T(8,128)(2,1)S(1)}, bf16[16,4736]{1,0:T(8,128)(2,1)S(1)}, f32[1,256]{1,0:T(1,128)S(1)}) custom-call(s32[8,16]{1,0:T(8,128)} %bitcast.59, f32[8,16]{1,0:T(8,128)} %bitcast.60, s32[16]{0:T(128)} %len_hbm.1, f32[16,1,256]{2,1,0:T(1,128)} %bitcast.52, ...), custom_call_target="tpu_custom_call" | custom-call | tf_op jit(solution)/shard_map/attend/pallas_call | solution.py:214
  2.6 4.1 %collective-permute-start = (bf16[16,4736]{1,0:T(8,128)(2,1)S(1)}, bf16[16,4736]{1,0:T(8,128)(2,1)S(1)}, u32[]{:S(2)}, u32[]{:S(2)}) collective-permute-start(bf16[16,4736]{1,0:T(8,128)(2,1)S(1)} %get-tuple-element.31), channel_id=1, source_target_pairs={{0,8},{1,9},{2,10},{3,11},{4,12},{5,13},{6,14},{7,15},{8,0},{9,1},... | collective-permute-start | bytes 454664 | tf_op jit(solution)/shard_map/ppermute | solution.py:31
  6.7 1.5 %collective-permute-start.3 = (bf16[16,5248]{1,0:T(8,128)(2,1)S(1)}, bf16[16,5248]{1,0:T(8,128)(2,1)S(1)}, u32[]{:S(2)}, u32[]{:S(2)}) collective-permute-start(bf16[16,5248]{1,0:T(8,128)(2,1)S(1)} %get-tuple-element.33), channel_id=1, source_target_pairs={{0,2},{1,3},{2,0},{3,1},{4,6},{5,7},{6,4},{7,5},{8,10},{9,11},{10,... | collective-permute-start | bytes 503816 | tf_op jit(solution)/shard_map/ppermute | solution.py:31
  8.3 1.5 %collective-permute-start.6 = (bf16[16,5248]{1,0:T(8,128)(2,1)S(1)}, bf16[16,5248]{1,0:T(8,128)(2,1)S(1)}, u32[]{:S(2)}, u32[]{:S(2)}) collective-permute-start(bf16[16,5248]{1,0:T(8,128)(2,1)S(1)} %get-tuple-element.33), channel_id=1, source_target_pairs={{0,1},{1,0},{2,3},{3,2},{4,5},{5,4},{6,7},{7,6},{8,9},{9,8},{10,11... | collective-permute-start | bytes 503816 | tf_op jit(solution)/shard_map/ppermute | solution.py:31
  9.7 1.6 %collective-permute-start.2 = (bf16[16,4736]{1,0:T(8,128)(2,1)S(1)}, bf16[16,4736]{1,0:T(8,128)(2,1)S(1)}, u32[]{:S(2)}, u32[]{:S(2)}) collective-permute-start(bf16[16,4736]{1,0:T(8,128)(2,1)S(1)} %get-tuple-element.32), channel_id=1, source_target_pairs={{0,4},{1,5},{2,6},{3,7},{4,0},{5,1},{6,2},{7,3},{8,12},{9,13},{10,... | collective-permute-start | bytes 454664 | tf_op jit(solution)/shard_map/ppermute | solution.py:31
  11.3 2.7 %collective-permute-done = bf16[16,4736]{1,0:T(8,128)(2,1)S(1)} collective-permute-done((bf16[16,4736]{1,0:T(8,128)(2,1)S(1)}, bf16[16,4736]{1,0:T(8,128)(2,1)S(1)}, u32[]{:S(2)}, u32[]{:S(2)}) %collective-permute-start) | collective-permute-done | bytes 151584 | tf_op jit(solution)/shard_map/ppermute | solution.py:31
  14.0 1.6 %collective-permute-start.1 = (bf16[16,4736]{1,0:T(8,128)(2,1)S(1)}, bf16[16,4736]{1,0:T(8,128)(2,1)S(1)}, u32[]{:S(2)}, u32[]{:S(2)}) collective-permute-start(bf16[16,4736]{1,0:T(8,128)(2,1)S(1)} %collective-permute-done), channel_id=1, source_target_pairs={{0,2},{1,3},{2,0},{3,1},{4,6},{5,7},{6,4},{7,5},{8,10},{9,11},{10,... | collective-permute-start | bytes 454664 | tf_op jit(solution)/shard_map/ppermute | solution.py:31
  15.6 1.5 %collective-permute-start.7 = (bf16[16,5248]{1,0:T(8,128)(2,1)S(1)}, bf16[16,5248]{1,0:T(8,128)(2,1)S(1)}, u32[]{:S(2)}, u32[]{:S(2)}) collective-permute-start(bf16[16,5248]{1,0:T(8,128)(2,1)S(1)} %collective-permute-done.3), channel_id=1, source_target_pairs={{0,1},{1,0},{2,3},{3,2},{4,5},{5,4},{6,7},{7,6},{8,9},{9,8},{10,11... | collective-permute-start | bytes 503816 | tf_op jit(solution)/shard_map/ppermute | solution.py:31
  17.1 0.6 collective-permute-start.8
  17.7 0.5 collective-permute-start.4
  18.2 2.9 %collective-permute-start.11 = (bf16[16,4736]{1,0:T(8,128)(2,1)S(1)}, bf16[16,4736]{1,0:T(8,128)(2,1)S(1)}, u32[]{:S(2)}, u32[]{:S(2)}) collective-permute-start(bf16[16,4736]{1,0:T(8,128)(2,1)S(1)} %get-tuple-element.38), channel_id=1, source_target_pairs={{0,12},{1,13},{2,14},{3,15},{4,8},{5,9},{6,10},{7,11},{8,4},{9,5},... | collective-permute-start | bytes 454664 | tf_op jit(solution)/shard_map/ppermute | solution.py:31
  21.2 0.5 collective-permute-start.10
  21.7 1.3 %collective-permute-start.9 = (bf16[16,5248]{1,0:T(8,128)(2,1)S(1)}, bf16[16,5248]{1,0:T(8,128)(2,1)S(1)}, u32[]{:S(2)}, u32[]{:S(2)}) collective-permute-start(bf16[16,5248]{1,0:T(8,128)(2,1)S(1)} %collective-permute-done.7), channel_id=1, source_target_pairs={{0,4},{1,5},{2,6},{3,7},{4,0},{5,1},{6,2},{7,3},{8,12},{9,13},{10,... | collective-permute-start | bytes 503816 | tf_op jit(solution)/shard_map/ppermute | solution.py:31
  23.0 1.3 %collective-permute-start.5 = (bf16[16,4736]{1,0:T(8,128)(2,1)S(1)}, bf16[16,4736]{1,0:T(8,128)(2,1)S(1)}, u32[]{:S(2)}, u32[]{:S(2)}) collective-permute-start(bf16[16,4736]{1,0:T(8,128)(2,1)S(1)} %collective-permute-done.1), channel_id=1, source_target_pairs={{0,1},{1,0},{2,3},{3,2},{4,5},{5,4},{6,7},{7,6},{8,9},{9,8},{10,11... | collective-permute-start | bytes 454664 | tf_op jit(solution)/shard_map/ppermute | solution.py:31
  24.3 4.6 %collective-permute-done.11 = bf16[16,4736]{1,0:T(8,128)(2,1)S(1)} collective-permute-done((bf16[16,4736]{1,0:T(8,128)(2,1)S(1)}, bf16[16,4736]{1,0:T(8,128)(2,1)S(1)}, u32[]{:S(2)}, u32[]{:S(2)}) %collective-permute-start.11) | collective-permute-done | bytes 151584 | tf_op jit(solution)/shard_map/ppermute | solution.py:31
  28.9 0.6 collective-permute-start.12
  29.5 0.5 collective-permute-start.13
  30.1 2.3 %collective-permute-start.14 = (bf16[16,4736]{1,0:T(8,128)(2,1)S(1)}, bf16[16,4736]{1,0:T(8,128)(2,1)S(1)}, u32[]{:S(2)}, u32[]{:S(2)}) collective-permute-start(bf16[16,4736]{1,0:T(8,128)(2,1)S(1)} %collective-permute-done.11), channel_id=1, source_target_pairs={{0,3},{1,2},{2,1},{3,0},{4,7},{5,6},{6,5},{7,4},{8,11},{9,10},{10,... | collective-permute-start | bytes 454664 | tf_op jit(solution)/shard_map/ppermute | solution.py:31
  32.4 4.7 %stage.1 = (bf16[4096,1536]{1,0:T(8,128)(2,1)S(1)}, f32[8,128]{1,0:T(8,128)S(1)}) custom-call(bf16[16,4736]{1,0:T(8,128)(2,1)S(1)} %collective-permute-done.5._, bf16[1,4096,1536]{2,1,0:T(8,128)(2,1)} %gu_hbm.1), custom_call_target="tpu_custom_call" | custom-call | bytes 12582912 | tf_op jit(solution)/shard_map/stage/pallas_call | solution.py:355
  37.2 1.3 %project.1 = (bf16[128,256]{1,0:T(8,128)(2,1)S(1)}, f32[128,1]{1,0:T(8,128)S(1)}) custom-call(f32[8,128]{1,0:T(8,128)S(1)} %get-tuple-element.36.refs_0_, bf16[1,16,5248]{2,1,0:T(8,128)(2,1)S(1)} %bitcast.37, bf16[1,16,5248]{2,1,0:T(8,128)(2,1)S(1)} %bitcast.39, bf16[1,16,5248]{2,1,0:T(8,128)(2,1)S(1)} %bitcast.38, bf16[1,16,5248]{2,1,0:T(8,128)(2,1)S(1)} %bitcast.40, ...), custom_call_target="tpu_custom_call" | custom-call | tf_op jit(solution)/shard_map/project/pallas_call | solution.py:304
  39.0 3.4 %collective-permute-start.15 = (bf16[128,256]{1,0:T(8,128)(2,1)S(1)}, bf16[128,256]{1,0:T(8,128)(2,1)S(1)}, u32[]{:S(2)}, u32[]{:S(2)}) collective-permute-start(bf16[128,256]{1,0:T(8,128)(2,1)S(1)} %get-tuple-element.41), channel_id=1, source_target_pairs={{0,8},{1,9},{2,10},{3,11},{4,12},{5,13},{6,14},{7,15},{8,0},{9,1},... | collective-permute-start | bytes 196616 | tf_op jit(solution)/shard_map/ppermute | solution.py:31
  42.4 0.5 collective-permute-start.16
  43.0 1.0 %collective-permute-start.21 = (bf16[2,128,256]{2,1,0:T(8,128)(2,1)S(1)}, bf16[2,128,256]{2,1,0:T(8,128)(2,1)S(1)}, u32[]{:S(2)}, u32[]{:S(2)}) collective-permute-start(bf16[2,128,256]{2,1,0:T(8,128)(2,1)S(1)} %pad_maximum_fusion.1.refs_0_), channel_id=1, source_target_pairs={{0,1},{1,0},{2,3},{3,2},{4,5},{5,4},{6,7},{7,6},{8,9},{9,8},{10,11... | collective-permute-start | bytes 393224 | tf_op jit(solution)/shard_map/ppermute | solution.py:31
  44.0 1.0 %collective-permute-start.22 = (bf16[2,128,256]{2,1,0:T(8,128)(2,1)S(1)}, bf16[2,128,256]{2,1,0:T(8,128)(2,1)S(1)}, u32[]{:S(2)}, u32[]{:S(2)}) collective-permute-start(bf16[2,128,256]{2,1,0:T(8,128)(2,1)S(1)} %pad_maximum_fusion.1.refs_0_), channel_id=1, source_target_pairs={{0,2},{1,3},{2,0},{3,1},{4,6},{5,7},{6,4},{7,5},{8,10},{9,11},{10,... | collective-permute-start | bytes 393224 | tf_op jit(solution)/shard_map/ppermute | solution.py:31
  44.9 1.6 %collective-permute-start.23 = (bf16[2,128,256]{2,1,0:T(8,128)(2,1)S(1)}, bf16[2,128,256]{2,1,0:T(8,128)(2,1)S(1)}, u32[]{:S(2)}, u32[]{:S(2)}) collective-permute-start(bf16[2,128,256]{2,1,0:T(8,128)(2,1)S(1)} %pad_maximum_fusion.1.refs_0_), channel_id=1, source_target_pairs={{0,3},{1,2},{2,1},{3,0},{4,7},{5,6},{6,5},{7,4},{8,11},{9,10},{10,... | collective-permute-start | bytes 393224 | tf_op jit(solution)/shard_map/ppermute | solution.py:31
  46.5 2.0 %collective-permute-done.16 = bf16[128,256]{1,0:T(8,128)(2,1)S(1)} collective-permute-done((bf16[128,256]{1,0:T(8,128)(2,1)S(1)}, bf16[128,256]{1,0:T(8,128)(2,1)S(1)}, u32[]{:S(2)}, u32[]{:S(2)}) %collective-permute-start.16) | collective-permute-done | bytes 65568 | tf_op jit(solution)/shard_map/ppermute | solution.py:31
  48.5 1.2 %collective-permute-start.18 = (bf16[2,128,256]{2,1,0:T(8,128)(2,1)S(1)}, bf16[2,128,256]{2,1,0:T(8,128)(2,1)S(1)}, u32[]{:S(2)}, u32[]{:S(2)}) collective-permute-start(bf16[2,128,256]{2,1,0:T(8,128)(2,1)S(1)} %pad_maximum_fusion.refs_0_), channel_id=1, source_target_pairs={{0,1},{1,0},{2,3},{3,2},{4,5},{5,4},{6,7},{7,6},{8,9},{9,8},{10,11... | collective-permute-start | bytes 393224 | tf_op jit(solution)/shard_map/ppermute | solution.py:31
  49.7 0.9 %collective-permute-start.19 = (bf16[2,128,256]{2,1,0:T(8,128)(2,1)S(1)}, bf16[2,128,256]{2,1,0:T(8,128)(2,1)S(1)}, u32[]{:S(2)}, u32[]{:S(2)}) collective-permute-start(bf16[2,128,256]{2,1,0:T(8,128)(2,1)S(1)} %pad_maximum_fusion.refs_0_), channel_id=1, source_target_pairs={{0,2},{1,3},{2,0},{3,1},{4,6},{5,7},{6,4},{7,5},{8,10},{9,11},{10,... | collective-permute-start | bytes 393224 | tf_op jit(solution)/shard_map/ppermute | solution.py:31
  50.6 1.5 %collective-permute-start.20 = (bf16[2,128,256]{2,1,0:T(8,128)(2,1)S(1)}, bf16[2,128,256]{2,1,0:T(8,128)(2,1)S(1)}, u32[]{:S(2)}, u32[]{:S(2)}) collective-permute-start(bf16[2,128,256]{2,1,0:T(8,128)(2,1)S(1)} %pad_maximum_fusion.refs_0_), channel_id=1, source_target_pairs={{0,3},{1,2},{2,1},{3,0},{4,7},{5,6},{6,5},{7,4},{8,11},{9,10},{10,... | collective-permute-start | bytes 393224 | tf_op jit(solution)/shard_map/ppermute | solution.py:31
  52.1 1.1 %near.1 = (f32[128,1536]{1,0:T(8,128)S(1)}, f32[128,128]{1,0:T(8,128)S(1)}, f32[16,2048]{1,0:T(8,128)S(1)}) custom-call(bf16[2,128,256]{2,1,0:T(8,128)(2,1)S(1)} %pad_maximum_fusion.1.refs_0_, bf16[2,128,256]{2,1,0:T(8,128)(2,1)S(1)} %collective-permute-done.21.refs_1_, bf16[2,128,256]{2,1,0:T(8,128)(2,1)S(1)} %collective-permute-done.22.refs_2_, ...), custom_call_target="tpu_custom_call" | custom-call | flops 805306368 | bytes 12582912 | tf_op jit(solution)/shard_map/near/pallas_call | solution.py:401
  53.7 1.0 %collective-permute-done.19.refs_2_ = bf16[2,128,256]{2,1,0:T(8,128)(2,1)S(1)} collective-permute-done((bf16[2,128,256]{2,1,0:T(8,128)(2,1)S(1)}, bf16[2,128,256]{2,1,0:T(8,128)(2,1)S(1)}, u32[]{:S(2)}, u32[]{:S(2)}) %collective-permute-start.19) | collective-permute-done | bytes 131104 | tf_op jit(solution)/shard_map/ppermute | solution.py:31
  54.7 1.8 %collective-permute-done.20.refs_3_ = bf16[2,128,256]{2,1,0:T(8,128)(2,1)S(1)} collective-permute-done((bf16[2,128,256]{2,1,0:T(8,128)(2,1)S(1)}, bf16[2,128,256]{2,1,0:T(8,128)(2,1)S(1)}, u32[]{:S(2)}, u32[]{:S(2)}) %collective-permute-start.20) | collective-permute-done | bytes 131104 | tf_op jit(solution)/shard_map/ppermute | solution.py:31
  56.5 2.1 %experts.1 = (bf16[2,16,2048]{2,1,0:T(8,128)(2,1)S(1)}, bf16[2,16,2048]{2,1,0:T(8,128)(2,1)S(1)}, bf16[2,16,2048]{2,1,0:T(8,128)(2,1)S(1)}, bf16[2,16,2048]{2,1,...) custom-call(bf16[2,128,256]{2,1,0:T(8,128)(2,1)S(1)} %pad_maximum_fu, ...), custom_call_target="tpu_custom_call" | custom-call | tf_op jit(solution)/shard_map/experts/pallas_call | solution.py:502
  58.6 1.6 %collective-permute-start.28 = (bf16[2,16,2048]{2,1,0:T(8,128)(2,1)S(1)}, bf16[2,16,2048]{2,1,0:T(8,128)(2,1)S(1)}, u32[]{:S(2)}, u32[]{:S(2)}) collective-permute-start(bf16[2,16,2048]{2,1,0:T(8,128)(2,1)S(1)} %get-tuple-element.54), channel_id=1, source_target_pairs={{0,3},{1,2},{2,1},{3,0},{4,7},{5,6},{6,5},{7,4},{8,11},{9,10},{10,... | collective-permute-start | bytes 393224 | tf_op jit(solution)/shard_map/ppermute | solution.py:31
  60.2 1.1 %collective-permute-start.29 = (bf16[2,16,2048]{2,1,0:T(8,128)(2,1)S(1)}, bf16[2,16,2048]{2,1,0:T(8,128)(2,1)S(1)}, u32[]{:S(2)}, u32[]{:S(2)}) collective-permute-start(bf16[2,16,2048]{2,1,0:T(8,128)(2,1)S(1)} %get-tuple-element.55), channel_id=1, source_target_pairs={{0,1},{1,0},{2,3},{3,2},{4,5},{5,4},{6,7},{7,6},{8,9},{9,8},{10,11... | collective-permute-start | bytes 393224 | tf_op jit(solution)/shard_map/ppermute | solution.py:31
  61.3 0.9 %collective-permute-start.30 = (bf16[2,16,2048]{2,1,0:T(8,128)(2,1)S(1)}, bf16[2,16,2048]{2,1,0:T(8,128)(2,1)S(1)}, u32[]{:S(2)}, u32[]{:S(2)}) collective-permute-start(bf16[2,16,2048]{2,1,0:T(8,128)(2,1)S(1)} %get-tuple-element.56), channel_id=1, source_target_pairs={{0,2},{1,3},{2,0},{3,1},{4,6},{5,7},{6,4},{7,5},{8,10},{9,11},{10,... | collective-permute-start | bytes 393224 | tf_op jit(solution)/shard_map/ppermute | solution.py:31
  62.2 1.5 %collective-permute-start.24 = (bf16[2,16,2048]{2,1,0:T(8,128)(2,1)S(1)}, bf16[2,16,2048]{2,1,0:T(8,128)(2,1)S(1)}, u32[]{:S(2)}, u32[]{:S(2)}) collective-permute-start(bf16[2,16,2048]{2,1,0:T(8,128)(2,1)S(1)} %get-tuple-element.50), channel_id=1, source_target_pairs={{0,3},{1,2},{2,1},{3,0},{4,7},{5,6},{6,5},{7,4},{8,11},{9,10},{10,... | collective-permute-start | bytes 393224 | tf_op jit(solution)/shard_map/ppermute | solution.py:31
  63.7 1.1 %collective-permute-start.25 = (bf16[2,16,2048]{2,1,0:T(8,128)(2,1)S(1)}, bf16[2,16,2048]{2,1,0:T(8,128)(2,1)S(1)}, u32[]{:S(2)}, u32[]{:S(2)}) collective-permute-start(bf16[2,16,2048]{2,1,0:T(8,128)(2,1)S(1)} %get-tuple-element.51), channel_id=1, source_target_pairs={{0,1},{1,0},{2,3},{3,2},{4,5},{5,4},{6,7},{7,6},{8,9},{9,8},{10,11... | collective-permute-start | bytes 393224 | tf_op jit(solution)/shard_map/ppermute | solution.py:31
  64.8 1.2 %collective-permute-done.28 = bf16[2,16,2048]{2,1,0:T(8,128)(2,1)S(1)} collective-permute-done((bf16[2,16,2048]{2,1,0:T(8,128)(2,1)S(1)}, bf16[2,16,2048]{2,1,0:T(8,128)(2,1)S(1)}, u32[]{:S(2)}, u32[]{:S(2)}) %collective-permute-start.28) | collective-permute-done | bytes 131104 | tf_op jit(solution)/shard_map/ppermute | solution.py:31
  66.0 1.0 %collective-permute-start.26 = (bf16[2,16,2048]{2,1,0:T(8,128)(2,1)S(1)}, bf16[2,16,2048]{2,1,0:T(8,128)(2,1)S(1)}, u32[]{:S(2)}, u32[]{:S(2)}) collective-permute-start(bf16[2,16,2048]{2,1,0:T(8,128)(2,1)S(1)} %get-tuple-element.52), channel_id=1, source_target_pairs={{0,2},{1,3},{2,0},{3,1},{4,6},{5,7},{6,4},{7,5},{8,10},{9,11},{10,... | collective-permute-start | bytes 393224 | tf_op jit(solution)/shard_map/ppermute | solution.py:31
  67.6 1.5 %collective-permute-start.31 = (bf16[16,2048]{1,0:T(8,128)(2,1)S(1)}, bf16[16,2048]{1,0:T(8,128)(2,1)S(1)}, u32[]{:S(2)}, u32[]{:S(2)}) collective-permute-start(bf16[16,2048]{1,0:T(8,128)(2,1)S(1)} %get-tuple-element.57), channel_id=1, source_target_pairs={{0,8},{1,9},{2,10},{3,11},{4,12},{5,13},{6,14},{7,15},{8,0},{9,1},... | collective-permute-start | bytes 196616 | tf_op jit(solution)/shard_map/ppermute | solution.py:31
  69.1 0.7 collective-permute-start.32
  69.8 1.2 %collective-permute-done.26 = bf16[2,16,2048]{2,1,0:T(8,128)(2,1)S(1)} collective-permute-done((bf16[2,16,2048]{2,1,0:T(8,128)(2,1)S(1)}, bf16[2,16,2048]{2,1,0:T(8,128)(2,1)S(1)}, u32[]{:S(2)}, u32[]{:S(2)}) %collective-permute-start.26) | collective-permute-done | bytes 131104 | tf_op jit(solution)/shard_map/ppermute | solution.py:31
  71.3 1.7 %collective-permute-done.31 = bf16[16,2048]{1,0:T(8,128)(2,1)S(1)} collective-permute-done((bf16[16,2048]{1,0:T(8,128)(2,1)S(1)}, bf16[16,2048]{1,0:T(8,128)(2,1)S(1)}, u32[]{:S(2)}, u32[]{:S(2)}) %collective-permute-start.31) | collective-permute-done | bytes 65568 | tf_op jit(solution)/shard_map/ppermute | solution.py:31
  72.9 2.3 %collective-permute-done.32 = bf16[16,2048]{1,0:T(8,128)(2,1)S(1)} collective-permute-done((bf16[16,2048]{1,0:T(8,128)(2,1)S(1)}, bf16[16,2048]{1,0:T(8,128)(2,1)S(1)}, u32[]{:S(2)}, u32[]{:S(2)}) %collective-permute-start.32) | collective-permute-done | bytes 65568 | tf_op jit(solution)/shard_map/ppermute | solution.py:31
  75.2 0.6 collective-permute-done.27
  76.0 1.2 %collective-permute-done.33 = bf16[8,2048]{1,0:T(8,128)(2,1)S(1)} collective-permute-done((bf16[8,2048]{1,0:T(8,128)(2,1)S(1)}, bf16[8,2048]{1,0:T(8,128)(2,1)S(1)}, u32[]{:S(2)}, u32[]{:S(2)}) %collective-permute-start.33) | collective-permute-done | bytes 32800 | tf_op jit(solution)/shard_map/ppermute | solution.py:583
  77.2 0.6 maximum_select_fusion
  (44 shorter events, 2.0 us)
Async XLA Ops:
  2.6 11.4 %collective-permute-start = (bf16[16,4736]{1,0:T(8,128)(2,1)S(1)}, bf16[16,4736]{1,0:T(8,128)(2,1)S(1)}, u32[]{:S(2)}, u32[]{:S(2)}) collective-permute-start(bf16[16,4736]{1,0:T(8,128)(2,1)S(1)} %get-tuple-element.31), channel_id=1, source_target_pairs={{0,8},{1,9},{2,10},{3,11},{4,12},{5,13},{6,14},{7,15},{8,0},{9,1},... | collective-permute-start | bytes 454664 | tf_op jit(solution)/shard_map/ppermute | solution.py:31
  6.7 8.9 %collective-permute-start.3 = (bf16[16,5248]{1,0:T(8,128)(2,1)S(1)}, bf16[16,5248]{1,0:T(8,128)(2,1)S(1)}, u32[]{:S(2)}, u32[]{:S(2)}) collective-permute-start(bf16[16,5248]{1,0:T(8,128)(2,1)S(1)} %get-tuple-element.33), channel_id=1, source_target_pairs={{0,2},{1,3},{2,0},{3,1},{4,6},{5,7},{6,4},{7,5},{8,10},{9,11},{10,... | collective-permute-start | bytes 503816 | tf_op jit(solution)/shard_map/ppermute | solution.py:31
  8.3 8.8 %collective-permute-start.6 = (bf16[16,5248]{1,0:T(8,128)(2,1)S(1)}, bf16[16,5248]{1,0:T(8,128)(2,1)S(1)}, u32[]{:S(2)}, u32[]{:S(2)}) collective-permute-start(bf16[16,5248]{1,0:T(8,128)(2,1)S(1)} %get-tuple-element.33), channel_id=1, source_target_pairs={{0,1},{1,0},{2,3},{3,2},{4,5},{5,4},{6,7},{7,6},{8,9},{9,8},{10,11... | collective-permute-start | bytes 503816 | tf_op jit(solution)/shard_map/ppermute | solution.py:31
  9.7 7.9 %collective-permute-start.2 = (bf16[16,4736]{1,0:T(8,128)(2,1)S(1)}, bf16[16,4736]{1,0:T(8,128)(2,1)S(1)}, u32[]{:S(2)}, u32[]{:S(2)}) collective-permute-start(bf16[16,4736]{1,0:T(8,128)(2,1)S(1)} %get-tuple-element.32), channel_id=1, source_target_pairs={{0,4},{1,5},{2,6},{3,7},{4,0},{5,1},{6,2},{7,3},{8,12},{9,13},{10,... | collective-permute-start | bytes 454664 | tf_op jit(solution)/shard_map/ppermute | solution.py:31
  14.0 7.1 %collective-permute-start.1 = (bf16[16,4736]{1,0:T(8,128)(2,1)S(1)}, bf16[16,4736]{1,0:T(8,128)(2,1)S(1)}, u32[]{:S(2)}, u32[]{:S(2)}) collective-permute-start(bf16[16,4736]{1,0:T(8,128)(2,1)S(1)} %collective-permute-done), channel_id=1, source_target_pairs={{0,2},{1,3},{2,0},{3,1},{4,6},{5,7},{6,4},{7,5},{8,10},{9,11},{10,... | collective-permute-start | bytes 454664 | tf_op jit(solution)/shard_map/ppermute | solution.py:31
  15.6 6.1 %collective-permute-start.7 = (bf16[16,5248]{1,0:T(8,128)(2,1)S(1)}, bf16[16,5248]{1,0:T(8,128)(2,1)S(1)}, u32[]{:S(2)}, u32[]{:S(2)}) collective-permute-start(bf16[16,5248]{1,0:T(8,128)(2,1)S(1)} %collective-permute-done.3), channel_id=1, source_target_pairs={{0,1},{1,0},{2,3},{3,2},{4,5},{5,4},{6,7},{7,6},{8,9},{9,8},{10,11... | collective-permute-start | bytes 503816 | tf_op jit(solution)/shard_map/ppermute | solution.py:31
  17.1 11.8 %collective-permute-start.8 = (bf16[16,5248]{1,0:T(8,128)(2,1)S(1)}, bf16[16,5248]{1,0:T(8,128)(2,1)S(1)}, u32[]{:S(2)}, u32[]{:S(2)}) collective-permute-start(bf16[16,5248]{1,0:T(8,128)(2,1)S(1)} %collective-permute-done.6), channel_id=1, source_target_pairs={{0,4},{1,5},{2,6},{3,7},{4,0},{5,1},{6,2},{7,3},{8,12},{9,13},{10,... | collective-permute-start | bytes 503816 | tf_op jit(solution)/shard_map/ppermute | solution.py:31
  17.7 5.3 %collective-permute-start.4 = (bf16[16,4736]{1,0:T(8,128)(2,1)S(1)}, bf16[16,4736]{1,0:T(8,128)(2,1)S(1)}, u32[]{:S(2)}, u32[]{:S(2)}) collective-permute-start(bf16[16,4736]{1,0:T(8,128)(2,1)S(1)} %collective-permute-done.2), channel_id=1, source_target_pairs={{0,2},{1,3},{2,0},{3,1},{4,6},{5,7},{6,4},{7,5},{8,10},{9,11},{10,... | collective-permute-start | bytes 454664 | tf_op jit(solution)/shard_map/ppermute | solution.py:31
  18.2 19.0 %copy-start = (bf16[8192,256]{1,0:T(8,128)(2,1)S(1)}, bf16[8192,256]{1,0:T(8,128)(2,1)}, u32[]{:S(2)}) copy-start(bf16[8192,256]{1,0:T(8,128)(2,1)} %refs_17_.1) | copy-start | bytes 12582916
  18.2 10.7 %collective-permute-start.11 = (bf16[16,4736]{1,0:T(8,128)(2,1)S(1)}, bf16[16,4736]{1,0:T(8,128)(2,1)S(1)}, u32[]{:S(2)}, u32[]{:S(2)}) collective-permute-start(bf16[16,4736]{1,0:T(8,128)(2,1)S(1)} %get-tuple-element.38), channel_id=1, source_target_pairs={{0,12},{1,13},{2,14},{3,15},{4,8},{5,9},{6,10},{7,11},{8,4},{9,5},... | collective-permute-start | bytes 454664 | tf_op jit(solution)/shard_map/ppermute | solution.py:31
  21.2 7.7 %collective-permute-start.10 = (bf16[16,4736]{1,0:T(8,128)(2,1)S(1)}, bf16[16,4736]{1,0:T(8,128)(2,1)S(1)}, u32[]{:S(2)}, u32[]{:S(2)}) collective-permute-start(bf16[16,4736]{1,0:T(8,128)(2,1)S(1)} %collective-permute-done), channel_id=1, source_target_pairs={{0,1},{1,0},{2,3},{3,2},{4,5},{5,4},{6,7},{7,6},{8,9},{9,8},{10,11... | collective-permute-start | bytes 454664 | tf_op jit(solution)/shard_map/ppermute | solution.py:31
  21.7 15.5 %collective-permute-start.9 = (bf16[16,5248]{1,0:T(8,128)(2,1)S(1)}, bf16[16,5248]{1,0:T(8,128)(2,1)S(1)}, u32[]{:S(2)}, u32[]{:S(2)}) collective-permute-start(bf16[16,5248]{1,0:T(8,128)(2,1)S(1)} %collective-permute-done.7), channel_id=1, source_target_pairs={{0,4},{1,5},{2,6},{3,7},{4,0},{5,1},{6,2},{7,3},{8,12},{9,13},{10,... | collective-permute-start | bytes 503816 | tf_op jit(solution)/shard_map/ppermute | solution.py:31
  23.0 9.4 %collective-permute-start.5 = (bf16[16,4736]{1,0:T(8,128)(2,1)S(1)}, bf16[16,4736]{1,0:T(8,128)(2,1)S(1)}, u32[]{:S(2)}, u32[]{:S(2)}) collective-permute-start(bf16[16,4736]{1,0:T(8,128)(2,1)S(1)} %collective-permute-done.1), channel_id=1, source_target_pairs={{0,1},{1,0},{2,3},{3,2},{4,5},{5,4},{6,7},{7,6},{8,9},{9,8},{10,11... | collective-permute-start | bytes 454664 | tf_op jit(solution)/shard_map/ppermute | solution.py:31
  28.9 8.2 %collective-permute-start.12 = (bf16[16,4736]{1,0:T(8,128)(2,1)S(1)}, bf16[16,4736]{1,0:T(8,128)(2,1)S(1)}, u32[]{:S(2)}, u32[]{:S(2)}) collective-permute-start(bf16[16,4736]{1,0:T(8,128)(2,1)S(1)} %collective-permute-done.11), channel_id=1, source_target_pairs={{0,1},{1,0},{2,3},{3,2},{4,5},{5,4},{6,7},{7,6},{8,9},{9,8},{10,11... | collective-permute-start | bytes 454664 | tf_op jit(solution)/shard_map/ppermute | solution.py:31
  29.5 7.6 %collective-permute-start.13 = (bf16[16,4736]{1,0:T(8,128)(2,1)S(1)}, bf16[16,4736]{1,0:T(8,128)(2,1)S(1)}, u32[]{:S(2)}, u32[]{:S(2)}) collective-permute-start(bf16[16,4736]{1,0:T(8,128)(2,1)S(1)} %collective-permute-done.11), channel_id=1, source_target_pairs={{0,2},{1,3},{2,0},{3,1},{4,6},{5,7},{6,4},{7,5},{8,10},{9,11},{10,... | collective-permute-start | bytes 454664 | tf_op jit(solution)/shard_map/ppermute | solution.py:31
  30.1 7.1 %collective-permute-start.14 = (bf16[16,4736]{1,0:T(8,128)(2,1)S(1)}, bf16[16,4736]{1,0:T(8,128)(2,1)S(1)}, u32[]{:S(2)}, u32[]{:S(2)}) collective-permute-start(bf16[16,4736]{1,0:T(8,128)(2,1)S(1)} %collective-permute-done.11), channel_id=1, source_target_pairs={{0,3},{1,2},{2,1},{3,0},{4,7},{5,6},{6,5},{7,4},{8,11},{9,10},{10,... | collective-permute-start | bytes 454664 | tf_op jit(solution)/shard_map/ppermute | solution.py:31
  37.1 14.9 %copy-start.1 = (f32[4096]{0:T(1024)S(1)}, f32[4096]{0:T(1024)}, u32[]{:S(2)}) copy-start(f32[4096]{0:T(1024)} %param.17) | copy-start | bytes 49156
  38.5 4.5 %collective-permute-start.17 = (bf16[128,256]{1,0:T(8,128)(2,1)S(1)}, bf16[128,256]{1,0:T(8,128)(2,1)S(1)}, u32[]{:S(2)}, u32[]{:S(2)}) collective-permute-start(bf16[128,256]{1,0:T(8,128)(2,1)S(1)} %get-tuple-element.41), channel_id=1, source_target_pairs={{0,4},{1,5},{2,6},{3,7},{4,0},{5,1},{6,2},{7,3},{8,12},{9,13},{10,... | collective-permute-start | bytes 196616 | tf_op jit(solution)/shard_map/ppermute | solution.py:31
  39.0 7.5 %collective-permute-start.15 = (bf16[128,256]{1,0:T(8,128)(2,1)S(1)}, bf16[128,256]{1,0:T(8,128)(2,1)S(1)}, u32[]{:S(2)}, u32[]{:S(2)}) collective-permute-start(bf16[128,256]{1,0:T(8,128)(2,1)S(1)} %get-tuple-element.41), channel_id=1, source_target_pairs={{0,8},{1,9},{2,10},{3,11},{4,12},{5,13},{6,14},{7,15},{8,0},{9,1},... | collective-permute-start | bytes 196616 | tf_op jit(solution)/shard_map/ppermute | solution.py:31
  42.4 6.1 %collective-permute-start.16 = (bf16[128,256]{1,0:T(8,128)(2,1)S(1)}, bf16[128,256]{1,0:T(8,128)(2,1)S(1)}, u32[]{:S(2)}, u32[]{:S(2)}) collective-permute-start(bf16[128,256]{1,0:T(8,128)(2,1)S(1)} %get-tuple-element.41), channel_id=1, source_target_pairs={{0,12},{1,13},{2,14},{3,15},{4,8},{5,9},{6,10},{7,11},{8,4},{9,5},... | collective-permute-start | bytes 196616 | tf_op jit(solution)/shard_map/ppermute | solution.py:31
  42.9 13.5 %slice-start = ((s8[6291456]{0:T(1024)(128)(4,1)}), s8[4194304]{0:T(1024)(128)(4,1)S(1)}, s32[]{:S(2)}) async-start(s8[6291456]{0:T(1024)(128)(4,1)} %bitcast.34), calls=%async_computation | async-start | bytes 8388608
  43.0 7.6 %collective-permute-start.21 = (bf16[2,128,256]{2,1,0:T(8,128)(2,1)S(1)}, bf16[2,128,256]{2,1,0:T(8,128)(2,1)S(1)}, u32[]{:S(2)}, u32[]{:S(2)}) collective-permute-start(bf16[2,128,256]{2,1,0:T(8,128)(2,1)S(1)} %pad_maximum_fusion.1.refs_0_), channel_id=1, source_target_pairs={{0,1},{1,0},{2,3},{3,2},{4,5},{5,4},{6,7},{7,6},{8,9},{9,8},{10,11... | collective-permute-start | bytes 393224 | tf_op jit(solution)/shard_map/ppermute | solution.py:31
  44.0 8.1 %collective-permute-start.22 = (bf16[2,128,256]{2,1,0:T(8,128)(2,1)S(1)}, bf16[2,128,256]{2,1,0:T(8,128)(2,1)S(1)}, u32[]{:S(2)}, u32[]{:S(2)}) collective-permute-start(bf16[2,128,256]{2,1,0:T(8,128)(2,1)S(1)} %pad_maximum_fusion.1.refs_0_), channel_id=1, source_target_pairs={{0,2},{1,3},{2,0},{3,1},{4,6},{5,7},{6,4},{7,5},{8,10},{9,11},{10,... | collective-permute-start | bytes 393224 | tf_op jit(solution)/shard_map/ppermute | solution.py:31
  44.9 7.1 %collective-permute-start.23 = (bf16[2,128,256]{2,1,0:T(8,128)(2,1)S(1)}, bf16[2,128,256]{2,1,0:T(8,128)(2,1)S(1)}, u32[]{:S(2)}, u32[]{:S(2)}) collective-permute-start(bf16[2,128,256]{2,1,0:T(8,128)(2,1)S(1)} %pad_maximum_fusion.1.refs_0_), channel_id=1, source_target_pairs={{0,3},{1,2},{2,1},{3,0},{4,7},{5,6},{6,5},{7,4},{8,11},{9,10},{10,... | collective-permute-start | bytes 393224 | tf_op jit(solution)/shard_map/ppermute | solution.py:31
  48.5 5.2 %collective-permute-start.18 = (bf16[2,128,256]{2,1,0:T(8,128)(2,1)S(1)}, bf16[2,128,256]{2,1,0:T(8,128)(2,1)S(1)}, u32[]{:S(2)}, u32[]{:S(2)}) collective-permute-start(bf16[2,128,256]{2,1,0:T(8,128)(2,1)S(1)} %pad_maximum_fusion.refs_0_), channel_id=1, source_target_pairs={{0,1},{1,0},{2,3},{3,2},{4,5},{5,4},{6,7},{7,6},{8,9},{9,8},{10,11... | collective-permute-start | bytes 393224 | tf_op jit(solution)/shard_map/ppermute | solution.py:31
  49.7 5.0 %collective-permute-start.19 = (bf16[2,128,256]{2,1,0:T(8,128)(2,1)S(1)}, bf16[2,128,256]{2,1,0:T(8,128)(2,1)S(1)}, u32[]{:S(2)}, u32[]{:S(2)}) collective-permute-start(bf16[2,128,256]{2,1,0:T(8,128)(2,1)S(1)} %pad_maximum_fusion.refs_0_), channel_id=1, source_target_pairs={{0,2},{1,3},{2,0},{3,1},{4,6},{5,7},{6,4},{7,5},{8,10},{9,11},{10,... | collective-permute-start | bytes 393224 | tf_op jit(solution)/shard_map/ppermute | solution.py:31
  50.6 5.9 %collective-permute-start.20 = (bf16[2,128,256]{2,1,0:T(8,128)(2,1)S(1)}, bf16[2,128,256]{2,1,0:T(8,128)(2,1)S(1)}, u32[]{:S(2)}, u32[]{:S(2)}) collective-permute-start(bf16[2,128,256]{2,1,0:T(8,128)(2,1)S(1)} %pad_maximum_fusion.refs_0_), channel_id=1, source_target_pairs={{0,3},{1,2},{2,1},{3,0},{4,7},{5,6},{6,5},{7,4},{8,11},{9,10},{10,... | collective-permute-start | bytes 393224 | tf_op jit(solution)/shard_map/ppermute | solution.py:31
  52.1 4.4 %slice-start.1 = ((s8[6291456]{0:T(1024)(128)(4,1)}), s8[2097152]{0:T(1024)(128)(4,1)S(1)}, s32[]{:S(2)}) async-start(s8[6291456]{0:T(1024)(128)(4,1)} %bitcast.34), calls=%async_computation.1 | async-start | bytes 4194304
  58.6 7.4 %collective-permute-start.28 = (bf16[2,16,2048]{2,1,0:T(8,128)(2,1)S(1)}, bf16[2,16,2048]{2,1,0:T(8,128)(2,1)S(1)}, u32[]{:S(2)}, u32[]{:S(2)}) collective-permute-start(bf16[2,16,2048]{2,1,0:T(8,128)(2,1)S(1)} %get-tuple-element.54), channel_id=1, source_target_pairs={{0,3},{1,2},{2,1},{3,0},{4,7},{5,6},{6,5},{7,4},{8,11},{9,10},{10,... | collective-permute-start | bytes 393224 | tf_op jit(solution)/shard_map/ppermute | solution.py:31
  60.2 6.8 %collective-permute-start.29 = (bf16[2,16,2048]{2,1,0:T(8,128)(2,1)S(1)}, bf16[2,16,2048]{2,1,0:T(8,128)(2,1)S(1)}, u32[]{:S(2)}, u32[]{:S(2)}) collective-permute-start(bf16[2,16,2048]{2,1,0:T(8,128)(2,1)S(1)} %get-tuple-element.55), channel_id=1, source_target_pairs={{0,1},{1,0},{2,3},{3,2},{4,5},{5,4},{6,7},{7,6},{8,9},{9,8},{10,11... | collective-permute-start | bytes 393224 | tf_op jit(solution)/shard_map/ppermute | solution.py:31
  61.3 6.2 %collective-permute-start.30 = (bf16[2,16,2048]{2,1,0:T(8,128)(2,1)S(1)}, bf16[2,16,2048]{2,1,0:T(8,128)(2,1)S(1)}, u32[]{:S(2)}, u32[]{:S(2)}) collective-permute-start(bf16[2,16,2048]{2,1,0:T(8,128)(2,1)S(1)} %get-tuple-element.56), channel_id=1, source_target_pairs={{0,2},{1,3},{2,0},{3,1},{4,6},{5,7},{6,4},{7,5},{8,10},{9,11},{10,... | collective-permute-start | bytes 393224 | tf_op jit(solution)/shard_map/ppermute | solution.py:31
  62.2 7.7 %collective-permute-start.24 = (bf16[2,16,2048]{2,1,0:T(8,128)(2,1)S(1)}, bf16[2,16,2048]{2,1,0:T(8,128)(2,1)S(1)}, u32[]{:S(2)}, u32[]{:S(2)}) collective-permute-start(bf16[2,16,2048]{2,1,0:T(8,128)(2,1)S(1)} %get-tuple-element.50), channel_id=1, source_target_pairs={{0,3},{1,2},{2,1},{3,0},{4,7},{5,6},{6,5},{7,4},{8,11},{9,10},{10,... | collective-permute-start | bytes 393224 | tf_op jit(solution)/shard_map/ppermute | solution.py:31
  63.7 6.2 %collective-permute-start.25 = (bf16[2,16,2048]{2,1,0:T(8,128)(2,1)S(1)}, bf16[2,16,2048]{2,1,0:T(8,128)(2,1)S(1)}, u32[]{:S(2)}, u32[]{:S(2)}) collective-permute-start(bf16[2,16,2048]{2,1,0:T(8,128)(2,1)S(1)} %get-tuple-element.51), channel_id=1, source_target_pairs={{0,1},{1,0},{2,3},{3,2},{4,5},{5,4},{6,7},{7,6},{8,9},{9,8},{10,11... | collective-permute-start | bytes 393224 | tf_op jit(solution)/shard_map/ppermute | solution.py:31
  66.0 5.0 %collective-permute-start.26 = (bf16[2,16,2048]{2,1,0:T(8,128)(2,1)S(1)}, bf16[2,16,2048]{2,1,0:T(8,128)(2,1)S(1)}, u32[]{:S(2)}, u32[]{:S(2)}) collective-permute-start(bf16[2,16,2048]{2,1,0:T(8,128)(2,1)S(1)} %get-tuple-element.52), channel_id=1, source_target_pairs={{0,2},{1,3},{2,0},{3,1},{4,6},{5,7},{6,4},{7,5},{8,10},{9,11},{10,... | collective-permute-start | bytes 393224 | tf_op jit(solution)/shard_map/ppermute | solution.py:31
  67.6 5.4 %collective-permute-start.31 = (bf16[16,2048]{1,0:T(8,128)(2,1)S(1)}, bf16[16,2048]{1,0:T(8,128)(2,1)S(1)}, u32[]{:S(2)}, u32[]{:S(2)}) collective-permute-start(bf16[16,2048]{1,0:T(8,128)(2,1)S(1)} %get-tuple-element.57), channel_id=1, source_target_pairs={{0,8},{1,9},{2,10},{3,11},{4,12},{5,13},{6,14},{7,15},{8,0},{9,1},... | collective-permute-start | bytes 196616 | tf_op jit(solution)/shard_map/ppermute | solution.py:31
  69.1 6.1 %collective-permute-start.32 = (bf16[16,2048]{1,0:T(8,128)(2,1)S(1)}, bf16[16,2048]{1,0:T(8,128)(2,1)S(1)}, u32[]{:S(2)}, u32[]{:S(2)}) collective-permute-start(bf16[16,2048]{1,0:T(8,128)(2,1)S(1)} %get-tuple-element.58), channel_id=1, source_target_pairs={{0,12},{1,13},{2,14},{3,15},{4,8},{5,9},{6,10},{7,11},{8,4},{9,5},... | collective-permute-start | bytes 196616 | tf_op jit(solution)/shard_map/ppermute | solution.py:31
  71.1 4.8 %collective-permute-start.27 = (bf16[16,2048]{1,0:T(8,128)(2,1)S(1)}, bf16[16,2048]{1,0:T(8,128)(2,1)S(1)}, u32[]{:S(2)}, u32[]{:S(2)}) collective-permute-start(bf16[16,2048]{1,0:T(8,128)(2,1)S(1)} %slice_bitcast_fusion.2), channel_id=1, source_target_pairs={{0,4},{1,5},{2,6},{3,7},{4,0},{5,1},{6,2},{7,3},{8,12},{9,13},{10,... | collective-permute-start | bytes 196616 | tf_op jit(solution)/shard_map/ppermute | solution.py:31
  75.9 1.3 %collective-permute-start.33 = (bf16[8,2048]{1,0:T(8,128)(2,1)S(1)}, bf16[8,2048]{1,0:T(8,128)(2,1)S(1)}, u32[]{:S(2)}, u32[]{:S(2)}) collective-permute-start(bf16[8,2048]{1,0:T(8,128)(2,1)S(1)} %get-tuple-element.60), channel_id=1, source_target_pairs={{0,16},{16,0},{1,17},{17,1},{2,18},{18,2},{3,19},{19,3},{4,20},{20... | collective-permute-start | bytes 98312 | tf_op jit(solution)/shard_map/ppermute | solution.py:583

commit v3 on v2

--- a/solution.py
+++ b/solution.py
@@ -49,17 +49,22 @@
 
 def gather(planes):
     own = planes[0]
-    z1, z2 = (exchange(planes[k], 4 * k) for k in (1, 2))
-    x0, y0 = (exchange(own, f) for f in (1, 2))
-    z3 = exchange(after(planes[3], z1), 12)
-    x1 = exchange(x0, 4)
-    c0 = exchange(y0, 1)
-    y1 = exchange(after(z1, y0), 2)
-    x2, y2 = (exchange(z2, f) for f in (1, 2))
+    z1 = exchange(planes[1], 4)
+    z2 = exchange(planes[2], 8)
+    x0 = exchange(own, 1)
+    y0 = exchange(own, 2)
+    z3 = exchange(after(planes[3], z2), 12)
+    c0 = exchange(x0, 2)
+    x1 = exchange(after(x0, z1), 4)
+    y1 = exchange(after(z1, z3), 2)
+    x2 = exchange(after(z2, y0), 1)
+    y2 = exchange(z2, 2)
     c1 = exchange(c0, 4)
-    c2 = exchange(after(y2, y1), 1)
-    d3, x3, y3 = (exchange(after(z3, x1, y1, x2), f) for f in (3, 1, 2))
-    return [own, x0, y0, c0, z1, x1, y1, c1, z2, x2, y2, c2, z3, x3, y3, d3]
+    c2 = exchange(after(x2, x1, z2, z3), 2)
+    x3 = exchange(after(z3, y2, x2), 1)
+    y3 = exchange(z3, 2)
+    c3 = exchange(after(y3, x1), 1)
+    return [own, x0, y0, c0, z1, x1, y1, c1, z2, x2, y2, c2, z3, x3, y3, c3]
 
 
 BY_NEXT_PLANE = (5, 7)
@@ -555,7 +560,7 @@
     if groups == CHIPS:
         *carried, gain = attend(groups, PLANES, *arrays)
         pieces = gather(carried)
-        staged, done = stage(gate_up, pieces[11])
+        staged, done = stage(gate_up, pieces[9])
         y, mix = project([p[None] for p in pieces], out_weight, gain, waits=(done,))
         nears, fars = gather_pairs(y)
         begun = near(nears, staged, norm_gain)

time: 78 us -> 76 us (0.974)
  waiting for transfers between devices: 21.2 us -> 17.1 us
  starting transfers between devices: 43.7 us -> 45.8 us
    ppermute x33, waiting for transfers between devices: 20 us -> 15.9 us  [exchange(): return lax.ppermute(value, 'grp', [(g, g ^ bits) for g in range(CHIPS)])]
    ppermute x33, starting transfers between devices: 43.6 us -> 45.7 us  [exchange(): return lax.ppermute(value, 'grp', [(g, g ^ bits) for g in range(CHIPS)])]
  transfers between devices with their start and end apart: 34 -> 34, of which waited for: 13 -> 14; matrix products, arithmetic and copies ran while one was open for 0% -> 0% of each run, Pallas kernels for 7% -> 8%
where the time goes in v3:
time: 76 us; the launch traced here: 75.8 us
  starting transfers between devices  45.8 us (60%)
  waiting for transfers between devices  17.1 us (23%)
  Pallas kernels  11.9 us (16%)
  other arithmetic  0.86 us (1%)
    ppermute x33, starting transfers between devices, exchange(): return lax.ppermute(value, 'grp', [(g, g ^ bits) for g in range(CHIPS)])  45.7 us
    ppermute x33, waiting for transfers between devices, exchange(): return lax.ppermute(value, 'grp', [(g, g ^ bits) for g in range(CHIPS)])  15.9 us
    pallas_call x1, Pallas kernels, stage(): pl.pallas_call(stage_kernel, in_specs=[pl.BlockSpec(memory_space=pl.ANY),...  4.72 us
    pallas_call x1, Pallas kernels, attend(): pl.pallas_call(functools.partial(attend_kernel, planes), in_specs=[hbm_sp...  2.62 us
    pallas_call x1, Pallas kernels, experts(): pl.pallas_call(functools.partial(expert_kernel, count, outs, bool(begun))...  2.15 us
  transfers between devices with their start and end apart: 34, of which 14 were waited for; matrix products, arithmetic and copies ran while one was open for 0% of the time, Pallas kernels for 8%

profile of v3, /device:TPU:0, one launch (start us, length us, event | category | flops | bytes accessed | tf_op | source)
XLA Modules:
  0.0 75.8 jit_solution(1777126210746891198)
XLA Ops:
  0.0 2.6 %attend.1 = (bf16[16,5248]{1,0:T(8,128)(2,1)S(1)}, bf16[16,4736]{1,0:T(8,128)(2,1)S(1)}, bf16[16,4736]{1,0:T(8,128)(2,1)S(1)}, bf16[16,4736]{1,0:T(8,128)(2,1)S(1)}, f32[1,256]{1,0:T(1,128)S(1)}) custom-call(s32[8,16]{1,0:T(8,128)} %bitcast.59, f32[8,16]{1,0:T(8,128)} %bitcast.60, s32[16]{0:T(128)} %len_hbm.1, f32[16,1,256]{2,1,0:T(1,128)} %bitcast.52, ...), custom_call_target="tpu_custom_call" | custom-call | tf_op jit(solution)/shard_map/attend/pallas_call | solution.py:219
  2.6 4.1 %collective-permute-start = (bf16[16,4736]{1,0:T(8,128)(2,1)S(1)}, bf16[16,4736]{1,0:T(8,128)(2,1)S(1)}, u32[]{:S(2)}, u32[]{:S(2)}) collective-permute-start(bf16[16,4736]{1,0:T(8,128)(2,1)S(1)} %get-tuple-element.34), channel_id=1, source_target_pairs={{0,8},{1,9},{2,10},{3,11},{4,12},{5,13},{6,14},{7,15},{8,0},{9,1},... | collective-permute-start | bytes 454664 | tf_op jit(solution)/shard_map/ppermute | solution.py:31
  6.7 1.5 %collective-permute-start.3 = (bf16[16,5248]{1,0:T(8,128)(2,1)S(1)}, bf16[16,5248]{1,0:T(8,128)(2,1)S(1)}, u32[]{:S(2)}, u32[]{:S(2)}) collective-permute-start(bf16[16,5248]{1,0:T(8,128)(2,1)S(1)} %get-tuple-element.35), channel_id=1, source_target_pairs={{0,1},{1,0},{2,3},{3,2},{4,5},{5,4},{6,7},{7,6},{8,9},{9,8},{10,11... | collective-permute-start | bytes 503816 | tf_op jit(solution)/shard_map/ppermute | solution.py:31
  8.2 1.5 %collective-permute-start.1 = (bf16[16,5248]{1,0:T(8,128)(2,1)S(1)}, bf16[16,5248]{1,0:T(8,128)(2,1)S(1)}, u32[]{:S(2)}, u32[]{:S(2)}) collective-permute-start(bf16[16,5248]{1,0:T(8,128)(2,1)S(1)} %get-tuple-element.35), channel_id=1, source_target_pairs={{0,2},{1,3},{2,0},{3,1},{4,6},{5,7},{6,4},{7,5},{8,10},{9,11},{10,... | collective-permute-start | bytes 503816 | tf_op jit(solution)/shard_map/ppermute | solution.py:31
  9.7 1.6 %collective-permute-start.5 = (bf16[16,4736]{1,0:T(8,128)(2,1)S(1)}, bf16[16,4736]{1,0:T(8,128)(2,1)S(1)}, u32[]{:S(2)}, u32[]{:S(2)}) collective-permute-start(bf16[16,4736]{1,0:T(8,128)(2,1)S(1)} %get-tuple-element.38), channel_id=1, source_target_pairs={{0,4},{1,5},{2,6},{3,7},{4,0},{5,1},{6,2},{7,3},{8,12},{9,13},{10,... | collective-permute-start | bytes 454664 | tf_op jit(solution)/shard_map/ppermute | solution.py:31
  11.3 2.7 %collective-permute-done = bf16[16,4736]{1,0:T(8,128)(2,1)S(1)} collective-permute-done((bf16[16,4736]{1,0:T(8,128)(2,1)S(1)}, bf16[16,4736]{1,0:T(8,128)(2,1)S(1)}, u32[]{:S(2)}, u32[]{:S(2)}) %collective-permute-start) | collective-permute-done | bytes 151584 | tf_op jit(solution)/shard_map/ppermute | solution.py:31
  14.0 3.5 %collective-permute-start.7 = (bf16[16,4736]{1,0:T(8,128)(2,1)S(1)}, bf16[16,4736]{1,0:T(8,128)(2,1)S(1)}, u32[]{:S(2)}, u32[]{:S(2)}) collective-permute-start(bf16[16,4736]{1,0:T(8,128)(2,1)S(1)} %get-tuple-element.41), channel_id=1, source_target_pairs={{0,12},{1,13},{2,14},{3,15},{4,8},{5,9},{6,10},{7,11},{8,4},{9,5},... | collective-permute-start | bytes 454664 | tf_op jit(solution)/shard_map/ppermute | solution.py:31
  17.6 1.5 %collective-permute-start.4 = (bf16[16,5248]{1,0:T(8,128)(2,1)S(1)}, bf16[16,5248]{1,0:T(8,128)(2,1)S(1)}, u32[]{:S(2)}, u32[]{:S(2)}) collective-permute-start(bf16[16,5248]{1,0:T(8,128)(2,1)S(1)} %collective-permute-done.3), channel_id=1, source_target_pairs={{0,2},{1,3},{2,0},{3,1},{4,6},{5,7},{6,4},{7,5},{8,10},{9,11},{10,... | collective-permute-start | bytes 503816 | tf_op jit(solution)/shard_map/ppermute | solution.py:31
  19.1 0.5 collective-permute-start.10
  19.6 1.5 %collective-permute-start.2 = (bf16[16,4736]{1,0:T(8,128)(2,1)S(1)}, bf16[16,4736]{1,0:T(8,128)(2,1)S(1)}, u32[]{:S(2)}, u32[]{:S(2)}) collective-permute-start(bf16[16,4736]{1,0:T(8,128)(2,1)S(1)} %collective-permute-done), channel_id=1, source_target_pairs={{0,1},{1,0},{2,3},{3,2},{4,5},{5,4},{6,7},{7,6},{8,9},{9,8},{10,11... | collective-permute-start | bytes 454664 | tf_op jit(solution)/shard_map/ppermute | solution.py:31
  21.1 1.5 %collective-permute-done.7 = bf16[16,4736]{1,0:T(8,128)(2,1)S(1)} collective-permute-done((bf16[16,4736]{1,0:T(8,128)(2,1)S(1)}, bf16[16,4736]{1,0:T(8,128)(2,1)S(1)}, u32[]{:S(2)}, u32[]{:S(2)}) %collective-permute-start.7) | collective-permute-done | bytes 151584 | tf_op jit(solution)/shard_map/ppermute | solution.py:31
  22.6 1.6 %collective-permute-start.13 = (bf16[16,4736]{1,0:T(8,128)(2,1)S(1)}, bf16[16,4736]{1,0:T(8,128)(2,1)S(1)}, u32[]{:S(2)}, u32[]{:S(2)}) collective-permute-start(bf16[16,4736]{1,0:T(8,128)(2,1)S(1)} %collective-permute-done.7), channel_id=1, source_target_pairs={{0,2},{1,3},{2,0},{3,1},{4,6},{5,7},{6,4},{7,5},{8,10},{9,11},{10,... | collective-permute-start | bytes 454664 | tf_op jit(solution)/shard_map/ppermute | solution.py:31
  24.2 0.6 collective-permute-done.4
  24.8 0.5 collective-permute-start.9
  25.3 2.7 %collective-permute-done.10 = bf16[16,4736]{1,0:T(8,128)(2,1)S(1)} collective-permute-done((bf16[16,4736]{1,0:T(8,128)(2,1)S(1)}, bf16[16,4736]{1,0:T(8,128)(2,1)S(1)}, u32[]{:S(2)}, u32[]{:S(2)}) %collective-permute-start.10) | collective-permute-done | bytes 151584 | tf_op jit(solution)/shard_map/ppermute | solution.py:31
  28.0 1.5 %collective-permute-start.8 = (bf16[16,4736]{1,0:T(8,128)(2,1)S(1)}, bf16[16,4736]{1,0:T(8,128)(2,1)S(1)}, u32[]{:S(2)}, u32[]{:S(2)}) collective-permute-start(bf16[16,4736]{1,0:T(8,128)(2,1)S(1)} %collective-permute-done.5), channel_id=1, source_target_pairs={{0,2},{1,3},{2,0},{3,1},{4,6},{5,7},{6,4},{7,5},{8,10},{9,11},{10,... | collective-permute-start | bytes 454664 | tf_op jit(solution)/shard_map/ppermute | solution.py:31
  29.5 1.4 %collective-permute-start.12 = (bf16[16,4736]{1,0:T(8,128)(2,1)S(1)}, bf16[16,4736]{1,0:T(8,128)(2,1)S(1)}, u32[]{:S(2)}, u32[]{:S(2)}) collective-permute-start(bf16[16,4736]{1,0:T(8,128)(2,1)S(1)} %collective-permute-done.7), channel_id=1, source_target_pairs={{0,1},{1,0},{2,3},{3,2},{4,5},{5,4},{6,7},{7,6},{8,9},{9,8},{10,11... | collective-permute-start | bytes 454664 | tf_op jit(solution)/shard_map/ppermute | solution.py:31
  30.9 0.6 collective-permute-start.11
  31.5 1.2 %collective-permute-start.14 = (bf16[16,4736]{1,0:T(8,128)(2,1)S(1)}, bf16[16,4736]{1,0:T(8,128)(2,1)S(1)}, u32[]{:S(2)}, u32[]{:S(2)}) collective-permute-start(bf16[16,4736]{1,0:T(8,128)(2,1)S(1)} %collective-permute-done.13), channel_id=1, source_target_pairs={{0,1},{1,0},{2,3},{3,2},{4,5},{5,4},{6,7},{7,6},{8,9},{9,8},{10,11... | collective-permute-start | bytes 454664 | tf_op jit(solution)/shard_map/ppermute | solution.py:31
  32.7 4.7 %stage.1 = (bf16[4096,1536]{1,0:T(8,128)(2,1)S(1)}, f32[8,128]{1,0:T(8,128)S(1)}) custom-call(bf16[16,4736]{1,0:T(8,128)(2,1)S(1)} %collective-permute-done.2._, bf16[1,4096,1536]{2,1,0:T(8,128)(2,1)} %gu_hbm.1), custom_call_target="tpu_custom_call" | custom-call | bytes 12582912 | tf_op jit(solution)/shard_map/stage/pallas_call | solution.py:360
  37.6 1.3 %project.1 = (bf16[128,256]{1,0:T(8,128)(2,1)S(1)}, f32[128,1]{1,0:T(8,128)S(1)}) custom-call(f32[8,128]{1,0:T(8,128)S(1)} %get-tuple-element.37.refs_0_, bf16[1,16,5248]{2,1,0:T(8,128)(2,1)S(1)} %bitcast.37, bf16[1,16,5248]{2,1,0:T(8,128)(2,1)S(1)} %bitcast.38, bf16[1,16,5248]{2,1,0:T(8,128)(2,1)S(1)} %bitcast.39, bf16[1,16,5248]{2,1,0:T(8,128)(2,1)S(1)} %bitcast.40, ...), custom_call_target="tpu_custom_call" | custom-call | tf_op jit(solution)/shard_map/project/pallas_call | solution.py:309
  38.9 2.3 %collective-permute-start.15 = (bf16[128,256]{1,0:T(8,128)(2,1)S(1)}, bf16[128,256]{1,0:T(8,128)(2,1)S(1)}, u32[]{:S(2)}, u32[]{:S(2)}) collective-permute-start(bf16[128,256]{1,0:T(8,128)(2,1)S(1)} %get-tuple-element.47), channel_id=1, source_target_pairs={{0,8},{1,9},{2,10},{3,11},{4,12},{5,13},{6,14},{7,15},{8,0},{9,1},... | collective-permute-start | bytes 196616 | tf_op jit(solution)/shard_map/ppermute | solution.py:31
  41.3 2.1 %collective-permute-start.16 = (bf16[128,256]{1,0:T(8,128)(2,1)S(1)}, bf16[128,256]{1,0:T(8,128)(2,1)S(1)}, u32[]{:S(2)}, u32[]{:S(2)}) collective-permute-start(bf16[128,256]{1,0:T(8,128)(2,1)S(1)} %get-tuple-element.47), channel_id=1, source_target_pairs={{0,12},{1,13},{2,14},{3,15},{4,8},{5,9},{6,10},{7,11},{8,4},{9,5},... | collective-permute-start | bytes 196616 | tf_op jit(solution)/shard_map/ppermute | solution.py:31
  43.3 2.2 %collective-permute-start.21 = (bf16[2,128,256]{2,1,0:T(8,128)(2,1)S(1)}, bf16[2,128,256]{2,1,0:T(8,128)(2,1)S(1)}, u32[]{:S(2)}, u32[]{:S(2)}) collective-permute-start(bf16[2,128,256]{2,1,0:T(8,128)(2,1)S(1)} %pad_maximum_fusion.1.refs_0_), channel_id=1, source_target_pairs={{0,1},{1,0},{2,3},{3,2},{4,5},{5,4},{6,7},{7,6},{8,9},{9,8},{10,11... | collective-permute-start | bytes 393224 | tf_op jit(solution)/shard_map/ppermute | solution.py:31
  45.5 1.4 %collective-permute-start.22 = (bf16[2,128,256]{2,1,0:T(8,128)(2,1)S(1)}, bf16[2,128,256]{2,1,0:T(8,128)(2,1)S(1)}, u32[]{:S(2)}, u32[]{:S(2)}) collective-permute-start(bf16[2,128,256]{2,1,0:T(8,128)(2,1)S(1)} %pad_maximum_fusion.1.refs_0_), channel_id=1, source_target_pairs={{0,2},{1,3},{2,0},{3,1},{4,6},{5,7},{6,4},{7,5},{8,10},{9,11},{10,... | collective-permute-start | bytes 393224 | tf_op jit(solution)/shard_map/ppermute | solution.py:31
  47.0 0.3 collective-permute-done.16
  47.3 1.7 %collective-permute-start.18 = (bf16[2,128,256]{2,1,0:T(8,128)(2,1)S(1)}, bf16[2,128,256]{2,1,0:T(8,128)(2,1)S(1)}, u32[]{:S(2)}, u32[]{:S(2)}) collective-permute-start(bf16[2,128,256]{2,1,0:T(8,128)(2,1)S(1)} %pad_maximum_fusion.refs_0_), channel_id=1, source_target_pairs={{0,1},{1,0},{2,3},{3,2},{4,5},{5,4},{6,7},{7,6},{8,9},{9,8},{10,11... | collective-permute-start | bytes 393224 | tf_op jit(solution)/shard_map/ppermute | solution.py:31
  49.1 1.4 %collective-permute-start.19 = (bf16[2,128,256]{2,1,0:T(8,128)(2,1)S(1)}, bf16[2,128,256]{2,1,0:T(8,128)(2,1)S(1)}, u32[]{:S(2)}, u32[]{:S(2)}) collective-permute-start(bf16[2,128,256]{2,1,0:T(8,128)(2,1)S(1)} %pad_maximum_fusion.refs_0_), channel_id=1, source_target_pairs={{0,2},{1,3},{2,0},{3,1},{4,6},{5,7},{6,4},{7,5},{8,10},{9,11},{10,... | collective-permute-start | bytes 393224 | tf_op jit(solution)/shard_map/ppermute | solution.py:31
  50.5 1.8 %collective-permute-start.20 = (bf16[2,128,256]{2,1,0:T(8,128)(2,1)S(1)}, bf16[2,128,256]{2,1,0:T(8,128)(2,1)S(1)}, u32[]{:S(2)}, u32[]{:S(2)}) collective-permute-start(bf16[2,128,256]{2,1,0:T(8,128)(2,1)S(1)} %pad_maximum_fusion.refs_0_), channel_id=1, source_target_pairs={{0,3},{1,2},{2,1},{3,0},{4,7},{5,6},{6,5},{7,4},{8,11},{9,10},{10,... | collective-permute-start | bytes 393224 | tf_op jit(solution)/shard_map/ppermute | solution.py:31
  52.2 1.0 %collective-permute-done.22.refs_2_ = bf16[2,128,256]{2,1,0:T(8,128)(2,1)S(1)} collective-permute-done((bf16[2,128,256]{2,1,0:T(8,128)(2,1)S(1)}, bf16[2,128,256]{2,1,0:T(8,128)(2,1)S(1)}, u32[]{:S(2)}, u32[]{:S(2)}) %collective-permute-start.22) | collective-permute-done | bytes 131104 | tf_op jit(solution)/shard_map/ppermute | solution.py:31
  53.3 1.1 %near.1 = (f32[128,1536]{1,0:T(8,128)S(1)}, f32[128,128]{1,0:T(8,128)S(1)}, f32[16,2048]{1,0:T(8,128)S(1)}) custom-call(bf16[2,128,256]{2,1,0:T(8,128)(2,1)S(1)} %pad_maximum_fusion.1.refs_0_, bf16[2,128,256]{2,1,0:T(8,128)(2,1)S(1)} %collective-permute-done.21.refs_1_, bf16[2,128,256]{2,1,0:T(8,128)(2,1)S(1)} %collective-permute-done.22.refs_2_, ...), custom_call_target="tpu_custom_call" | custom-call | flops 805306368 | bytes 12582912 | tf_op jit(solution)/shard_map/near/pallas_call | solution.py:406
  54.4 0.3 collective-permute-done.19.refs_2_
  54.7 1.7 %collective-permute-done.20.refs_3_ = bf16[2,128,256]{2,1,0:T(8,128)(2,1)S(1)} collective-permute-done((bf16[2,128,256]{2,1,0:T(8,128)(2,1)S(1)}, bf16[2,128,256]{2,1,0:T(8,128)(2,1)S(1)}, u32[]{:S(2)}, u32[]{:S(2)}) %collective-permute-start.20) | collective-permute-done | bytes 131104 | tf_op jit(solution)/shard_map/ppermute | solution.py:31
  56.4 2.2 %experts.1 = (bf16[2,16,2048]{2,1,0:T(8,128)(2,1)S(1)}, bf16[2,16,2048]{2,1,0:T(8,128)(2,1)S(1)}, bf16[2,16,2048]{2,1,0:T(8,128)(2,1)S(1)}, bf16[2,16,2048]{2,1,...) custom-call(bf16[2,128,256]{2,1,0:T(8,128)(2,1)S(1)} %pad_maximum_fu, ...), custom_call_target="tpu_custom_call" | custom-call | tf_op jit(solution)/shard_map/experts/pallas_call | solution.py:507
  58.5 1.8 %collective-permute-start.28 = (bf16[2,16,2048]{2,1,0:T(8,128)(2,1)S(1)}, bf16[2,16,2048]{2,1,0:T(8,128)(2,1)S(1)}, u32[]{:S(2)}, u32[]{:S(2)}) collective-permute-start(bf16[2,16,2048]{2,1,0:T(8,128)(2,1)S(1)} %get-tuple-element.60), channel_id=1, source_target_pairs={{0,3},{1,2},{2,1},{3,0},{4,7},{5,6},{6,5},{7,4},{8,11},{9,10},{10,... | collective-permute-start | bytes 393224 | tf_op jit(solution)/shard_map/ppermute | solution.py:31
  60.3 0.5 collective-permute-start.29
  60.9 1.2 %collective-permute-start.30 = (bf16[2,16,2048]{2,1,0:T(8,128)(2,1)S(1)}, bf16[2,16,2048]{2,1,0:T(8,128)(2,1)S(1)}, u32[]{:S(2)}, u32[]{:S(2)}) collective-permute-start(bf16[2,16,2048]{2,1,0:T(8,128)(2,1)S(1)} %get-tuple-element.62), channel_id=1, source_target_pairs={{0,2},{1,3},{2,0},{3,1},{4,6},{5,7},{6,4},{7,5},{8,10},{9,11},{10,... | collective-permute-start | bytes 393224 | tf_op jit(solution)/shard_map/ppermute | solution.py:31
  62.1 1.8 %collective-permute-start.24 = (bf16[2,16,2048]{2,1,0:T(8,128)(2,1)S(1)}, bf16[2,16,2048]{2,1,0:T(8,128)(2,1)S(1)}, u32[]{:S(2)}, u32[]{:S(2)}) collective-permute-start(bf16[2,16,2048]{2,1,0:T(8,128)(2,1)S(1)} %get-tuple-element.56), channel_id=1, source_target_pairs={{0,3},{1,2},{2,1},{3,0},{4,7},{5,6},{6,5},{7,4},{8,11},{9,10},{10,... | collective-permute-start | bytes 393224 | tf_op jit(solution)/shard_map/ppermute | solution.py:31
  63.8 0.5 collective-permute-start.25
  64.5 1.1 %collective-permute-start.26 = (bf16[2,16,2048]{2,1,0:T(8,128)(2,1)S(1)}, bf16[2,16,2048]{2,1,0:T(8,128)(2,1)S(1)}, u32[]{:S(2)}, u32[]{:S(2)}) collective-permute-start(bf16[2,16,2048]{2,1,0:T(8,128)(2,1)S(1)} %get-tuple-element.58), channel_id=1, source_target_pairs={{0,2},{1,3},{2,0},{3,1},{4,6},{5,7},{6,4},{7,5},{8,10},{9,11},{10,... | collective-permute-start | bytes 393224 | tf_op jit(solution)/shard_map/ppermute | solution.py:31
  65.6 0.3 collective-permute-done.30
  66.0 2.7 %collective-permute-start.32 = (bf16[16,2048]{1,0:T(8,128)(2,1)S(1)}, bf16[16,2048]{1,0:T(8,128)(2,1)S(1)}, u32[]{:S(2)}, u32[]{:S(2)}) collective-permute-start(bf16[16,2048]{1,0:T(8,128)(2,1)S(1)} %get-tuple-element.64), channel_id=1, source_target_pairs={{0,12},{1,13},{2,14},{3,15},{4,8},{5,9},{6,10},{7,11},{8,4},{9,5},... | collective-permute-start | bytes 196616 | tf_op jit(solution)/shard_map/ppermute | solution.py:31
  68.8 0.6 collective-permute-done.26
  69.5 0.3 collective-permute-start.27
  69.8 2.6 %collective-permute-done.31 = bf16[16,2048]{1,0:T(8,128)(2,1)S(1)} collective-permute-done((bf16[16,2048]{1,0:T(8,128)(2,1)S(1)}, bf16[16,2048]{1,0:T(8,128)(2,1)S(1)}, u32[]{:S(2)}, u32[]{:S(2)}) %collective-permute-start.31) | collective-permute-done | bytes 65568 | tf_op jit(solution)/shard_map/ppermute | solution.py:31
  72.4 1.5 %collective-permute-done.27 = bf16[16,2048]{1,0:T(8,128)(2,1)S(1)} collective-permute-done((bf16[16,2048]{1,0:T(8,128)(2,1)S(1)}, bf16[16,2048]{1,0:T(8,128)(2,1)S(1)}, u32[]{:S(2)}, u32[]{:S(2)}) %collective-permute-start.27) | collective-permute-done | bytes 65568 | tf_op jit(solution)/shard_map/ppermute | solution.py:31
  74.0 1.2 %collective-permute-done.33 = bf16[8,2048]{1,0:T(8,128)(2,1)S(1)} collective-permute-done((bf16[8,2048]{1,0:T(8,128)(2,1)S(1)}, bf16[8,2048]{1,0:T(8,128)(2,1)S(1)}, u32[]{:S(2)}, u32[]{:S(2)}) %collective-permute-start.33) | collective-permute-done | bytes 32800 | tf_op jit(solution)/shard_map/ppermute | solution.py:588
  75.2 0.6 maximum_select_fusion
  (44 shorter events, 0.7 us)
Async XLA Ops:
  2.6 11.4 %collective-permute-start = (bf16[16,4736]{1,0:T(8,128)(2,1)S(1)}, bf16[16,4736]{1,0:T(8,128)(2,1)S(1)}, u32[]{:S(2)}, u32[]{:S(2)}) collective-permute-start(bf16[16,4736]{1,0:T(8,128)(2,1)S(1)} %get-tuple-element.34), channel_id=1, source_target_pairs={{0,8},{1,9},{2,10},{3,11},{4,12},{5,13},{6,14},{7,15},{8,0},{9,1},... | collective-permute-start | bytes 454664 | tf_op jit(solution)/shard_map/ppermute | solution.py:31
  6.7 10.8 %collective-permute-start.3 = (bf16[16,5248]{1,0:T(8,128)(2,1)S(1)}, bf16[16,5248]{1,0:T(8,128)(2,1)S(1)}, u32[]{:S(2)}, u32[]{:S(2)}) collective-permute-start(bf16[16,5248]{1,0:T(8,128)(2,1)S(1)} %get-tuple-element.35), channel_id=1, source_target_pairs={{0,1},{1,0},{2,3},{3,2},{4,5},{5,4},{6,7},{7,6},{8,9},{9,8},{10,11... | collective-permute-start | bytes 503816 | tf_op jit(solution)/shard_map/ppermute | solution.py:31
  8.2 11.4 %collective-permute-start.1 = (bf16[16,5248]{1,0:T(8,128)(2,1)S(1)}, bf16[16,5248]{1,0:T(8,128)(2,1)S(1)}, u32[]{:S(2)}, u32[]{:S(2)}) collective-permute-start(bf16[16,5248]{1,0:T(8,128)(2,1)S(1)} %get-tuple-element.35), channel_id=1, source_target_pairs={{0,2},{1,3},{2,0},{3,1},{4,6},{5,7},{6,4},{7,5},{8,10},{9,11},{10,... | collective-permute-start | bytes 503816 | tf_op jit(solution)/shard_map/ppermute | solution.py:31
  9.7 9.3 %collective-permute-start.5 = (bf16[16,4736]{1,0:T(8,128)(2,1)S(1)}, bf16[16,4736]{1,0:T(8,128)(2,1)S(1)}, u32[]{:S(2)}, u32[]{:S(2)}) collective-permute-start(bf16[16,4736]{1,0:T(8,128)(2,1)S(1)} %get-tuple-element.38), channel_id=1, source_target_pairs={{0,4},{1,5},{2,6},{3,7},{4,0},{5,1},{6,2},{7,3},{8,12},{9,13},{10,... | collective-permute-start | bytes 454664 | tf_op jit(solution)/shard_map/ppermute | solution.py:31
  14.0 23.5 %copy-start = (bf16[8192,256]{1,0:T(8,128)(2,1)S(1)}, bf16[8192,256]{1,0:T(8,128)(2,1)}, u32[]{:S(2)}) copy-start(bf16[8192,256]{1,0:T(8,128)(2,1)} %refs_17_.1) | copy-start | bytes 12582916
  14.0 8.6 %collective-permute-start.7 = (bf16[16,4736]{1,0:T(8,128)(2,1)S(1)}, bf16[16,4736]{1,0:T(8,128)(2,1)S(1)}, u32[]{:S(2)}, u32[]{:S(2)}) collective-permute-start(bf16[16,4736]{1,0:T(8,128)(2,1)S(1)} %get-tuple-element.41), channel_id=1, source_target_pairs={{0,12},{1,13},{2,14},{3,15},{4,8},{5,9},{6,10},{7,11},{8,4},{9,5},... | collective-permute-start | bytes 454664 | tf_op jit(solution)/shard_map/ppermute | solution.py:31
  17.6 7.2 %collective-permute-start.4 = (bf16[16,5248]{1,0:T(8,128)(2,1)S(1)}, bf16[16,5248]{1,0:T(8,128)(2,1)S(1)}, u32[]{:S(2)}, u32[]{:S(2)}) collective-permute-start(bf16[16,5248]{1,0:T(8,128)(2,1)S(1)} %collective-permute-done.3), channel_id=1, source_target_pairs={{0,2},{1,3},{2,0},{3,1},{4,6},{5,7},{6,4},{7,5},{8,10},{9,11},{10,... | collective-permute-start | bytes 503816 | tf_op jit(solution)/shard_map/ppermute | solution.py:31
  19.1 11.8 %collective-permute-start.6 = (bf16[16,5248]{1,0:T(8,128)(2,1)S(1)}, bf16[16,5248]{1,0:T(8,128)(2,1)S(1)}, u32[]{:S(2)}, u32[]{:S(2)}) collective-permute-start(bf16[16,5248]{1,0:T(8,128)(2,1)S(1)} %collective-permute-done.3), channel_id=1, source_target_pairs={{0,4},{1,5},{2,6},{3,7},{4,0},{5,1},{6,2},{7,3},{8,12},{9,13},{10,... | collective-permute-start | bytes 503816 | tf_op jit(solution)/shard_map/ppermute | solution.py:31
  19.1 8.9 %collective-permute-start.10 = (bf16[16,4736]{1,0:T(8,128)(2,1)S(1)}, bf16[16,4736]{1,0:T(8,128)(2,1)S(1)}, u32[]{:S(2)}, u32[]{:S(2)}) collective-permute-start(bf16[16,4736]{1,0:T(8,128)(2,1)S(1)} %collective-permute-done), channel_id=1, source_target_pairs={{0,2},{1,3},{2,0},{3,1},{4,6},{5,7},{6,4},{7,5},{8,10},{9,11},{10,... | collective-permute-start | bytes 454664 | tf_op jit(solution)/shard_map/ppermute | solution.py:31
  19.6 9.9 %collective-permute-start.2 = (bf16[16,4736]{1,0:T(8,128)(2,1)S(1)}, bf16[16,4736]{1,0:T(8,128)(2,1)S(1)}, u32[]{:S(2)}, u32[]{:S(2)}) collective-permute-start(bf16[16,4736]{1,0:T(8,128)(2,1)S(1)} %collective-permute-done), channel_id=1, source_target_pairs={{0,1},{1,0},{2,3},{3,2},{4,5},{5,4},{6,7},{7,6},{8,9},{9,8},{10,11... | collective-permute-start | bytes 454664 | tf_op jit(solution)/shard_map/ppermute | solution.py:31
  22.6 8.9 %collective-permute-start.13 = (bf16[16,4736]{1,0:T(8,128)(2,1)S(1)}, bf16[16,4736]{1,0:T(8,128)(2,1)S(1)}, u32[]{:S(2)}, u32[]{:S(2)}) collective-permute-start(bf16[16,4736]{1,0:T(8,128)(2,1)S(1)} %collective-permute-done.7), channel_id=1, source_target_pairs={{0,2},{1,3},{2,0},{3,1},{4,6},{5,7},{6,4},{7,5},{8,10},{9,11},{10,... | collective-permute-start | bytes 454664 | tf_op jit(solution)/shard_map/ppermute | solution.py:31
  24.8 12.8 %collective-permute-start.9 = (bf16[16,5248]{1,0:T(8,128)(2,1)S(1)}, bf16[16,5248]{1,0:T(8,128)(2,1)S(1)}, u32[]{:S(2)}, u32[]{:S(2)}) collective-permute-start(bf16[16,5248]{1,0:T(8,128)(2,1)S(1)} %collective-permute-done.4), channel_id=1, source_target_pairs={{0,4},{1,5},{2,6},{3,7},{4,0},{5,1},{6,2},{7,3},{8,12},{9,13},{10,... | collective-permute-start | bytes 503816 | tf_op jit(solution)/shard_map/ppermute | solution.py:31
  28.0 9.5 %collective-permute-start.8 = (bf16[16,4736]{1,0:T(8,128)(2,1)S(1)}, bf16[16,4736]{1,0:T(8,128)(2,1)S(1)}, u32[]{:S(2)}, u32[]{:S(2)}) collective-permute-start(bf16[16,4736]{1,0:T(8,128)(2,1)S(1)} %collective-permute-done.5), channel_id=1, source_target_pairs={{0,2},{1,3},{2,0},{3,1},{4,6},{5,7},{6,4},{7,5},{8,10},{9,11},{10,... | collective-permute-start | bytes 454664 | tf_op jit(solution)/shard_map/ppermute | solution.py:31
  29.5 8.0 %collective-permute-start.12 = (bf16[16,4736]{1,0:T(8,128)(2,1)S(1)}, bf16[16,4736]{1,0:T(8,128)(2,1)S(1)}, u32[]{:S(2)}, u32[]{:S(2)}) collective-permute-start(bf16[16,4736]{1,0:T(8,128)(2,1)S(1)} %collective-permute-done.7), channel_id=1, source_target_pairs={{0,1},{1,0},{2,3},{3,2},{4,5},{5,4},{6,7},{7,6},{8,9},{9,8},{10,11... | collective-permute-start | bytes 454664 | tf_op jit(solution)/shard_map/ppermute | solution.py:31
  30.9 6.6 %collective-permute-start.11 = (bf16[16,4736]{1,0:T(8,128)(2,1)S(1)}, bf16[16,4736]{1,0:T(8,128)(2,1)S(1)}, u32[]{:S(2)}, u32[]{:S(2)}) collective-permute-start(bf16[16,4736]{1,0:T(8,128)(2,1)S(1)} %collective-permute-done.2._), channel_id=1, source_target_pairs={{0,2},{1,3},{2,0},{3,1},{4,6},{5,7},{6,4},{7,5},{8,10},{9,11},{10,... | collective-permute-start | bytes 454664 | tf_op jit(solution)/shard_map/ppermute | solution.py:31
  31.5 6.0 %collective-permute-start.14 = (bf16[16,4736]{1,0:T(8,128)(2,1)S(1)}, bf16[16,4736]{1,0:T(8,128)(2,1)S(1)}, u32[]{:S(2)}, u32[]{:S(2)}) collective-permute-start(bf16[16,4736]{1,0:T(8,128)(2,1)S(1)} %collective-permute-done.13), channel_id=1, source_target_pairs={{0,1},{1,0},{2,3},{3,2},{4,5},{5,4},{6,7},{7,6},{8,9},{9,8},{10,11... | collective-permute-start | bytes 454664 | tf_op jit(solution)/shard_map/ppermute | solution.py:31
  37.5 15.8 %copy-start.1 = (f32[4096]{0:T(1024)S(1)}, f32[4096]{0:T(1024)}, u32[]{:S(2)}) copy-start(f32[4096]{0:T(1024)} %param.17) | copy-start | bytes 49156
  38.9 4.5 %collective-permute-start.17 = (bf16[128,256]{1,0:T(8,128)(2,1)S(1)}, bf16[128,256]{1,0:T(8,128)(2,1)S(1)}, u32[]{:S(2)}, u32[]{:S(2)}) collective-permute-start(bf16[128,256]{1,0:T(8,128)(2,1)S(1)} %get-tuple-element.47), channel_id=1, source_target_pairs={{0,4},{1,5},{2,6},{3,7},{4,0},{5,1},{6,2},{7,3},{8,12},{9,13},{10,... | collective-permute-start | bytes 196616 | tf_op jit(solution)/shard_map/ppermute | solution.py:31
  38.9 8.1 %collective-permute-start.15 = (bf16[128,256]{1,0:T(8,128)(2,1)S(1)}, bf16[128,256]{1,0:T(8,128)(2,1)S(1)}, u32[]{:S(2)}, u32[]{:S(2)}) collective-permute-start(bf16[128,256]{1,0:T(8,128)(2,1)S(1)} %get-tuple-element.47), channel_id=1, source_target_pairs={{0,8},{1,9},{2,10},{3,11},{4,12},{5,13},{6,14},{7,15},{8,0},{9,1},... | collective-permute-start | bytes 196616 | tf_op jit(solution)/shard_map/ppermute | solution.py:31
  41.3 6.1 %collective-permute-start.16 = (bf16[128,256]{1,0:T(8,128)(2,1)S(1)}, bf16[128,256]{1,0:T(8,128)(2,1)S(1)}, u32[]{:S(2)}, u32[]{:S(2)}) collective-permute-start(bf16[128,256]{1,0:T(8,128)(2,1)S(1)} %get-tuple-element.47), channel_id=1, source_target_pairs={{0,12},{1,13},{2,14},{3,15},{4,8},{5,9},{6,10},{7,11},{8,4},{9,5},... | collective-permute-start | bytes 196616 | tf_op jit(solution)/shard_map/ppermute | solution.py:31
  43.3 13.1 %slice-start = ((s8[6291456]{0:T(1024)(128)(4,1)}), s8[4194304]{0:T(1024)(128)(4,1)S(1)}, s32[]{:S(2)}) async-start(s8[6291456]{0:T(1024)(128)(4,1)} %bitcast.34), calls=%async_computation | async-start | bytes 8388608
  43.3 7.2 %collective-permute-start.21 = (bf16[2,128,256]{2,1,0:T(8,128)(2,1)S(1)}, bf16[2,128,256]{2,1,0:T(8,128)(2,1)S(1)}, u32[]{:S(2)}, u32[]{:S(2)}) collective-permute-start(bf16[2,128,256]{2,1,0:T(8,128)(2,1)S(1)} %pad_maximum_fusion.1.refs_0_), channel_id=1, source_target_pairs={{0,1},{1,0},{2,3},{3,2},{4,5},{5,4},{6,7},{7,6},{8,9},{9,8},{10,11... | collective-permute-start | bytes 393224 | tf_op jit(solution)/shard_map/ppermute | solution.py:31
  45.5 7.8 %collective-permute-start.22 = (bf16[2,128,256]{2,1,0:T(8,128)(2,1)S(1)}, bf16[2,128,256]{2,1,0:T(8,128)(2,1)S(1)}, u32[]{:S(2)}, u32[]{:S(2)}) collective-permute-start(bf16[2,128,256]{2,1,0:T(8,128)(2,1)S(1)} %pad_maximum_fusion.1.refs_0_), channel_id=1, source_target_pairs={{0,2},{1,3},{2,0},{3,1},{4,6},{5,7},{6,4},{7,5},{8,10},{9,11},{10,... | collective-permute-start | bytes 393224 | tf_op jit(solution)/shard_map/ppermute | solution.py:31
  46.9 6.4 %collective-permute-start.23 = (bf16[2,128,256]{2,1,0:T(8,128)(2,1)S(1)}, bf16[2,128,256]{2,1,0:T(8,128)(2,1)S(1)}, u32[]{:S(2)}, u32[]{:S(2)}) collective-permute-start(bf16[2,128,256]{2,1,0:T(8,128)(2,1)S(1)} %pad_maximum_fusion.1.refs_0_), channel_id=1, source_target_pairs={{0,3},{1,2},{2,1},{3,0},{4,7},{5,6},{6,5},{7,4},{8,11},{9,10},{10,... | collective-permute-start | bytes 393224 | tf_op jit(solution)/shard_map/ppermute | solution.py:31
  47.3 7.0 %collective-permute-start.18 = (bf16[2,128,256]{2,1,0:T(8,128)(2,1)S(1)}, bf16[2,128,256]{2,1,0:T(8,128)(2,1)S(1)}, u32[]{:S(2)}, u32[]{:S(2)}) collective-permute-start(bf16[2,128,256]{2,1,0:T(8,128)(2,1)S(1)} %pad_maximum_fusion.refs_0_), channel_id=1, source_target_pairs={{0,1},{1,0},{2,3},{3,2},{4,5},{5,4},{6,7},{7,6},{8,9},{9,8},{10,11... | collective-permute-start | bytes 393224 | tf_op jit(solution)/shard_map/ppermute | solution.py:31
  49.1 5.6 %collective-permute-start.19 = (bf16[2,128,256]{2,1,0:T(8,128)(2,1)S(1)}, bf16[2,128,256]{2,1,0:T(8,128)(2,1)S(1)}, u32[]{:S(2)}, u32[]{:S(2)}) collective-permute-start(bf16[2,128,256]{2,1,0:T(8,128)(2,1)S(1)} %pad_maximum_fusion.refs_0_), channel_id=1, source_target_pairs={{0,2},{1,3},{2,0},{3,1},{4,6},{5,7},{6,4},{7,5},{8,10},{9,11},{10,... | collective-permute-start | bytes 393224 | tf_op jit(solution)/shard_map/ppermute | solution.py:31
  50.5 5.9 %collective-permute-start.20 = (bf16[2,128,256]{2,1,0:T(8,128)(2,1)S(1)}, bf16[2,128,256]{2,1,0:T(8,128)(2,1)S(1)}, u32[]{:S(2)}, u32[]{:S(2)}) collective-permute-start(bf16[2,128,256]{2,1,0:T(8,128)(2,1)S(1)} %pad_maximum_fusion.refs_0_), channel_id=1, source_target_pairs={{0,3},{1,2},{2,1},{3,0},{4,7},{5,6},{6,5},{7,4},{8,11},{9,10},{10,... | collective-permute-start | bytes 393224 | tf_op jit(solution)/shard_map/ppermute | solution.py:31
  53.3 3.1 %slice-start.1 = ((s8[6291456]{0:T(1024)(128)(4,1)}), s8[2097152]{0:T(1024)(128)(4,1)S(1)}, s32[]{:S(2)}) async-start(s8[6291456]{0:T(1024)(128)(4,1)} %bitcast.34), calls=%async_computation.1 | async-start | bytes 4194304
  58.5 5.9 %collective-permute-start.28 = (bf16[2,16,2048]{2,1,0:T(8,128)(2,1)S(1)}, bf16[2,16,2048]{2,1,0:T(8,128)(2,1)S(1)}, u32[]{:S(2)}, u32[]{:S(2)}) collective-permute-start(bf16[2,16,2048]{2,1,0:T(8,128)(2,1)S(1)} %get-tuple-element.60), channel_id=1, source_target_pairs={{0,3},{1,2},{2,1},{3,0},{4,7},{5,6},{6,5},{7,4},{8,11},{9,10},{10,... | collective-permute-start | bytes 393224 | tf_op jit(solution)/shard_map/ppermute | solution.py:31
  60.3 5.2 %collective-permute-start.29 = (bf16[2,16,2048]{2,1,0:T(8,128)(2,1)S(1)}, bf16[2,16,2048]{2,1,0:T(8,128)(2,1)S(1)}, u32[]{:S(2)}, u32[]{:S(2)}) collective-permute-start(bf16[2,16,2048]{2,1,0:T(8,128)(2,1)S(1)} %get-tuple-element.61), channel_id=1, source_target_pairs={{0,1},{1,0},{2,3},{3,2},{4,5},{5,4},{6,7},{7,6},{8,9},{9,8},{10,11... | collective-permute-start | bytes 393224 | tf_op jit(solution)/shard_map/ppermute | solution.py:31
  60.9 5.0 %collective-permute-start.30 = (bf16[2,16,2048]{2,1,0:T(8,128)(2,1)S(1)}, bf16[2,16,2048]{2,1,0:T(8,128)(2,1)S(1)}, u32[]{:S(2)}, u32[]{:S(2)}) collective-permute-start(bf16[2,16,2048]{2,1,0:T(8,128)(2,1)S(1)} %get-tuple-element.62), channel_id=1, source_target_pairs={{0,2},{1,3},{2,0},{3,1},{4,6},{5,7},{6,4},{7,5},{8,10},{9,11},{10,... | collective-permute-start | bytes 393224 | tf_op jit(solution)/shard_map/ppermute | solution.py:31
  62.1 6.7 %collective-permute-start.24 = (bf16[2,16,2048]{2,1,0:T(8,128)(2,1)S(1)}, bf16[2,16,2048]{2,1,0:T(8,128)(2,1)S(1)}, u32[]{:S(2)}, u32[]{:S(2)}) collective-permute-start(bf16[2,16,2048]{2,1,0:T(8,128)(2,1)S(1)} %get-tuple-element.56), channel_id=1, source_target_pairs={{0,3},{1,2},{2,1},{3,0},{4,7},{5,6},{6,5},{7,4},{8,11},{9,10},{10,... | collective-permute-start | bytes 393224 | tf_op jit(solution)/shard_map/ppermute | solution.py:31
  63.8 5.0 %collective-permute-start.25 = (bf16[2,16,2048]{2,1,0:T(8,128)(2,1)S(1)}, bf16[2,16,2048]{2,1,0:T(8,128)(2,1)S(1)}, u32[]{:S(2)}, u32[]{:S(2)}) collective-permute-start(bf16[2,16,2048]{2,1,0:T(8,128)(2,1)S(1)} %get-tuple-element.57), channel_id=1, source_target_pairs={{0,1},{1,0},{2,3},{3,2},{4,5},{5,4},{6,7},{7,6},{8,9},{9,8},{10,11... | collective-permute-start | bytes 393224 | tf_op jit(solution)/shard_map/ppermute | solution.py:31
  64.5 5.0 %collective-permute-start.26 = (bf16[2,16,2048]{2,1,0:T(8,128)(2,1)S(1)}, bf16[2,16,2048]{2,1,0:T(8,128)(2,1)S(1)}, u32[]{:S(2)}, u32[]{:S(2)}) collective-permute-start(bf16[2,16,2048]{2,1,0:T(8,128)(2,1)S(1)} %get-tuple-element.58), channel_id=1, source_target_pairs={{0,2},{1,3},{2,0},{3,1},{4,6},{5,7},{6,4},{7,5},{8,10},{9,11},{10,... | collective-permute-start | bytes 393224 | tf_op jit(solution)/shard_map/ppermute | solution.py:31
  66.0 6.4 %collective-permute-start.31 = (bf16[16,2048]{1,0:T(8,128)(2,1)S(1)}, bf16[16,2048]{1,0:T(8,128)(2,1)S(1)}, u32[]{:S(2)}, u32[]{:S(2)}) collective-permute-start(bf16[16,2048]{1,0:T(8,128)(2,1)S(1)} %get-tuple-element.63), channel_id=1, source_target_pairs={{0,8},{1,9},{2,10},{3,11},{4,12},{5,13},{6,14},{7,15},{8,0},{9,1},... | collective-permute-start | bytes 196616 | tf_op jit(solution)/shard_map/ppermute | solution.py:31
  66.0 6.3 %collective-permute-start.32 = (bf16[16,2048]{1,0:T(8,128)(2,1)S(1)}, bf16[16,2048]{1,0:T(8,128)(2,1)S(1)}, u32[]{:S(2)}, u32[]{:S(2)}) collective-permute-start(bf16[16,2048]{1,0:T(8,128)(2,1)S(1)} %get-tuple-element.64), channel_id=1, source_target_pairs={{0,12},{1,13},{2,14},{3,15},{4,8},{5,9},{6,10},{7,11},{8,4},{9,5},... | collective-permute-start | bytes 196616 | tf_op jit(solution)/shard_map/ppermute | solution.py:31
  69.5 4.3 %collective-permute-start.27 = (bf16[16,2048]{1,0:T(8,128)(2,1)S(1)}, bf16[16,2048]{1,0:T(8,128)(2,1)S(1)}, u32[]{:S(2)}, u32[]{:S(2)}) collective-permute-start(bf16[16,2048]{1,0:T(8,128)(2,1)S(1)} %slice_bitcast_fusion.2), channel_id=1, source_target_pairs={{0,4},{1,5},{2,6},{3,7},{4,0},{5,1},{6,2},{7,3},{8,12},{9,13},{10,... | collective-permute-start | bytes 196616 | tf_op jit(solution)/shard_map/ppermute | solution.py:31
  73.9 1.3 %collective-permute-start.33 = (bf16[8,2048]{1,0:T(8,128)(2,1)S(1)}, bf16[8,2048]{1,0:T(8,128)(2,1)S(1)}, u32[]{:S(2)}, u32[]{:S(2)}) collective-permute-start(bf16[8,2048]{1,0:T(8,128)(2,1)S(1)} %get-tuple-element.66), channel_id=1, source_target_pairs={{0,16},{16,0},{1,17},{17,1},{2,18},{18,2},{3,19},{19,3},{4,20},{20... | collective-permute-start | bytes 98312 | tf_op jit(solution)/shard_map/ppermute | solution.py:588

commit v4 on v3

--- a/solution.py
+++ b/solution.py
@@ -247,8 +247,15 @@
     )
 
 
-def project_kernel(count, waits, *refs):
-    refs = refs[waits:]
+def project_kernel(count, staged, *refs):
+    copies = []
+    if staged:
+        _, gu_hbm, *refs, quarter, plain, sems = refs
+        refs.append(plain)
+        chunks = gu_hbm.shape[1] // CHUNK
+        copies = weight_copies(gu_hbm, quarter, sems, first_chunk(1, chunks))
+    for copy in copies:
+        copy.start()
     pieces = refs[:count]
     *rest, w_ref, g_ref, y_ref, mix_ref, plain = refs[count:]
     blocks, sessions, _ = pieces[0].shape
@@ -298,28 +305,38 @@
     if rest:
         hidden = hidden + rest[0][...].astype(jnp.float32)
     y_ref[...] = (hidden * g_ref[...]).astype(jnp.bfloat16)
-
-
-def project(pieces, out_weight, gain_columns, residual_columns=None, waits=()):
+    for copy in copies:
+        copy.wait()
+
+
+def project(pieces, out_weight, gain_columns, residual_columns=None, staged=()):
     count = len(pieces)
     columns = out_weight.shape[1]
     rows = sum(p.shape[0] for p in pieces) * pieces[0].shape[1] // 2
     rest = [] if residual_columns is None else [residual_columns]
     vmem_spec = pl.BlockSpec(memory_space=pltpu.VMEM)
+    extra_specs, extra, extra_shapes, extra_scratch = [], [], [], []
+    if staged:
+        done, gate_up = staged
+        quarter = gate_up.shape[1] // 4
+        extra_specs = [pl.BlockSpec(memory_space=pl.ANY), pl.BlockSpec(memory_space=pltpu.HBM)]
+        extra = [done, pltpu.with_memory_space_constraint(gate_up, pltpu.HBM)]
+        extra_shapes = [jax.ShapeDtypeStruct((quarter, 2 * HID), jnp.bfloat16)]
+        extra_scratch = [pltpu.SemaphoreType.DMA((quarter // CHUNK,))]
     return pl.pallas_call(
-        functools.partial(project_kernel, count, len(waits)),
-        in_specs=[pl.BlockSpec(memory_space=pl.ANY)] * len(waits)
-        + [vmem_spec] * (count + len(rest) + 2),
-        out_specs=[vmem_spec] * 2,
+        functools.partial(project_kernel, count, bool(staged)),
+        in_specs=extra_specs + [vmem_spec] * (count + len(rest) + 2),
+        out_specs=[vmem_spec] * (2 + len(extra_shapes)),
         out_shape=[
             jax.ShapeDtypeStruct((rows, columns), jnp.bfloat16),
             jax.ShapeDtypeStruct((rows, 1), jnp.float32),
-        ],
-        scratch_shapes=[pltpu.VMEM((rows, columns), jnp.float32)],
+        ]
+        + extra_shapes,
+        scratch_shapes=[pltpu.VMEM((rows, columns), jnp.float32)] + extra_scratch,
         compiler_params=pltpu.CompilerParams(vmem_limit_bytes=8 * MIB),
         name="project",
     )(
-        *waits,
+        *extra,
         *pieces,
         *rest,
         pltpu.with_memory_space_constraint(out_weight, pltpu.VMEM),
@@ -339,13 +356,24 @@
     return squares[:, :LANES] + squares[:, LANES:]
 
 
+def weight_copies(gu_hbm, dst, sems, first):
+    return [
+        pltpu.make_async_copy(
+            gu_hbm.at[0, pl.ds(pl.multiple_of((first + j) * CHUNK, CHUNK), CHUNK)],
+            dst.at[pl.ds(j * CHUNK, CHUNK)],
+            sems.at[j],
+        )
+        for j in range(dst.shape[0] // CHUNK)
+    ]
+
+
+def first_chunk(half, chunks):
+    return ((lax.axis_index("grp") // (CHIPS // 2)) ^ half) * (chunks // 2)
+
+
 def stage_kernel(_, gu_hbm, weights, done, sems):
-    copies = [
-        pltpu.make_async_copy(
-            gu_hbm.at[0, pl.ds(j * CHUNK, CHUNK)], weights.at[pl.ds(j * CHUNK, CHUNK)], sems.at[j]
-        )
-        for j in range(weights.shape[0] // CHUNK)
-    ]
+    chunks = gu_hbm.shape[1] // CHUNK
+    copies = weight_copies(gu_hbm, weights, sems, first_chunk(0, chunks))
     for copy in copies:
         copy.start()
     done[...] = jnp.zeros_like(done)
@@ -354,7 +382,7 @@
 
 
 def stage(gate_up, arrived):
-    depth = gate_up.shape[1]
+    depth = gate_up.shape[1] // 2
     hbm_spec = pl.BlockSpec(memory_space=pltpu.HBM)
     vmem_spec = pl.BlockSpec(memory_space=pltpu.VMEM)
     return pl.pallas_call(
@@ -376,45 +404,49 @@
 
 def near_kernel(count, *refs):
     pieces = refs[:count]
-    weights, g_ref, acc, sq_ref, hid_ref, store, plain = refs[count:]
-    place = lax.axis_index("grp")
+    weights, gu_hbm, g_ref, acc, sq_ref, hid_ref, quarter, store, plain, sems = refs[count:]
     chunks = g_ref.shape[0]
     own = chunks // 2
-    first = (place // (CHIPS // 2)) * own
-    order = pair_order(place, CHIPS, PAIRS)[:own]
-    mine = weights.at[pl.ds(pl.multiple_of(first * CHUNK, CHUNK), own * CHUNK)]
+    copies = weight_copies(gu_hbm, quarter, sems, first_chunk(1, chunks) + own // 2)
+    for copy in copies:
+        copy.start()
+    order = pair_order(lax.axis_index("grp"), CHIPS, PAIRS)[:own]
     squares = jnp.zeros(sq_ref.shape, jnp.float32)
     for n in range(count):
         for b in range(2):
             chunk = order[2 * n + b]
             piece = pieces[n][b]
-            store[chunk - first] = piece
+            store[chunk - first_chunk(0, chunks)] = piece
             squares += take_chunk(piece, g_ref, plain, hid_ref, chunk, chunks)
     sq_ref[...] = squares
     y = jnp.concatenate([store[j] for j in range(own)], axis=1)
     for n in range(2 * HID // CHUNK):
         cols = slice(n * CHUNK, (n + 1) * CHUNK)
-        acc[:, cols] = jnp.dot(y, mine[:, cols], preferred_element_type=jnp.float32)
-
-
-def near(pieces, staged, norm_gain):
+        acc[:, cols] = jnp.dot(y, weights[:, cols], preferred_element_type=jnp.float32)
+    for copy in copies:
+        copy.wait()
+
+
+def near(pieces, staged, gate_up, norm_gain):
     rows = pieces[0].shape[1]
-    width = staged.shape[0]
+    width = gate_up.shape[1]
     chunks = width // CHUNK
     vmem_spec = pl.BlockSpec(memory_space=pltpu.VMEM)
     count = len(pieces)
     return pl.pallas_call(
         functools.partial(near_kernel, count),
-        in_specs=[vmem_spec] * (count + 2),
-        out_specs=[vmem_spec] * 3,
+        in_specs=[vmem_spec] * (count + 1) + [pl.BlockSpec(memory_space=pltpu.HBM), vmem_spec],
+        out_specs=[vmem_spec] * 4,
         out_shape=[
             jax.ShapeDtypeStruct((rows, 2 * HID), jnp.float32),
             jax.ShapeDtypeStruct((rows, LANES), jnp.float32),
             jax.ShapeDtypeStruct((16, width // 2), jnp.float32),
+            jax.ShapeDtypeStruct((width // 4, 2 * HID), jnp.bfloat16),
         ],
         scratch_shapes=[
             pltpu.VMEM((chunks // 2, rows, CHUNK), jnp.bfloat16),
             pltpu.VMEM((rows, CHUNK), jnp.float32),
+            pltpu.SemaphoreType.DMA((chunks // 4,)),
         ],
         compiler_params=pltpu.CompilerParams(vmem_limit_bytes=6 * MIB),
         cost_estimate=pl.CostEstimate(
@@ -424,14 +456,15 @@
     )(
         *pieces,
         pltpu.with_memory_space_constraint(staged, pltpu.VMEM),
+        pltpu.with_memory_space_constraint(gate_up, pltpu.HBM),
         norm_gain.reshape(chunks, 1, CHUNK),
     )
 
 
-def expert_kernel(count, outs, resumed, *refs):
+def expert_kernel(count, outs, parts, resumed, *refs):
     pieces = refs[:count]
-    gu_ref, dn_ref, g_ref, mix_ref = refs[count : count + 4]
-    rest = refs[count + 4 :]
+    gu_refs = refs[count : count + parts]
+    dn_ref, g_ref, mix_ref, *rest = refs[count + parts :]
     if resumed:
         acc_ref, sq_ref, old_ref = rest[:3]
         rest = rest[3:]
@@ -446,8 +479,7 @@
     back = pair_order(place, groups, BACK_PAIRS)
     if resumed:
         order = pair_order(place, groups, PAIRS)[own:]
-        base = own - (place // (CHIPS // 2)) * own
-        gu_ref = gu_ref.at[pl.ds(pl.multiple_of(base * CHUNK, CHUNK), own * CHUNK)]
+        base = first_chunk(1, chunks)
         squares = sq_ref[...]
         hid_ref[...] = old_ref[...]
     else:
@@ -461,13 +493,19 @@
             squares += take_chunk(piece, g_ref, plain, hid_ref, chunk, chunks)
     mean = jnp.sum(squares, axis=-1, keepdims=True) * (1.0 / width)
     scaling = lax.rsqrt(mean + EPS)
-    y = jnp.concatenate([store[j] for j in range(own)], axis=1)
+    span = own // parts
+    ys = [
+        jnp.concatenate([store[p * span + j] for j in range(span)], axis=1) for p in range(parts)
+    ]
     activated = []
     for n in range(HID // CHUNK):
         halves = []
         for start in (0, HID):
             cols = slice(start + n * CHUNK, start + (n + 1) * CHUNK)
-            value = jnp.dot(y, gu_ref[:, cols], preferred_element_type=jnp.float32)
+            value = sum(
+                jnp.dot(y, gu_ref[:, cols], preferred_element_type=jnp.float32)
+                for y, gu_ref in zip(ys, gu_refs)
+            )
             if resumed:
                 value = value + acc_ref[:, cols]
             halves.append(value * scaling)
@@ -496,7 +534,7 @@
                 ).astype(jnp.bfloat16)
 
 
-def experts(pieces, gate_up, down_weight, norm_gain, mix, outs, begun=()):
+def experts(pieces, gate_ups, down_weight, norm_gain, mix, outs, begun=()):
     rows = mix.shape[0]
     width = down_weight.shape[2]
     chunks = width // CHUNK
@@ -505,8 +543,8 @@
     count = len(pieces)
     in_vmem = functools.partial(pltpu.with_memory_space_constraint, memory_space=pltpu.VMEM)
     return pl.pallas_call(
-        functools.partial(expert_kernel, count, outs, bool(begun)),
-        in_specs=[vmem_spec] * (count + 4 + len(begun)),
+        functools.partial(expert_kernel, count, outs, len(gate_ups), bool(begun)),
+        in_specs=[vmem_spec] * (count + len(gate_ups) + 3 + len(begun)),
         out_specs=[vmem_spec] * (outs + 1),
         out_shape=[jax.ShapeDtypeStruct((groups // outs, 16, width // 2), jnp.bfloat16)] * outs
         + [jax.ShapeDtypeStruct((16, width // 2), jnp.float32)],
@@ -520,7 +558,7 @@
         name="experts",
     )(
         *pieces,
-        in_vmem(gate_up),
+        *(in_vmem(part) for part in gate_ups),
         in_vmem(down_weight),
         norm_gain.reshape(chunks, 1, CHUNK),
         mix,
@@ -561,10 +599,14 @@
         *carried, gain = attend(groups, PLANES, *arrays)
         pieces = gather(carried)
         staged, done = stage(gate_up, pieces[9])
-        y, mix = project([p[None] for p in pieces], out_weight, gain, waits=(done,))
+        y, mix, third = project(
+            [p[None] for p in pieces], out_weight, gain, staged=(done, gate_up)
+        )
         nears, fars = gather_pairs(y)
-        begun = near(nears, staged, norm_gain)
-        *sums, hidden = experts(fars, staged, down_weight, norm_gain, mix, 8, begun)
+        *begun, fourth = near(nears, staged, gate_up, norm_gain)
+        *sums, hidden = experts(
+            fars, [third, fourth], down_weight, norm_gain, mix, 8, begun
+        )
         mixture = scatter_sum(sums[:4], sums[4:])
     else:
         own_residual = lax.dynamic_slice_in_dim(residual, side * half, half, axis=0)
@@ -580,7 +622,7 @@
         y, mix = project([pieces], out_weight, gain, residual_columns)
         y_all = lax.all_gather(y, "grp", axis=0).transpose(1, 0, 2)
         y_chunks = y_all.reshape(rows, width // CHUNK, CHUNK).transpose(1, 0, 2)
-        *sums, hidden = experts([y_chunks], gate_up[0], down_weight, norm_gain, mix, 1)
+        *sums, hidden = experts([y_chunks], [gate_up[0]], down_weight, norm_gain, mix, 1)
         sent = lax.all_to_all(sums[0], "grp", split_axis=0, concat_axis=0, tiled=True)
         mixture = jnp.sum(sent.astype(jnp.float32), axis=0)
     ready = (hidden + mixture).astype(jnp.bfloat16)

time: 76 us -> 79 us (1.039)
  Pallas kernels: 11.9 us -> 14 us
    pallas_call x1, Pallas kernels: 1.09 us -> 3.25 us  [near(): pl.pallas_call(functools.partial(near_kernel, count), in_specs=[vmem_spec...]
    pallas_call x1, Pallas kernels: 4.72 us -> 2.86 us  [stage(): pl.pallas_call(stage_kernel, in_specs=[pl.BlockSpec(memory_space=pl.ANY),...]
    pallas_call x2, Pallas kernels: 3.44 us -> 5.27 us  [the longest x1 3.1 us: project(): pl.pallas_call(functools.partial(project_kernel, count, bool(staged)), in...]
where the time goes in v4:
time: 79 us; the launch traced here: 78.8 us
  starting transfers between devices  46.2 us (58%)
  waiting for transfers between devices  17 us (22%)
  Pallas kernels  14 us (18%)
  other arithmetic  0.86 us (1%)
    ppermute x33, starting transfers between devices, exchange(): return lax.ppermute(value, 'grp', [(g, g ^ bits) for g in range(CHIPS)])  46.1 us
    ppermute x33, waiting for transfers between devices, exchange(): return lax.ppermute(value, 'grp', [(g, g ^ bits) for g in range(CHIPS)])  15.9 us
    pallas_call x1, Pallas kernels, near(): pl.pallas_call(functools.partial(near_kernel, count), in_specs=[vmem_spec...  3.25 us
    pallas_call x1, Pallas kernels, project(): pl.pallas_call(functools.partial(project_kernel, count, bool(staged)), in...  3.1 us
    pallas_call x1, Pallas kernels, stage(): pl.pallas_call(stage_kernel, in_specs=[pl.BlockSpec(memory_space=pl.ANY),...  2.86 us
    pallas_call x1, Pallas kernels, attend(): pl.pallas_call(functools.partial(attend_kernel, planes), in_specs=[hbm_sp...  2.62 us
    pallas_call x1, Pallas kernels, experts(): pl.pallas_call(functools.partial(expert_kernel, count, outs, len(gate_ups...  2.18 us
  transfers between devices with their start and end apart: 34, of which 14 were waited for; matrix products, arithmetic and copies ran while one was open for 0% of the time, Pallas kernels for 8%

profile of v4, /device:TPU:0, one launch (start us, length us, event | category | flops | bytes accessed | tf_op | source)
XLA Modules:
  0.0 78.8 jit_solution(14944550182367146002)
XLA Ops:
  0.0 2.6 %attend.1 = (bf16[16,5248]{1,0:T(8,128)(2,1)S(1)}, bf16[16,4736]{1,0:T(8,128)(2,1)S(1)}, bf16[16,4736]{1,0:T(8,128)(2,1)S(1)}, bf16[16,4736]{1,0:T(8,128)(2,1)S(1)}, f32[1,256]{1,0:T(1,128)S(1)}) custom-call(s32[8,16]{1,0:T(8,128)} %bitcast.59, f32[8,16]{1,0:T(8,128)} %bitcast.60, s32[16]{0:T(128)} %len_hbm.1, f32[16,1,256]{2,1,0:T(1,128)} %bitcast.52, ...), custom_call_target="tpu_custom_call" | custom-call | tf_op jit(solution)/shard_map/attend/pallas_call | solution.py:219
  2.6 4.1 %collective-permute-start = (bf16[16,4736]{1,0:T(8,128)(2,1)S(1)}, bf16[16,4736]{1,0:T(8,128)(2,1)S(1)}, u32[]{:S(2)}, u32[]{:S(2)}) collective-permute-start(bf16[16,4736]{1,0:T(8,128)(2,1)S(1)} %get-tuple-element.36), channel_id=1, source_target_pairs={{0,8},{1,9},{2,10},{3,11},{4,12},{5,13},{6,14},{7,15},{8,0},{9,1},... | collective-permute-start | bytes 454664 | tf_op jit(solution)/shard_map/ppermute | solution.py:31
  6.7 1.5 %collective-permute-start.3 = (bf16[16,5248]{1,0:T(8,128)(2,1)S(1)}, bf16[16,5248]{1,0:T(8,128)(2,1)S(1)}, u32[]{:S(2)}, u32[]{:S(2)}) collective-permute-start(bf16[16,5248]{1,0:T(8,128)(2,1)S(1)} %get-tuple-element.37), channel_id=1, source_target_pairs={{0,1},{1,0},{2,3},{3,2},{4,5},{5,4},{6,7},{7,6},{8,9},{9,8},{10,11... | collective-permute-start | bytes 503816 | tf_op jit(solution)/shard_map/ppermute | solution.py:31
  8.2 1.5 %collective-permute-start.1 = (bf16[16,5248]{1,0:T(8,128)(2,1)S(1)}, bf16[16,5248]{1,0:T(8,128)(2,1)S(1)}, u32[]{:S(2)}, u32[]{:S(2)}) collective-permute-start(bf16[16,5248]{1,0:T(8,128)(2,1)S(1)} %get-tuple-element.37), channel_id=1, source_target_pairs={{0,2},{1,3},{2,0},{3,1},{4,6},{5,7},{6,4},{7,5},{8,10},{9,11},{10,... | collective-permute-start | bytes 503816 | tf_op jit(solution)/shard_map/ppermute | solution.py:31
  9.7 1.6 %collective-permute-start.5 = (bf16[16,4736]{1,0:T(8,128)(2,1)S(1)}, bf16[16,4736]{1,0:T(8,128)(2,1)S(1)}, u32[]{:S(2)}, u32[]{:S(2)}) collective-permute-start(bf16[16,4736]{1,0:T(8,128)(2,1)S(1)} %get-tuple-element.40), channel_id=1, source_target_pairs={{0,4},{1,5},{2,6},{3,7},{4,0},{5,1},{6,2},{7,3},{8,12},{9,13},{10,... | collective-permute-start | bytes 454664 | tf_op jit(solution)/shard_map/ppermute | solution.py:31
  11.3 2.7 %collective-permute-done = bf16[16,4736]{1,0:T(8,128)(2,1)S(1)} collective-permute-done((bf16[16,4736]{1,0:T(8,128)(2,1)S(1)}, bf16[16,4736]{1,0:T(8,128)(2,1)S(1)}, u32[]{:S(2)}, u32[]{:S(2)}) %collective-permute-start) | collective-permute-done | bytes 151584 | tf_op jit(solution)/shard_map/ppermute | solution.py:31
  14.0 3.5 %collective-permute-start.7 = (bf16[16,4736]{1,0:T(8,128)(2,1)S(1)}, bf16[16,4736]{1,0:T(8,128)(2,1)S(1)}, u32[]{:S(2)}, u32[]{:S(2)}) collective-permute-start(bf16[16,4736]{1,0:T(8,128)(2,1)S(1)} %get-tuple-element.43), channel_id=1, source_target_pairs={{0,12},{1,13},{2,14},{3,15},{4,8},{5,9},{6,10},{7,11},{8,4},{9,5},... | collective-permute-start | bytes 454664 | tf_op jit(solution)/shard_map/ppermute | solution.py:31
  17.6 1.5 %collective-permute-start.4 = (bf16[16,5248]{1,0:T(8,128)(2,1)S(1)}, bf16[16,5248]{1,0:T(8,128)(2,1)S(1)}, u32[]{:S(2)}, u32[]{:S(2)}) collective-permute-start(bf16[16,5248]{1,0:T(8,128)(2,1)S(1)} %collective-permute-done.3), channel_id=1, source_target_pairs={{0,2},{1,3},{2,0},{3,1},{4,6},{5,7},{6,4},{7,5},{8,10},{9,11},{10,... | collective-permute-start | bytes 503816 | tf_op jit(solution)/shard_map/ppermute | solution.py:31
  19.1 0.5 collective-permute-start.10
  19.6 1.5 %collective-permute-start.2 = (bf16[16,4736]{1,0:T(8,128)(2,1)S(1)}, bf16[16,4736]{1,0:T(8,128)(2,1)S(1)}, u32[]{:S(2)}, u32[]{:S(2)}) collective-permute-start(bf16[16,4736]{1,0:T(8,128)(2,1)S(1)} %collective-permute-done), channel_id=1, source_target_pairs={{0,1},{1,0},{2,3},{3,2},{4,5},{5,4},{6,7},{7,6},{8,9},{9,8},{10,11... | collective-permute-start | bytes 454664 | tf_op jit(solution)/shard_map/ppermute | solution.py:31
  21.1 1.5 %collective-permute-done.7 = bf16[16,4736]{1,0:T(8,128)(2,1)S(1)} collective-permute-done((bf16[16,4736]{1,0:T(8,128)(2,1)S(1)}, bf16[16,4736]{1,0:T(8,128)(2,1)S(1)}, u32[]{:S(2)}, u32[]{:S(2)}) %collective-permute-start.7) | collective-permute-done | bytes 151584 | tf_op jit(solution)/shard_map/ppermute | solution.py:31
  22.6 1.6 %collective-permute-start.13 = (bf16[16,4736]{1,0:T(8,128)(2,1)S(1)}, bf16[16,4736]{1,0:T(8,128)(2,1)S(1)}, u32[]{:S(2)}, u32[]{:S(2)}) collective-permute-start(bf16[16,4736]{1,0:T(8,128)(2,1)S(1)} %collective-permute-done.7), channel_id=1, source_target_pairs={{0,2},{1,3},{2,0},{3,1},{4,6},{5,7},{6,4},{7,5},{8,10},{9,11},{10,... | collective-permute-start | bytes 454664 | tf_op jit(solution)/shard_map/ppermute | solution.py:31
  24.2 0.6 collective-permute-done.4
  24.8 0.5 collective-permute-start.9
  25.3 2.7 %collective-permute-done.10 = bf16[16,4736]{1,0:T(8,128)(2,1)S(1)} collective-permute-done((bf16[16,4736]{1,0:T(8,128)(2,1)S(1)}, bf16[16,4736]{1,0:T(8,128)(2,1)S(1)}, u32[]{:S(2)}, u32[]{:S(2)}) %collective-permute-start.10) | collective-permute-done | bytes 151584 | tf_op jit(solution)/shard_map/ppermute | solution.py:31
  28.0 1.5 %collective-permute-start.8 = (bf16[16,4736]{1,0:T(8,128)(2,1)S(1)}, bf16[16,4736]{1,0:T(8,128)(2,1)S(1)}, u32[]{:S(2)}, u32[]{:S(2)}) collective-permute-start(bf16[16,4736]{1,0:T(8,128)(2,1)S(1)} %collective-permute-done.5), channel_id=1, source_target_pairs={{0,2},{1,3},{2,0},{3,1},{4,6},{5,7},{6,4},{7,5},{8,10},{9,11},{10,... | collective-permute-start | bytes 454664 | tf_op jit(solution)/shard_map/ppermute | solution.py:31
  29.5 1.4 %collective-permute-start.12 = (bf16[16,4736]{1,0:T(8,128)(2,1)S(1)}, bf16[16,4736]{1,0:T(8,128)(2,1)S(1)}, u32[]{:S(2)}, u32[]{:S(2)}) collective-permute-start(bf16[16,4736]{1,0:T(8,128)(2,1)S(1)} %collective-permute-done.7), channel_id=1, source_target_pairs={{0,1},{1,0},{2,3},{3,2},{4,5},{5,4},{6,7},{7,6},{8,9},{9,8},{10,11... | collective-permute-start | bytes 454664 | tf_op jit(solution)/shard_map/ppermute | solution.py:31
  30.9 0.6 collective-permute-start.11
  31.5 1.2 %collective-permute-start.14 = (bf16[16,4736]{1,0:T(8,128)(2,1)S(1)}, bf16[16,4736]{1,0:T(8,128)(2,1)S(1)}, u32[]{:S(2)}, u32[]{:S(2)}) collective-permute-start(bf16[16,4736]{1,0:T(8,128)(2,1)S(1)} %collective-permute-done.13), channel_id=1, source_target_pairs={{0,1},{1,0},{2,3},{3,2},{4,5},{5,4},{6,7},{7,6},{8,9},{9,8},{10,11... | collective-permute-start | bytes 454664 | tf_op jit(solution)/shard_map/ppermute | solution.py:31
  32.7 2.9 %stage.1 = (bf16[2048,1536]{1,0:T(8,128)(2,1)S(1)}, f32[8,128]{1,0:T(8,128)S(1)}) custom-call(bf16[16,4736]{1,0:T(8,128)(2,1)S(1)} %collective-permute-done.2._, bf16[1,4096,1536]{2,1,0:T(8,128)(2,1)} %refs_5_.1), custom_call_target="tpu_custom_call" | custom-call | bytes 6291456 | tf_op jit(solution)/shard_map/stage/pallas_call | solution.py:388
  35.6 0.8 %collective-permute-done.11 = bf16[16,4736]{1,0:T(8,128)(2,1)S(1)} collective-permute-done((bf16[16,4736]{1,0:T(8,128)(2,1)S(1)}, bf16[16,4736]{1,0:T(8,128)(2,1)S(1)}, u32[]{:S(2)}, u32[]{:S(2)}) %collective-permute-start.11) | collective-permute-done | bytes 151584 | tf_op jit(solution)/shard_map/ppermute | solution.py:31
  36.7 3.1 %project.1 = (bf16[128,256]{1,0:T(8,128)(2,1)S(1)}, f32[128,1]{1,0:T(8,128)S(1)}, bf16[1024,1536]{1,0:T(8,128)(2,1)S(1)}) custom-call(f32[8,128]{1,0:T(8,128)S(1)} %get-tuple-element.39.refs_0_, bf16[1,4096,1536]{2,1,0:T(8,128)(2,1)} %refs_5_.1, bf16[1,16,5248]{2,1,0:T(8,128)(2,1)S(1)} %bitcast.37, bf16[1,16,5248]{2,1,0:T(8,128)(2,1)S(1)} %bitcast.38, ...), custom_call_target="tpu_custom_call" | custom-call | tf_op jit(solution)/shard_map/project/pallas_call | solution.py:326
  39.9 2.0 %collective-permute-start.15 = (bf16[128,256]{1,0:T(8,128)(2,1)S(1)}, bf16[128,256]{1,0:T(8,128)(2,1)S(1)}, u32[]{:S(2)}, u32[]{:S(2)}) collective-permute-start(bf16[128,256]{1,0:T(8,128)(2,1)S(1)} %get-tuple-element.49), channel_id=1, source_target_pairs={{0,8},{1,9},{2,10},{3,11},{4,12},{5,13},{6,14},{7,15},{8,0},{9,1},... | collective-permute-start | bytes 196616 | tf_op jit(solution)/shard_map/ppermute | solution.py:31
  41.9 2.4 %collective-permute-start.16 = (bf16[128,256]{1,0:T(8,128)(2,1)S(1)}, bf16[128,256]{1,0:T(8,128)(2,1)S(1)}, u32[]{:S(2)}, u32[]{:S(2)}) collective-permute-start(bf16[128,256]{1,0:T(8,128)(2,1)S(1)} %get-tuple-element.49), channel_id=1, source_target_pairs={{0,12},{1,13},{2,14},{3,15},{4,8},{5,9},{6,10},{7,11},{8,4},{9,5},... | collective-permute-start | bytes 196616 | tf_op jit(solution)/shard_map/ppermute | solution.py:31
  44.4 1.1 %collective-permute-start.21 = (bf16[2,128,256]{2,1,0:T(8,128)(2,1)S(1)}, bf16[2,128,256]{2,1,0:T(8,128)(2,1)S(1)}, u32[]{:S(2)}, u32[]{:S(2)}) collective-permute-start(bf16[2,128,256]{2,1,0:T(8,128)(2,1)S(1)} %pad_maximum_fusion.1.refs_0_), channel_id=1, source_target_pairs={{0,1},{1,0},{2,3},{3,2},{4,5},{5,4},{6,7},{7,6},{8,9},{9,8},{10,11... | collective-permute-start | bytes 393224 | tf_op jit(solution)/shard_map/ppermute | solution.py:31
  45.6 1.5 %collective-permute-start.22 = (bf16[2,128,256]{2,1,0:T(8,128)(2,1)S(1)}, bf16[2,128,256]{2,1,0:T(8,128)(2,1)S(1)}, u32[]{:S(2)}, u32[]{:S(2)}) collective-permute-start(bf16[2,128,256]{2,1,0:T(8,128)(2,1)S(1)} %pad_maximum_fusion.1.refs_0_), channel_id=1, source_target_pairs={{0,2},{1,3},{2,0},{3,1},{4,6},{5,7},{6,4},{7,5},{8,10},{9,11},{10,... | collective-permute-start | bytes 393224 | tf_op jit(solution)/shard_map/ppermute | solution.py:31
  47.1 0.9 %collective-permute-start.23 = (bf16[2,128,256]{2,1,0:T(8,128)(2,1)S(1)}, bf16[2,128,256]{2,1,0:T(8,128)(2,1)S(1)}, u32[]{:S(2)}, u32[]{:S(2)}) collective-permute-start(bf16[2,128,256]{2,1,0:T(8,128)(2,1)S(1)} %pad_maximum_fusion.1.refs_0_), channel_id=1, source_target_pairs={{0,3},{1,2},{2,1},{3,0},{4,7},{5,6},{6,5},{7,4},{8,11},{9,10},{10,... | collective-permute-start | bytes 393224 | tf_op jit(solution)/shard_map/ppermute | solution.py:31
  48.0 1.6 %collective-permute-start.18 = (bf16[2,128,256]{2,1,0:T(8,128)(2,1)S(1)}, bf16[2,128,256]{2,1,0:T(8,128)(2,1)S(1)}, u32[]{:S(2)}, u32[]{:S(2)}) collective-permute-start(bf16[2,128,256]{2,1,0:T(8,128)(2,1)S(1)} %pad_maximum_fusion.refs_0_), channel_id=1, source_target_pairs={{0,1},{1,0},{2,3},{3,2},{4,5},{5,4},{6,7},{7,6},{8,9},{9,8},{10,11... | collective-permute-start | bytes 393224 | tf_op jit(solution)/shard_map/ppermute | solution.py:31
  49.6 1.4 %collective-permute-start.19 = (bf16[2,128,256]{2,1,0:T(8,128)(2,1)S(1)}, bf16[2,128,256]{2,1,0:T(8,128)(2,1)S(1)}, u32[]{:S(2)}, u32[]{:S(2)}) collective-permute-start(bf16[2,128,256]{2,1,0:T(8,128)(2,1)S(1)} %pad_maximum_fusion.refs_0_), channel_id=1, source_target_pairs={{0,2},{1,3},{2,0},{3,1},{4,6},{5,7},{6,4},{7,5},{8,10},{9,11},{10,... | collective-permute-start | bytes 393224 | tf_op jit(solution)/shard_map/ppermute | solution.py:31
  51.0 1.8 %collective-permute-start.20 = (bf16[2,128,256]{2,1,0:T(8,128)(2,1)S(1)}, bf16[2,128,256]{2,1,0:T(8,128)(2,1)S(1)}, u32[]{:S(2)}, u32[]{:S(2)}) collective-permute-start(bf16[2,128,256]{2,1,0:T(8,128)(2,1)S(1)} %pad_maximum_fusion.refs_0_), channel_id=1, source_target_pairs={{0,3},{1,2},{2,1},{3,0},{4,7},{5,6},{6,5},{7,4},{8,11},{9,10},{10,... | collective-permute-start | bytes 393224 | tf_op jit(solution)/shard_map/ppermute | solution.py:31
  53.3 1.4 %collective-permute-done.23.refs_3_ = bf16[2,128,256]{2,1,0:T(8,128)(2,1)S(1)} collective-permute-done((bf16[2,128,256]{2,1,0:T(8,128)(2,1)S(1)}, bf16[2,128,256]{2,1,0:T(8,128)(2,1)S(1)}, u32[]{:S(2)}, u32[]{:S(2)}) %collective-permute-start.23) | collective-permute-done | bytes 131104 | tf_op jit(solution)/shard_map/ppermute | solution.py:31
  54.6 3.2 %near.1 = (f32[128,1536]{1,0:T(8,128)S(1)}, f32[128,128]{1,0:T(8,128)S(1)}, f32[16,2048]{1,0:T(8,128)S(1)}, bf16[1024,1536]{1,0:T(8,128)(2,1)S(1)}) custom-call(bf16[2,128,256]{2,1,0:T(8,128)(2,1)S(1)} %pad_maximum_fusion.1.refs_0_, bf16[2,128,256]{2,1,0:T(8,128)(2,1)S(1)} %collective-permute-done.21.refs_1_, ...), custom_call_target="tpu_custom_call" | custom-call | flops 805306368 | bytes 12582912 | tf_op jit(solution)/shard_map/near/pallas_call | solution.py:436
  57.9 0.5 slice-done.1
  58.4 2.2 %experts.1 = (bf16[2,16,2048]{2,1,0:T(8,128)(2,1)S(1)}, bf16[2,16,2048]{2,1,0:T(8,128)(2,1)S(1)}, bf16[2,16,2048]{2,1,0:T(8,128)(2,1)S(1)}, bf16[2,16,2048]{2,1,...) custom-call(bf16[2,128,256]{2,1,0:T(8,128)(2,1)S(1)} %pad_maximum_fu, ...), custom_call_target="tpu_custom_call" | custom-call | tf_op jit(solution)/shard_map/experts/pallas_call | solution.py:545
  60.6 1.1 %collective-permute-start.28 = (bf16[2,16,2048]{2,1,0:T(8,128)(2,1)S(1)}, bf16[2,16,2048]{2,1,0:T(8,128)(2,1)S(1)}, u32[]{:S(2)}, u32[]{:S(2)}) collective-permute-start(bf16[2,16,2048]{2,1,0:T(8,128)(2,1)S(1)} %get-tuple-element.64), channel_id=1, source_target_pairs={{0,3},{1,2},{2,1},{3,0},{4,7},{5,6},{6,5},{7,4},{8,11},{9,10},{10,... | collective-permute-start | bytes 393224 | tf_op jit(solution)/shard_map/ppermute | solution.py:31
  61.7 1.5 %collective-permute-start.29 = (bf16[2,16,2048]{2,1,0:T(8,128)(2,1)S(1)}, bf16[2,16,2048]{2,1,0:T(8,128)(2,1)S(1)}, u32[]{:S(2)}, u32[]{:S(2)}) collective-permute-start(bf16[2,16,2048]{2,1,0:T(8,128)(2,1)S(1)} %get-tuple-element.65), channel_id=1, source_target_pairs={{0,1},{1,0},{2,3},{3,2},{4,5},{5,4},{6,7},{7,6},{8,9},{9,8},{10,11... | collective-permute-start | bytes 393224 | tf_op jit(solution)/shard_map/ppermute | solution.py:31
  63.2 0.9 %collective-permute-start.30 = (bf16[2,16,2048]{2,1,0:T(8,128)(2,1)S(1)}, bf16[2,16,2048]{2,1,0:T(8,128)(2,1)S(1)}, u32[]{:S(2)}, u32[]{:S(2)}) collective-permute-start(bf16[2,16,2048]{2,1,0:T(8,128)(2,1)S(1)} %get-tuple-element.66), channel_id=1, source_target_pairs={{0,2},{1,3},{2,0},{3,1},{4,6},{5,7},{6,4},{7,5},{8,10},{9,11},{10,... | collective-permute-start | bytes 393224 | tf_op jit(solution)/shard_map/ppermute | solution.py:31
  64.2 1.0 %collective-permute-start.24 = (bf16[2,16,2048]{2,1,0:T(8,128)(2,1)S(1)}, bf16[2,16,2048]{2,1,0:T(8,128)(2,1)S(1)}, u32[]{:S(2)}, u32[]{:S(2)}) collective-permute-start(bf16[2,16,2048]{2,1,0:T(8,128)(2,1)S(1)} %get-tuple-element.60), channel_id=1, source_target_pairs={{0,3},{1,2},{2,1},{3,0},{4,7},{5,6},{6,5},{7,4},{8,11},{9,10},{10,... | collective-permute-start | bytes 393224 | tf_op jit(solution)/shard_map/ppermute | solution.py:31
  65.2 1.5 %collective-permute-start.25 = (bf16[2,16,2048]{2,1,0:T(8,128)(2,1)S(1)}, bf16[2,16,2048]{2,1,0:T(8,128)(2,1)S(1)}, u32[]{:S(2)}, u32[]{:S(2)}) collective-permute-start(bf16[2,16,2048]{2,1,0:T(8,128)(2,1)S(1)} %get-tuple-element.61), channel_id=1, source_target_pairs={{0,1},{1,0},{2,3},{3,2},{4,5},{5,4},{6,7},{7,6},{8,9},{9,8},{10,11... | collective-permute-start | bytes 393224 | tf_op jit(solution)/shard_map/ppermute | solution.py:31
  66.7 0.7 collective-permute-done.28
  67.5 0.6 collective-permute-start.26
  68.1 0.7 collective-permute-done.30
  69.0 3.4 %collective-permute-start.32 = (bf16[16,2048]{1,0:T(8,128)(2,1)S(1)}, bf16[16,2048]{1,0:T(8,128)(2,1)S(1)}, u32[]{:S(2)}, u32[]{:S(2)}) collective-permute-start(bf16[16,2048]{1,0:T(8,128)(2,1)S(1)} %get-tuple-element.68), channel_id=1, source_target_pairs={{0,12},{1,13},{2,14},{3,15},{4,8},{5,9},{6,10},{7,11},{8,4},{9,5},... | collective-permute-start | bytes 196616 | tf_op jit(solution)/shard_map/ppermute | solution.py:31
  72.5 0.5 collective-permute-start.27
  73.1 2.5 %collective-permute-done.31 = bf16[16,2048]{1,0:T(8,128)(2,1)S(1)} collective-permute-done((bf16[16,2048]{1,0:T(8,128)(2,1)S(1)}, bf16[16,2048]{1,0:T(8,128)(2,1)S(1)}, u32[]{:S(2)}, u32[]{:S(2)}) %collective-permute-start.31) | collective-permute-done | bytes 65568 | tf_op jit(solution)/shard_map/ppermute | solution.py:31
  75.6 1.3 %collective-permute-done.27 = bf16[16,2048]{1,0:T(8,128)(2,1)S(1)} collective-permute-done((bf16[16,2048]{1,0:T(8,128)(2,1)S(1)}, bf16[16,2048]{1,0:T(8,128)(2,1)S(1)}, u32[]{:S(2)}, u32[]{:S(2)}) %collective-permute-start.27) | collective-permute-done | bytes 65568 | tf_op jit(solution)/shard_map/ppermute | solution.py:31
  77.0 1.2 %collective-permute-done.33 = bf16[8,2048]{1,0:T(8,128)(2,1)S(1)} collective-permute-done((bf16[8,2048]{1,0:T(8,128)(2,1)S(1)}, bf16[8,2048]{1,0:T(8,128)(2,1)S(1)}, u32[]{:S(2)}, u32[]{:S(2)}) %collective-permute-start.33) | collective-permute-done | bytes 32800 | tf_op jit(solution)/shard_map/ppermute | solution.py:630
  78.2 0.6 maximum_select_fusion
  (44 shorter events, 1.4 us)
Async XLA Ops:
  2.6 11.4 %collective-permute-start = (bf16[16,4736]{1,0:T(8,128)(2,1)S(1)}, bf16[16,4736]{1,0:T(8,128)(2,1)S(1)}, u32[]{:S(2)}, u32[]{:S(2)}) collective-permute-start(bf16[16,4736]{1,0:T(8,128)(2,1)S(1)} %get-tuple-element.36), channel_id=1, source_target_pairs={{0,8},{1,9},{2,10},{3,11},{4,12},{5,13},{6,14},{7,15},{8,0},{9,1},... | collective-permute-start | bytes 454664 | tf_op jit(solution)/shard_map/ppermute | solution.py:31
  6.7 10.8 %collective-permute-start.3 = (bf16[16,5248]{1,0:T(8,128)(2,1)S(1)}, bf16[16,5248]{1,0:T(8,128)(2,1)S(1)}, u32[]{:S(2)}, u32[]{:S(2)}) collective-permute-start(bf16[16,5248]{1,0:T(8,128)(2,1)S(1)} %get-tuple-element.37), channel_id=1, source_target_pairs={{0,1},{1,0},{2,3},{3,2},{4,5},{5,4},{6,7},{7,6},{8,9},{9,8},{10,11... | collective-permute-start | bytes 503816 | tf_op jit(solution)/shard_map/ppermute | solution.py:31
  8.2 11.4 %collective-permute-start.1 = (bf16[16,5248]{1,0:T(8,128)(2,1)S(1)}, bf16[16,5248]{1,0:T(8,128)(2,1)S(1)}, u32[]{:S(2)}, u32[]{:S(2)}) collective-permute-start(bf16[16,5248]{1,0:T(8,128)(2,1)S(1)} %get-tuple-element.37), channel_id=1, source_target_pairs={{0,2},{1,3},{2,0},{3,1},{4,6},{5,7},{6,4},{7,5},{8,10},{9,11},{10,... | collective-permute-start | bytes 503816 | tf_op jit(solution)/shard_map/ppermute | solution.py:31
  9.7 9.3 %collective-permute-start.5 = (bf16[16,4736]{1,0:T(8,128)(2,1)S(1)}, bf16[16,4736]{1,0:T(8,128)(2,1)S(1)}, u32[]{:S(2)}, u32[]{:S(2)}) collective-permute-start(bf16[16,4736]{1,0:T(8,128)(2,1)S(1)} %get-tuple-element.40), channel_id=1, source_target_pairs={{0,4},{1,5},{2,6},{3,7},{4,0},{5,1},{6,2},{7,3},{8,12},{9,13},{10,... | collective-permute-start | bytes 454664 | tf_op jit(solution)/shard_map/ppermute | solution.py:31
  14.0 22.7 %copy-start = (bf16[8192,256]{1,0:T(8,128)(2,1)S(1)}, bf16[8192,256]{1,0:T(8,128)(2,1)}, u32[]{:S(2)}) copy-start(bf16[8192,256]{1,0:T(8,128)(2,1)} %refs_18_.1) | copy-start | bytes 12582916
  14.0 8.6 %collective-permute-start.7 = (bf16[16,4736]{1,0:T(8,128)(2,1)S(1)}, bf16[16,4736]{1,0:T(8,128)(2,1)S(1)}, u32[]{:S(2)}, u32[]{:S(2)}) collective-permute-start(bf16[16,4736]{1,0:T(8,128)(2,1)S(1)} %get-tuple-element.43), channel_id=1, source_target_pairs={{0,12},{1,13},{2,14},{3,15},{4,8},{5,9},{6,10},{7,11},{8,4},{9,5},... | collective-permute-start | bytes 454664 | tf_op jit(solution)/shard_map/ppermute | solution.py:31
  17.6 7.2 %collective-permute-start.4 = (bf16[16,5248]{1,0:T(8,128)(2,1)S(1)}, bf16[16,5248]{1,0:T(8,128)(2,1)S(1)}, u32[]{:S(2)}, u32[]{:S(2)}) collective-permute-start(bf16[16,5248]{1,0:T(8,128)(2,1)S(1)} %collective-permute-done.3), channel_id=1, source_target_pairs={{0,2},{1,3},{2,0},{3,1},{4,6},{5,7},{6,4},{7,5},{8,10},{9,11},{10,... | collective-permute-start | bytes 503816 | tf_op jit(solution)/shard_map/ppermute | solution.py:31
  19.1 11.8 %collective-permute-start.6 = (bf16[16,5248]{1,0:T(8,128)(2,1)S(1)}, bf16[16,5248]{1,0:T(8,128)(2,1)S(1)}, u32[]{:S(2)}, u32[]{:S(2)}) collective-permute-start(bf16[16,5248]{1,0:T(8,128)(2,1)S(1)} %collective-permute-done.3), channel_id=1, source_target_pairs={{0,4},{1,5},{2,6},{3,7},{4,0},{5,1},{6,2},{7,3},{8,12},{9,13},{10,... | collective-permute-start | bytes 503816 | tf_op jit(solution)/shard_map/ppermute | solution.py:31
  19.1 8.9 %collective-permute-start.10 = (bf16[16,4736]{1,0:T(8,128)(2,1)S(1)}, bf16[16,4736]{1,0:T(8,128)(2,1)S(1)}, u32[]{:S(2)}, u32[]{:S(2)}) collective-permute-start(bf16[16,4736]{1,0:T(8,128)(2,1)S(1)} %collective-permute-done), channel_id=1, source_target_pairs={{0,2},{1,3},{2,0},{3,1},{4,6},{5,7},{6,4},{7,5},{8,10},{9,11},{10,... | collective-permute-start | bytes 454664 | tf_op jit(solution)/shard_map/ppermute | solution.py:31
  19.6 9.9 %collective-permute-start.2 = (bf16[16,4736]{1,0:T(8,128)(2,1)S(1)}, bf16[16,4736]{1,0:T(8,128)(2,1)S(1)}, u32[]{:S(2)}, u32[]{:S(2)}) collective-permute-start(bf16[16,4736]{1,0:T(8,128)(2,1)S(1)} %collective-permute-done), channel_id=1, source_target_pairs={{0,1},{1,0},{2,3},{3,2},{4,5},{5,4},{6,7},{7,6},{8,9},{9,8},{10,11... | collective-permute-start | bytes 454664 | tf_op jit(solution)/shard_map/ppermute | solution.py:31
  22.6 8.9 %collective-permute-start.13 = (bf16[16,4736]{1,0:T(8,128)(2,1)S(1)}, bf16[16,4736]{1,0:T(8,128)(2,1)S(1)}, u32[]{:S(2)}, u32[]{:S(2)}) collective-permute-start(bf16[16,4736]{1,0:T(8,128)(2,1)S(1)} %collective-permute-done.7), channel_id=1, source_target_pairs={{0,2},{1,3},{2,0},{3,1},{4,6},{5,7},{6,4},{7,5},{8,10},{9,11},{10,... | collective-permute-start | bytes 454664 | tf_op jit(solution)/shard_map/ppermute | solution.py:31
  24.8 11.7 %collective-permute-start.9 = (bf16[16,5248]{1,0:T(8,128)(2,1)S(1)}, bf16[16,5248]{1,0:T(8,128)(2,1)S(1)}, u32[]{:S(2)}, u32[]{:S(2)}) collective-permute-start(bf16[16,5248]{1,0:T(8,128)(2,1)S(1)} %collective-permute-done.4), channel_id=1, source_target_pairs={{0,4},{1,5},{2,6},{3,7},{4,0},{5,1},{6,2},{7,3},{8,12},{9,13},{10,... | collective-permute-start | bytes 503816 | tf_op jit(solution)/shard_map/ppermute | solution.py:31
  28.0 7.6 %collective-permute-start.8 = (bf16[16,4736]{1,0:T(8,128)(2,1)S(1)}, bf16[16,4736]{1,0:T(8,128)(2,1)S(1)}, u32[]{:S(2)}, u32[]{:S(2)}) collective-permute-start(bf16[16,4736]{1,0:T(8,128)(2,1)S(1)} %collective-permute-done.5), channel_id=1, source_target_pairs={{0,2},{1,3},{2,0},{3,1},{4,6},{5,7},{6,4},{7,5},{8,10},{9,11},{10,... | collective-permute-start | bytes 454664 | tf_op jit(solution)/shard_map/ppermute | solution.py:31
  29.5 6.1 %collective-permute-start.12 = (bf16[16,4736]{1,0:T(8,128)(2,1)S(1)}, bf16[16,4736]{1,0:T(8,128)(2,1)S(1)}, u32[]{:S(2)}, u32[]{:S(2)}) collective-permute-start(bf16[16,4736]{1,0:T(8,128)(2,1)S(1)} %collective-permute-done.7), channel_id=1, source_target_pairs={{0,1},{1,0},{2,3},{3,2},{4,5},{5,4},{6,7},{7,6},{8,9},{9,8},{10,11... | collective-permute-start | bytes 454664 | tf_op jit(solution)/shard_map/ppermute | solution.py:31
  30.9 5.5 %collective-permute-start.11 = (bf16[16,4736]{1,0:T(8,128)(2,1)S(1)}, bf16[16,4736]{1,0:T(8,128)(2,1)S(1)}, u32[]{:S(2)}, u32[]{:S(2)}) collective-permute-start(bf16[16,4736]{1,0:T(8,128)(2,1)S(1)} %collective-permute-done.2._), channel_id=1, source_target_pairs={{0,2},{1,3},{2,0},{3,1},{4,6},{5,7},{6,4},{7,5},{8,10},{9,11},{10,... | collective-permute-start | bytes 454664 | tf_op jit(solution)/shard_map/ppermute | solution.py:31
  31.5 5.2 %collective-permute-start.14 = (bf16[16,4736]{1,0:T(8,128)(2,1)S(1)}, bf16[16,4736]{1,0:T(8,128)(2,1)S(1)}, u32[]{:S(2)}, u32[]{:S(2)}) collective-permute-start(bf16[16,4736]{1,0:T(8,128)(2,1)S(1)} %collective-permute-done.13), channel_id=1, source_target_pairs={{0,1},{1,0},{2,3},{3,2},{4,5},{5,4},{6,7},{7,6},{8,9},{9,8},{10,11... | collective-permute-start | bytes 454664 | tf_op jit(solution)/shard_map/ppermute | solution.py:31
  36.7 17.9 %copy-start.1 = (f32[4096]{0:T(1024)S(1)}, f32[4096]{0:T(1024)}, u32[]{:S(2)}) copy-start(f32[4096]{0:T(1024)} %param.17) | copy-start | bytes 49156
  39.8 4.6 %collective-permute-start.17 = (bf16[128,256]{1,0:T(8,128)(2,1)S(1)}, bf16[128,256]{1,0:T(8,128)(2,1)S(1)}, u32[]{:S(2)}, u32[]{:S(2)}) collective-permute-start(bf16[128,256]{1,0:T(8,128)(2,1)S(1)} %get-tuple-element.49), channel_id=1, source_target_pairs={{0,4},{1,5},{2,6},{3,7},{4,0},{5,1},{6,2},{7,3},{8,12},{9,13},{10,... | collective-permute-start | bytes 196616 | tf_op jit(solution)/shard_map/ppermute | solution.py:31
  39.9 8.1 %collective-permute-start.15 = (bf16[128,256]{1,0:T(8,128)(2,1)S(1)}, bf16[128,256]{1,0:T(8,128)(2,1)S(1)}, u32[]{:S(2)}, u32[]{:S(2)}) collective-permute-start(bf16[128,256]{1,0:T(8,128)(2,1)S(1)} %get-tuple-element.49), channel_id=1, source_target_pairs={{0,8},{1,9},{2,10},{3,11},{4,12},{5,13},{6,14},{7,15},{8,0},{9,1},... | collective-permute-start | bytes 196616 | tf_op jit(solution)/shard_map/ppermute | solution.py:31
  41.9 6.1 %collective-permute-start.16 = (bf16[128,256]{1,0:T(8,128)(2,1)S(1)}, bf16[128,256]{1,0:T(8,128)(2,1)S(1)}, u32[]{:S(2)}, u32[]{:S(2)}) collective-permute-start(bf16[128,256]{1,0:T(8,128)(2,1)S(1)} %get-tuple-element.49), channel_id=1, source_target_pairs={{0,12},{1,13},{2,14},{3,15},{4,8},{5,9},{6,10},{7,11},{8,4},{9,5},... | collective-permute-start | bytes 196616 | tf_op jit(solution)/shard_map/ppermute | solution.py:31
  44.4 6.6 %collective-permute-start.21 = (bf16[2,128,256]{2,1,0:T(8,128)(2,1)S(1)}, bf16[2,128,256]{2,1,0:T(8,128)(2,1)S(1)}, u32[]{:S(2)}, u32[]{:S(2)}) collective-permute-start(bf16[2,128,256]{2,1,0:T(8,128)(2,1)S(1)} %pad_maximum_fusion.1.refs_0_), channel_id=1, source_target_pairs={{0,1},{1,0},{2,3},{3,2},{4,5},{5,4},{6,7},{7,6},{8,9},{9,8},{10,11... | collective-permute-start | bytes 393224 | tf_op jit(solution)/shard_map/ppermute | solution.py:31
  45.6 7.7 %collective-permute-start.22 = (bf16[2,128,256]{2,1,0:T(8,128)(2,1)S(1)}, bf16[2,128,256]{2,1,0:T(8,128)(2,1)S(1)}, u32[]{:S(2)}, u32[]{:S(2)}) collective-permute-start(bf16[2,128,256]{2,1,0:T(8,128)(2,1)S(1)} %pad_maximum_fusion.1.refs_0_), channel_id=1, source_target_pairs={{0,2},{1,3},{2,0},{3,1},{4,6},{5,7},{6,4},{7,5},{8,10},{9,11},{10,... | collective-permute-start | bytes 393224 | tf_op jit(solution)/shard_map/ppermute | solution.py:31
  47.1 7.6 %collective-permute-start.23 = (bf16[2,128,256]{2,1,0:T(8,128)(2,1)S(1)}, bf16[2,128,256]{2,1,0:T(8,128)(2,1)S(1)}, u32[]{:S(2)}, u32[]{:S(2)}) collective-permute-start(bf16[2,128,256]{2,1,0:T(8,128)(2,1)S(1)} %pad_maximum_fusion.1.refs_0_), channel_id=1, source_target_pairs={{0,3},{1,2},{2,1},{3,0},{4,7},{5,6},{6,5},{7,4},{8,11},{9,10},{10,... | collective-permute-start | bytes 393224 | tf_op jit(solution)/shard_map/ppermute | solution.py:31
  48.0 9.9 %collective-permute-start.18 = (bf16[2,128,256]{2,1,0:T(8,128)(2,1)S(1)}, bf16[2,128,256]{2,1,0:T(8,128)(2,1)S(1)}, u32[]{:S(2)}, u32[]{:S(2)}) collective-permute-start(bf16[2,128,256]{2,1,0:T(8,128)(2,1)S(1)} %pad_maximum_fusion.refs_0_), channel_id=1, source_target_pairs={{0,1},{1,0},{2,3},{3,2},{4,5},{5,4},{6,7},{7,6},{8,9},{9,8},{10,11... | collective-permute-start | bytes 393224 | tf_op jit(solution)/shard_map/ppermute | solution.py:31
  49.6 8.3 %collective-permute-start.19 = (bf16[2,128,256]{2,1,0:T(8,128)(2,1)S(1)}, bf16[2,128,256]{2,1,0:T(8,128)(2,1)S(1)}, u32[]{:S(2)}, u32[]{:S(2)}) collective-permute-start(bf16[2,128,256]{2,1,0:T(8,128)(2,1)S(1)} %pad_maximum_fusion.refs_0_), channel_id=1, source_target_pairs={{0,2},{1,3},{2,0},{3,1},{4,6},{5,7},{6,4},{7,5},{8,10},{9,11},{10,... | collective-permute-start | bytes 393224 | tf_op jit(solution)/shard_map/ppermute | solution.py:31
  51.0 6.9 %collective-permute-start.20 = (bf16[2,128,256]{2,1,0:T(8,128)(2,1)S(1)}, bf16[2,128,256]{2,1,0:T(8,128)(2,1)S(1)}, u32[]{:S(2)}, u32[]{:S(2)}) collective-permute-start(bf16[2,128,256]{2,1,0:T(8,128)(2,1)S(1)} %pad_maximum_fusion.refs_0_), channel_id=1, source_target_pairs={{0,3},{1,2},{2,1},{3,0},{4,7},{5,6},{6,5},{7,4},{8,11},{9,10},{10,... | collective-permute-start | bytes 393224 | tf_op jit(solution)/shard_map/ppermute | solution.py:31
  54.6 3.3 %slice-start = ((s8[6291456]{0:T(1024)(128)(4,1)}), s8[4194304]{0:T(1024)(128)(4,1)S(1)}, s32[]{:S(2)}) async-start(s8[6291456]{0:T(1024)(128)(4,1)} %bitcast.34), calls=%async_computation | async-start | bytes 8388608
  54.6 3.8 %slice-start.1 = ((s8[6291456]{0:T(1024)(128)(4,1)}), s8[2097152]{0:T(1024)(128)(4,1)S(1)}, s32[]{:S(2)}) async-start(s8[6291456]{0:T(1024)(128)(4,1)} %bitcast.34), calls=%async_computation.1 | async-start | bytes 4194304
  60.6 6.8 %collective-permute-start.28 = (bf16[2,16,2048]{2,1,0:T(8,128)(2,1)S(1)}, bf16[2,16,2048]{2,1,0:T(8,128)(2,1)S(1)}, u32[]{:S(2)}, u32[]{:S(2)}) collective-permute-start(bf16[2,16,2048]{2,1,0:T(8,128)(2,1)S(1)} %get-tuple-element.64), channel_id=1, source_target_pairs={{0,3},{1,2},{2,1},{3,0},{4,7},{5,6},{6,5},{7,4},{8,11},{9,10},{10,... | collective-permute-start | bytes 393224 | tf_op jit(solution)/shard_map/ppermute | solution.py:31
  61.7 6.4 %collective-permute-start.29 = (bf16[2,16,2048]{2,1,0:T(8,128)(2,1)S(1)}, bf16[2,16,2048]{2,1,0:T(8,128)(2,1)S(1)}, u32[]{:S(2)}, u32[]{:S(2)}) collective-permute-start(bf16[2,16,2048]{2,1,0:T(8,128)(2,1)S(1)} %get-tuple-element.65), channel_id=1, source_target_pairs={{0,1},{1,0},{2,3},{3,2},{4,5},{5,4},{6,7},{7,6},{8,9},{9,8},{10,11... | collective-permute-start | bytes 393224 | tf_op jit(solution)/shard_map/ppermute | solution.py:31
  63.2 5.6 %collective-permute-start.30 = (bf16[2,16,2048]{2,1,0:T(8,128)(2,1)S(1)}, bf16[2,16,2048]{2,1,0:T(8,128)(2,1)S(1)}, u32[]{:S(2)}, u32[]{:S(2)}) collective-permute-start(bf16[2,16,2048]{2,1,0:T(8,128)(2,1)S(1)} %get-tuple-element.66), channel_id=1, source_target_pairs={{0,2},{1,3},{2,0},{3,1},{4,6},{5,7},{6,4},{7,5},{8,10},{9,11},{10,... | collective-permute-start | bytes 393224 | tf_op jit(solution)/shard_map/ppermute | solution.py:31
  64.2 8.2 %collective-permute-start.24 = (bf16[2,16,2048]{2,1,0:T(8,128)(2,1)S(1)}, bf16[2,16,2048]{2,1,0:T(8,128)(2,1)S(1)}, u32[]{:S(2)}, u32[]{:S(2)}) collective-permute-start(bf16[2,16,2048]{2,1,0:T(8,128)(2,1)S(1)} %get-tuple-element.60), channel_id=1, source_target_pairs={{0,3},{1,2},{2,1},{3,0},{4,7},{5,6},{6,5},{7,4},{8,11},{9,10},{10,... | collective-permute-start | bytes 393224 | tf_op jit(solution)/shard_map/ppermute | solution.py:31
  65.2 7.2 %collective-permute-start.25 = (bf16[2,16,2048]{2,1,0:T(8,128)(2,1)S(1)}, bf16[2,16,2048]{2,1,0:T(8,128)(2,1)S(1)}, u32[]{:S(2)}, u32[]{:S(2)}) collective-permute-start(bf16[2,16,2048]{2,1,0:T(8,128)(2,1)S(1)} %get-tuple-element.61), channel_id=1, source_target_pairs={{0,1},{1,0},{2,3},{3,2},{4,5},{5,4},{6,7},{7,6},{8,9},{9,8},{10,11... | collective-permute-start | bytes 393224 | tf_op jit(solution)/shard_map/ppermute | solution.py:31
  67.5 5.0 %collective-permute-start.26 = (bf16[2,16,2048]{2,1,0:T(8,128)(2,1)S(1)}, bf16[2,16,2048]{2,1,0:T(8,128)(2,1)S(1)}, u32[]{:S(2)}, u32[]{:S(2)}) collective-permute-start(bf16[2,16,2048]{2,1,0:T(8,128)(2,1)S(1)} %get-tuple-element.62), channel_id=1, source_target_pairs={{0,2},{1,3},{2,0},{3,1},{4,6},{5,7},{6,4},{7,5},{8,10},{9,11},{10,... | collective-permute-start | bytes 393224 | tf_op jit(solution)/shard_map/ppermute | solution.py:31
  68.9 6.6 %collective-permute-start.31 = (bf16[16,2048]{1,0:T(8,128)(2,1)S(1)}, bf16[16,2048]{1,0:T(8,128)(2,1)S(1)}, u32[]{:S(2)}, u32[]{:S(2)}) collective-permute-start(bf16[16,2048]{1,0:T(8,128)(2,1)S(1)} %get-tuple-element.67), channel_id=1, source_target_pairs={{0,8},{1,9},{2,10},{3,11},{4,12},{5,13},{6,14},{7,15},{8,0},{9,1},... | collective-permute-start | bytes 196616 | tf_op jit(solution)/shard_map/ppermute | solution.py:31
  69.0 6.6 %collective-permute-start.32 = (bf16[16,2048]{1,0:T(8,128)(2,1)S(1)}, bf16[16,2048]{1,0:T(8,128)(2,1)S(1)}, u32[]{:S(2)}, u32[]{:S(2)}) collective-permute-start(bf16[16,2048]{1,0:T(8,128)(2,1)S(1)} %get-tuple-element.68), channel_id=1, source_target_pairs={{0,12},{1,13},{2,14},{3,15},{4,8},{5,9},{6,10},{7,11},{8,4},{9,5},... | collective-permute-start | bytes 196616 | tf_op jit(solution)/shard_map/ppermute | solution.py:31
  72.5 4.3 %collective-permute-start.27 = (bf16[16,2048]{1,0:T(8,128)(2,1)S(1)}, bf16[16,2048]{1,0:T(8,128)(2,1)S(1)}, u32[]{:S(2)}, u32[]{:S(2)}) collective-permute-start(bf16[16,2048]{1,0:T(8,128)(2,1)S(1)} %slice_bitcast_fusion.2), channel_id=1, source_target_pairs={{0,4},{1,5},{2,6},{3,7},{4,0},{5,1},{6,2},{7,3},{8,12},{9,13},{10,... | collective-permute-start | bytes 196616 | tf_op jit(solution)/shard_map/ppermute | solution.py:31
  76.9 1.3 %collective-permute-start.33 = (bf16[8,2048]{1,0:T(8,128)(2,1)S(1)}, bf16[8,2048]{1,0:T(8,128)(2,1)S(1)}, u32[]{:S(2)}, u32[]{:S(2)}) collective-permute-start(bf16[8,2048]{1,0:T(8,128)(2,1)S(1)} %get-tuple-element.70), channel_id=1, source_target_pairs={{0,16},{16,0},{1,17},{17,1},{2,18},{18,2},{3,19},{19,3},{4,20},{20... | collective-permute-start | bytes 98312 | tf_op jit(solution)/shard_map/ppermute | solution.py:630

commit v5 on v4

--- a/solution.py
+++ b/solution.py
@@ -247,15 +247,8 @@
     )
 
 
-def project_kernel(count, staged, *refs):
-    copies = []
-    if staged:
-        _, gu_hbm, *refs, quarter, plain, sems = refs
-        refs.append(plain)
-        chunks = gu_hbm.shape[1] // CHUNK
-        copies = weight_copies(gu_hbm, quarter, sems, first_chunk(1, chunks))
-    for copy in copies:
-        copy.start()
+def project_kernel(count, waits, *refs):
+    refs = refs[waits:]
     pieces = refs[:count]
     *rest, w_ref, g_ref, y_ref, mix_ref, plain = refs[count:]
     blocks, sessions, _ = pieces[0].shape
@@ -305,38 +298,28 @@
     if rest:
         hidden = hidden + rest[0][...].astype(jnp.float32)
     y_ref[...] = (hidden * g_ref[...]).astype(jnp.bfloat16)
-    for copy in copies:
-        copy.wait()
-
-
-def project(pieces, out_weight, gain_columns, residual_columns=None, staged=()):
+
+
+def project(pieces, out_weight, gain_columns, residual_columns=None, waits=()):
     count = len(pieces)
     columns = out_weight.shape[1]
     rows = sum(p.shape[0] for p in pieces) * pieces[0].shape[1] // 2
     rest = [] if residual_columns is None else [residual_columns]
     vmem_spec = pl.BlockSpec(memory_space=pltpu.VMEM)
-    extra_specs, extra, extra_shapes, extra_scratch = [], [], [], []
-    if staged:
-        done, gate_up = staged
-        quarter = gate_up.shape[1] // 4
-        extra_specs = [pl.BlockSpec(memory_space=pl.ANY), pl.BlockSpec(memory_space=pltpu.HBM)]
-        extra = [done, pltpu.with_memory_space_constraint(gate_up, pltpu.HBM)]
-        extra_shapes = [jax.ShapeDtypeStruct((quarter, 2 * HID), jnp.bfloat16)]
-        extra_scratch = [pltpu.SemaphoreType.DMA((quarter // CHUNK,))]
     return pl.pallas_call(
-        functools.partial(project_kernel, count, bool(staged)),
-        in_specs=extra_specs + [vmem_spec] * (count + len(rest) + 2),
-        out_specs=[vmem_spec] * (2 + len(extra_shapes)),
+        functools.partial(project_kernel, count, len(waits)),
+        in_specs=[pl.BlockSpec(memory_space=pl.ANY)] * len(waits)
+        + [vmem_spec] * (count + len(rest) + 2),
+        out_specs=[vmem_spec] * 2,
         out_shape=[
             jax.ShapeDtypeStruct((rows, columns), jnp.bfloat16),
             jax.ShapeDtypeStruct((rows, 1), jnp.float32),
-        ]
-        + extra_shapes,
-        scratch_shapes=[pltpu.VMEM((rows, columns), jnp.float32)] + extra_scratch,
+        ],
+        scratch_shapes=[pltpu.VMEM((rows, columns), jnp.float32)],
         compiler_params=pltpu.CompilerParams(vmem_limit_bytes=8 * MIB),
         name="project",
     )(
-        *extra,
+        *waits,
         *pieces,
         *rest,
         pltpu.with_memory_space_constraint(out_weight, pltpu.VMEM),
@@ -371,9 +354,10 @@
     return ((lax.axis_index("grp") // (CHIPS // 2)) ^ half) * (chunks // 2)
 
 
-def stage_kernel(_, gu_hbm, weights, done, sems):
+def stage_kernel(_, gu_hbm, weights, quarter, done, sems, quarter_sems):
     chunks = gu_hbm.shape[1] // CHUNK
     copies = weight_copies(gu_hbm, weights, sems, first_chunk(0, chunks))
+    copies += weight_copies(gu_hbm, quarter, quarter_sems, first_chunk(1, chunks))
     for copy in copies:
         copy.start()
     done[...] = jnp.zeros_like(done)
@@ -388,15 +372,19 @@
     return pl.pallas_call(
         stage_kernel,
         in_specs=[pl.BlockSpec(memory_space=pl.ANY), hbm_spec],
-        out_specs=[vmem_spec] * 2,
+        out_specs=[vmem_spec] * 3,
         out_shape=[
             jax.ShapeDtypeStruct((depth, 2 * HID), jnp.bfloat16),
+            jax.ShapeDtypeStruct((depth // 2, 2 * HID), jnp.bfloat16),
             jax.ShapeDtypeStruct((8, LANES), jnp.float32),
         ],
-        scratch_shapes=[pltpu.SemaphoreType.DMA((depth // CHUNK,))],
+        scratch_shapes=[
+            pltpu.SemaphoreType.DMA((depth // CHUNK,)),
+            pltpu.SemaphoreType.DMA((depth // 2 // CHUNK,)),
+        ],
         compiler_params=pltpu.CompilerParams(vmem_limit_bytes=2 * MIB),
         cost_estimate=pl.CostEstimate(
-            flops=0, bytes_accessed=depth * 4 * HID, transcendentals=0
+            flops=0, bytes_accessed=depth * 6 * HID, transcendentals=0
         ),
         name="stage",
     )(arrived, pltpu.with_memory_space_constraint(gate_up, pltpu.HBM))
@@ -598,10 +586,8 @@
     if groups == CHIPS:
         *carried, gain = attend(groups, PLANES, *arrays)
         pieces = gather(carried)
-        staged, done = stage(gate_up, pieces[9])
-        y, mix, third = project(
-            [p[None] for p in pieces], out_weight, gain, staged=(done, gate_up)
-        )
+        staged, third, done = stage(gate_up, pieces[9])
+        y, mix = project([p[None] for p in pieces], out_weight, gain, waits=(done,))
         nears, fars = gather_pairs(y)
         *begun, fourth = near(nears, staged, gate_up, norm_gain)
         *sums, hidden = experts(

time: 79 us -> 77.2 us (0.977)
  Pallas kernels: 14 us -> 13.1 us
    pallas_call x1, Pallas kernels: 3.1 us -> 1.27 us  [project(): pl.pallas_call(functools.partial(project_kernel, count, len(waits)), in_s...]
    pallas_call x1, Pallas kernels: 2.86 us -> 3.79 us  [stage(): pl.pallas_call(stage_kernel, in_specs=[pl.BlockSpec(memory_space=pl.ANY),...]
  transfers between devices with their start and end apart: 34 -> 34, of which waited for: 14 -> 15; matrix products, arithmetic and copies ran while one was open for 0% -> 0% of each run, Pallas kernels for 8% -> 9%
where the time goes in v5:
time: 77.2 us; the launch traced here: 77 us
  starting transfers between devices  45.8 us (59%)
  waiting for transfers between devices  16.5 us (21%)
  Pallas kernels  13.1 us (17%)
  other arithmetic  0.86 us (1%)
    ppermute x33, starting transfers between devices, exchange(): return lax.ppermute(value, 'grp', [(g, g ^ bits) for g in range(CHIPS)])  45.8 us
    ppermute x33, waiting for transfers between devices, exchange(): return lax.ppermute(value, 'grp', [(g, g ^ bits) for g in range(CHIPS)])  15.3 us
    pallas_call x1, Pallas kernels, stage(): pl.pallas_call(stage_kernel, in_specs=[pl.BlockSpec(memory_space=pl.ANY),...  3.79 us
    pallas_call x1, Pallas kernels, near(): pl.pallas_call(functools.partial(near_kernel, count), in_specs=[vmem_spec...  3.24 us
    pallas_call x1, Pallas kernels, attend(): pl.pallas_call(functools.partial(attend_kernel, planes), in_specs=[hbm_sp...  2.62 us
    pallas_call x1, Pallas kernels, experts(): pl.pallas_call(functools.partial(expert_kernel, count, outs, len(gate_ups...  2.16 us
  transfers between devices with their start and end apart: 34, of which 15 were waited for; matrix products, arithmetic and copies ran while one was open for 0% of the time, Pallas kernels for 9%

profile of v5, /device:TPU:0, one launch (start us, length us, event | category | flops | bytes accessed | tf_op | source)
XLA Modules:
  0.0 77.0 jit_solution(1559239078280193808)
XLA Ops:
  0.0 2.6 %attend.1 = (bf16[16,5248]{1,0:T(8,128)(2,1)S(1)}, bf16[16,4736]{1,0:T(8,128)(2,1)S(1)}, bf16[16,4736]{1,0:T(8,128)(2,1)S(1)}, bf16[16,4736]{1,0:T(8,128)(2,1)S(1)}, f32[1,256]{1,0:T(1,128)S(1)}) custom-call(s32[8,16]{1,0:T(8,128)} %bitcast.59, f32[8,16]{1,0:T(8,128)} %bitcast.60, s32[16]{0:T(128)} %len_hbm.1, f32[16,1,256]{2,1,0:T(1,128)} %bitcast.52, ...), custom_call_target="tpu_custom_call" | custom-call | tf_op jit(solution)/shard_map/attend/pallas_call | solution.py:219
  2.6 4.1 %collective-permute-start = (bf16[16,4736]{1,0:T(8,128)(2,1)S(1)}, bf16[16,4736]{1,0:T(8,128)(2,1)S(1)}, u32[]{:S(2)}, u32[]{:S(2)}) collective-permute-start(bf16[16,4736]{1,0:T(8,128)(2,1)S(1)} %get-tuple-element.36), channel_id=1, source_target_pairs={{0,8},{1,9},{2,10},{3,11},{4,12},{5,13},{6,14},{7,15},{8,0},{9,1},... | collective-permute-start | bytes 454664 | tf_op jit(solution)/shard_map/ppermute | solution.py:31
  6.7 1.5 %collective-permute-start.3 = (bf16[16,5248]{1,0:T(8,128)(2,1)S(1)}, bf16[16,5248]{1,0:T(8,128)(2,1)S(1)}, u32[]{:S(2)}, u32[]{:S(2)}) collective-permute-start(bf16[16,5248]{1,0:T(8,128)(2,1)S(1)} %get-tuple-element.37), channel_id=1, source_target_pairs={{0,1},{1,0},{2,3},{3,2},{4,5},{5,4},{6,7},{7,6},{8,9},{9,8},{10,11... | collective-permute-start | bytes 503816 | tf_op jit(solution)/shard_map/ppermute | solution.py:31
  8.2 1.5 %collective-permute-start.1 = (bf16[16,5248]{1,0:T(8,128)(2,1)S(1)}, bf16[16,5248]{1,0:T(8,128)(2,1)S(1)}, u32[]{:S(2)}, u32[]{:S(2)}) collective-permute-start(bf16[16,5248]{1,0:T(8,128)(2,1)S(1)} %get-tuple-element.37), channel_id=1, source_target_pairs={{0,2},{1,3},{2,0},{3,1},{4,6},{5,7},{6,4},{7,5},{8,10},{9,11},{10,... | collective-permute-start | bytes 503816 | tf_op jit(solution)/shard_map/ppermute | solution.py:31
  9.7 1.6 %collective-permute-start.5 = (bf16[16,4736]{1,0:T(8,128)(2,1)S(1)}, bf16[16,4736]{1,0:T(8,128)(2,1)S(1)}, u32[]{:S(2)}, u32[]{:S(2)}) collective-permute-start(bf16[16,4736]{1,0:T(8,128)(2,1)S(1)} %get-tuple-element.40), channel_id=1, source_target_pairs={{0,4},{1,5},{2,6},{3,7},{4,0},{5,1},{6,2},{7,3},{8,12},{9,13},{10,... | collective-permute-start | bytes 454664 | tf_op jit(solution)/shard_map/ppermute | solution.py:31
  11.3 2.7 %collective-permute-done = bf16[16,4736]{1,0:T(8,128)(2,1)S(1)} collective-permute-done((bf16[16,4736]{1,0:T(8,128)(2,1)S(1)}, bf16[16,4736]{1,0:T(8,128)(2,1)S(1)}, u32[]{:S(2)}, u32[]{:S(2)}) %collective-permute-start) | collective-permute-done | bytes 151584 | tf_op jit(solution)/shard_map/ppermute | solution.py:31
  14.0 3.5 %collective-permute-start.7 = (bf16[16,4736]{1,0:T(8,128)(2,1)S(1)}, bf16[16,4736]{1,0:T(8,128)(2,1)S(1)}, u32[]{:S(2)}, u32[]{:S(2)}) collective-permute-start(bf16[16,4736]{1,0:T(8,128)(2,1)S(1)} %get-tuple-element.43), channel_id=1, source_target_pairs={{0,12},{1,13},{2,14},{3,15},{4,8},{5,9},{6,10},{7,11},{8,4},{9,5},... | collective-permute-start | bytes 454664 | tf_op jit(solution)/shard_map/ppermute | solution.py:31
  17.6 1.5 %collective-permute-start.4 = (bf16[16,5248]{1,0:T(8,128)(2,1)S(1)}, bf16[16,5248]{1,0:T(8,128)(2,1)S(1)}, u32[]{:S(2)}, u32[]{:S(2)}) collective-permute-start(bf16[16,5248]{1,0:T(8,128)(2,1)S(1)} %collective-permute-done.3), channel_id=1, source_target_pairs={{0,2},{1,3},{2,0},{3,1},{4,6},{5,7},{6,4},{7,5},{8,10},{9,11},{10,... | collective-permute-start | bytes 503816 | tf_op jit(solution)/shard_map/ppermute | solution.py:31
  19.1 0.5 collective-permute-start.10
  19.6 1.5 %collective-permute-start.2 = (bf16[16,4736]{1,0:T(8,128)(2,1)S(1)}, bf16[16,4736]{1,0:T(8,128)(2,1)S(1)}, u32[]{:S(2)}, u32[]{:S(2)}) collective-permute-start(bf16[16,4736]{1,0:T(8,128)(2,1)S(1)} %collective-permute-done), channel_id=1, source_target_pairs={{0,1},{1,0},{2,3},{3,2},{4,5},{5,4},{6,7},{7,6},{8,9},{9,8},{10,11... | collective-permute-start | bytes 454664 | tf_op jit(solution)/shard_map/ppermute | solution.py:31
  21.1 1.5 %collective-permute-done.7 = bf16[16,4736]{1,0:T(8,128)(2,1)S(1)} collective-permute-done((bf16[16,4736]{1,0:T(8,128)(2,1)S(1)}, bf16[16,4736]{1,0:T(8,128)(2,1)S(1)}, u32[]{:S(2)}, u32[]{:S(2)}) %collective-permute-start.7) | collective-permute-done | bytes 151584 | tf_op jit(solution)/shard_map/ppermute | solution.py:31
  22.6 1.6 %collective-permute-start.13 = (bf16[16,4736]{1,0:T(8,128)(2,1)S(1)}, bf16[16,4736]{1,0:T(8,128)(2,1)S(1)}, u32[]{:S(2)}, u32[]{:S(2)}) collective-permute-start(bf16[16,4736]{1,0:T(8,128)(2,1)S(1)} %collective-permute-done.7), channel_id=1, source_target_pairs={{0,2},{1,3},{2,0},{3,1},{4,6},{5,7},{6,4},{7,5},{8,10},{9,11},{10,... | collective-permute-start | bytes 454664 | tf_op jit(solution)/shard_map/ppermute | solution.py:31
  24.2 0.6 collective-permute-done.4
  24.8 0.5 collective-permute-start.9
  25.3 2.7 %collective-permute-done.10 = bf16[16,4736]{1,0:T(8,128)(2,1)S(1)} collective-permute-done((bf16[16,4736]{1,0:T(8,128)(2,1)S(1)}, bf16[16,4736]{1,0:T(8,128)(2,1)S(1)}, u32[]{:S(2)}, u32[]{:S(2)}) %collective-permute-start.10) | collective-permute-done | bytes 151584 | tf_op jit(solution)/shard_map/ppermute | solution.py:31
  28.0 1.5 %collective-permute-start.8 = (bf16[16,4736]{1,0:T(8,128)(2,1)S(1)}, bf16[16,4736]{1,0:T(8,128)(2,1)S(1)}, u32[]{:S(2)}, u32[]{:S(2)}) collective-permute-start(bf16[16,4736]{1,0:T(8,128)(2,1)S(1)} %collective-permute-done.5), channel_id=1, source_target_pairs={{0,2},{1,3},{2,0},{3,1},{4,6},{5,7},{6,4},{7,5},{8,10},{9,11},{10,... | collective-permute-start | bytes 454664 | tf_op jit(solution)/shard_map/ppermute | solution.py:31
  29.5 1.4 %collective-permute-start.12 = (bf16[16,4736]{1,0:T(8,128)(2,1)S(1)}, bf16[16,4736]{1,0:T(8,128)(2,1)S(1)}, u32[]{:S(2)}, u32[]{:S(2)}) collective-permute-start(bf16[16,4736]{1,0:T(8,128)(2,1)S(1)} %collective-permute-done.7), channel_id=1, source_target_pairs={{0,1},{1,0},{2,3},{3,2},{4,5},{5,4},{6,7},{7,6},{8,9},{9,8},{10,11... | collective-permute-start | bytes 454664 | tf_op jit(solution)/shard_map/ppermute | solution.py:31
  30.9 0.6 collective-permute-start.11
  31.5 1.2 %collective-permute-start.14 = (bf16[16,4736]{1,0:T(8,128)(2,1)S(1)}, bf16[16,4736]{1,0:T(8,128)(2,1)S(1)}, u32[]{:S(2)}, u32[]{:S(2)}) collective-permute-start(bf16[16,4736]{1,0:T(8,128)(2,1)S(1)} %collective-permute-done.13), channel_id=1, source_target_pairs={{0,1},{1,0},{2,3},{3,2},{4,5},{5,4},{6,7},{7,6},{8,9},{9,8},{10,11... | collective-permute-start | bytes 454664 | tf_op jit(solution)/shard_map/ppermute | solution.py:31
  32.7 3.8 %stage.1 = (bf16[2048,1536]{1,0:T(8,128)(2,1)S(1)}, bf16[1024,1536]{1,0:T(8,128)(2,1)S(1)}, f32[8,128]{1,0:T(8,128)S(1)}) custom-call(bf16[16,4736]{1,0:T(8,128)(2,1)S(1)} %collective-permute-done.2._, bf16[1,4096,1536]{2,1,0:T(8,128)(2,1)} %refs_5_.1), custom_call_target="tpu_custom_call" | custom-call | bytes 9437184 | tf_op jit(solution)/shard_map/stage/pallas_call | solution.py:372
  36.7 1.3 %project.1 = (bf16[128,256]{1,0:T(8,128)(2,1)S(1)}, f32[128,1]{1,0:T(8,128)S(1)}) custom-call(f32[8,128]{1,0:T(8,128)S(1)} %get-tuple-element.39.refs_0_, bf16[1,16,5248]{2,1,0:T(8,128)(2,1)S(1)} %bitcast.37, bf16[1,16,5248]{2,1,0:T(8,128)(2,1)S(1)} %bitcast.38, bf16[1,16,5248]{2,1,0:T(8,128)(2,1)S(1)} %bitcast.39, bf16[1,16,5248]{2,1,0:T(8,128)(2,1)S(1)} %bitcast.40, ...), custom_call_target="tpu_custom_call" | custom-call | tf_op jit(solution)/shard_map/project/pallas_call | solution.py:309
  38.1 2.2 %collective-permute-start.15 = (bf16[128,256]{1,0:T(8,128)(2,1)S(1)}, bf16[128,256]{1,0:T(8,128)(2,1)S(1)}, u32[]{:S(2)}, u32[]{:S(2)}) collective-permute-start(bf16[128,256]{1,0:T(8,128)(2,1)S(1)} %get-tuple-element.49), channel_id=1, source_target_pairs={{0,8},{1,9},{2,10},{3,11},{4,12},{5,13},{6,14},{7,15},{8,0},{9,1},... | collective-permute-start | bytes 196616 | tf_op jit(solution)/shard_map/ppermute | solution.py:31
  40.3 2.1 %collective-permute-start.16 = (bf16[128,256]{1,0:T(8,128)(2,1)S(1)}, bf16[128,256]{1,0:T(8,128)(2,1)S(1)}, u32[]{:S(2)}, u32[]{:S(2)}) collective-permute-start(bf16[128,256]{1,0:T(8,128)(2,1)S(1)} %get-tuple-element.49), channel_id=1, source_target_pairs={{0,12},{1,13},{2,14},{3,15},{4,8},{5,9},{6,10},{7,11},{8,4},{9,5},... | collective-permute-start | bytes 196616 | tf_op jit(solution)/shard_map/ppermute | solution.py:31
  42.7 1.1 %collective-permute-start.21 = (bf16[2,128,256]{2,1,0:T(8,128)(2,1)S(1)}, bf16[2,128,256]{2,1,0:T(8,128)(2,1)S(1)}, u32[]{:S(2)}, u32[]{:S(2)}) collective-permute-start(bf16[2,128,256]{2,1,0:T(8,128)(2,1)S(1)} %pad_maximum_fusion.1.refs_0_), channel_id=1, source_target_pairs={{0,1},{1,0},{2,3},{3,2},{4,5},{5,4},{6,7},{7,6},{8,9},{9,8},{10,11... | collective-permute-start | bytes 393224 | tf_op jit(solution)/shard_map/ppermute | solution.py:31
  43.8 1.5 %collective-permute-start.22 = (bf16[2,128,256]{2,1,0:T(8,128)(2,1)S(1)}, bf16[2,128,256]{2,1,0:T(8,128)(2,1)S(1)}, u32[]{:S(2)}, u32[]{:S(2)}) collective-permute-start(bf16[2,128,256]{2,1,0:T(8,128)(2,1)S(1)} %pad_maximum_fusion.1.refs_0_), channel_id=1, source_target_pairs={{0,2},{1,3},{2,0},{3,1},{4,6},{5,7},{6,4},{7,5},{8,10},{9,11},{10,... | collective-permute-start | bytes 393224 | tf_op jit(solution)/shard_map/ppermute | solution.py:31
  45.3 1.0 %collective-permute-start.23 = (bf16[2,128,256]{2,1,0:T(8,128)(2,1)S(1)}, bf16[2,128,256]{2,1,0:T(8,128)(2,1)S(1)}, u32[]{:S(2)}, u32[]{:S(2)}) collective-permute-start(bf16[2,128,256]{2,1,0:T(8,128)(2,1)S(1)} %pad_maximum_fusion.1.refs_0_), channel_id=1, source_target_pairs={{0,3},{1,2},{2,1},{3,0},{4,7},{5,6},{6,5},{7,4},{8,11},{9,10},{10,... | collective-permute-start | bytes 393224 | tf_op jit(solution)/shard_map/ppermute | solution.py:31
  46.4 1.4 %collective-permute-start.18 = (bf16[2,128,256]{2,1,0:T(8,128)(2,1)S(1)}, bf16[2,128,256]{2,1,0:T(8,128)(2,1)S(1)}, u32[]{:S(2)}, u32[]{:S(2)}) collective-permute-start(bf16[2,128,256]{2,1,0:T(8,128)(2,1)S(1)} %pad_maximum_fusion.refs_0_), channel_id=1, source_target_pairs={{0,1},{1,0},{2,3},{3,2},{4,5},{5,4},{6,7},{7,6},{8,9},{9,8},{10,11... | collective-permute-start | bytes 393224 | tf_op jit(solution)/shard_map/ppermute | solution.py:31
  47.8 1.4 %collective-permute-start.19 = (bf16[2,128,256]{2,1,0:T(8,128)(2,1)S(1)}, bf16[2,128,256]{2,1,0:T(8,128)(2,1)S(1)}, u32[]{:S(2)}, u32[]{:S(2)}) collective-permute-start(bf16[2,128,256]{2,1,0:T(8,128)(2,1)S(1)} %pad_maximum_fusion.refs_0_), channel_id=1, source_target_pairs={{0,2},{1,3},{2,0},{3,1},{4,6},{5,7},{6,4},{7,5},{8,10},{9,11},{10,... | collective-permute-start | bytes 393224 | tf_op jit(solution)/shard_map/ppermute | solution.py:31
  49.2 1.8 %collective-permute-start.20 = (bf16[2,128,256]{2,1,0:T(8,128)(2,1)S(1)}, bf16[2,128,256]{2,1,0:T(8,128)(2,1)S(1)}, u32[]{:S(2)}, u32[]{:S(2)}) collective-permute-start(bf16[2,128,256]{2,1,0:T(8,128)(2,1)S(1)} %pad_maximum_fusion.refs_0_), channel_id=1, source_target_pairs={{0,3},{1,2},{2,1},{3,0},{4,7},{5,6},{6,5},{7,4},{8,11},{9,10},{10,... | collective-permute-start | bytes 393224 | tf_op jit(solution)/shard_map/ppermute | solution.py:31
  51.0 0.4 collective-permute-done.22.refs_2_
  51.4 1.4 %collective-permute-done.23.refs_3_ = bf16[2,128,256]{2,1,0:T(8,128)(2,1)S(1)} collective-permute-done((bf16[2,128,256]{2,1,0:T(8,128)(2,1)S(1)}, bf16[2,128,256]{2,1,0:T(8,128)(2,1)S(1)}, u32[]{:S(2)}, u32[]{:S(2)}) %collective-permute-start.23) | collective-permute-done | bytes 131104 | tf_op jit(solution)/shard_map/ppermute | solution.py:31
  52.8 3.2 %near.1 = (f32[128,1536]{1,0:T(8,128)S(1)}, f32[128,128]{1,0:T(8,128)S(1)}, f32[16,2048]{1,0:T(8,128)S(1)}, bf16[1024,1536]{1,0:T(8,128)(2,1)S(1)}) custom-call(bf16[2,128,256]{2,1,0:T(8,128)(2,1)S(1)} %pad_maximum_fusion.1.refs_0_, bf16[2,128,256]{2,1,0:T(8,128)(2,1)S(1)} %collective-permute-done.21.refs_1_, ...), custom_call_target="tpu_custom_call" | custom-call | flops 805306368 | bytes 12582912 | tf_op jit(solution)/shard_map/near/pallas_call | solution.py:424
  56.1 0.5 slice-done.1
  56.6 2.2 %experts.1 = (bf16[2,16,2048]{2,1,0:T(8,128)(2,1)S(1)}, bf16[2,16,2048]{2,1,0:T(8,128)(2,1)S(1)}, bf16[2,16,2048]{2,1,0:T(8,128)(2,1)S(1)}, bf16[2,16,2048]{2,1,...) custom-call(bf16[2,128,256]{2,1,0:T(8,128)(2,1)S(1)} %pad_maximum_fu, ...), custom_call_target="tpu_custom_call" | custom-call | tf_op jit(solution)/shard_map/experts/pallas_call | solution.py:533
  58.8 1.1 %collective-permute-start.28 = (bf16[2,16,2048]{2,1,0:T(8,128)(2,1)S(1)}, bf16[2,16,2048]{2,1,0:T(8,128)(2,1)S(1)}, u32[]{:S(2)}, u32[]{:S(2)}) collective-permute-start(bf16[2,16,2048]{2,1,0:T(8,128)(2,1)S(1)} %get-tuple-element.64), channel_id=1, source_target_pairs={{0,3},{1,2},{2,1},{3,0},{4,7},{5,6},{6,5},{7,4},{8,11},{9,10},{10,... | collective-permute-start | bytes 393224 | tf_op jit(solution)/shard_map/ppermute | solution.py:31
  59.9 1.5 %collective-permute-start.29 = (bf16[2,16,2048]{2,1,0:T(8,128)(2,1)S(1)}, bf16[2,16,2048]{2,1,0:T(8,128)(2,1)S(1)}, u32[]{:S(2)}, u32[]{:S(2)}) collective-permute-start(bf16[2,16,2048]{2,1,0:T(8,128)(2,1)S(1)} %get-tuple-element.65), channel_id=1, source_target_pairs={{0,1},{1,0},{2,3},{3,2},{4,5},{5,4},{6,7},{7,6},{8,9},{9,8},{10,11... | collective-permute-start | bytes 393224 | tf_op jit(solution)/shard_map/ppermute | solution.py:31
  61.4 1.0 %collective-permute-start.30 = (bf16[2,16,2048]{2,1,0:T(8,128)(2,1)S(1)}, bf16[2,16,2048]{2,1,0:T(8,128)(2,1)S(1)}, u32[]{:S(2)}, u32[]{:S(2)}) collective-permute-start(bf16[2,16,2048]{2,1,0:T(8,128)(2,1)S(1)} %get-tuple-element.66), channel_id=1, source_target_pairs={{0,2},{1,3},{2,0},{3,1},{4,6},{5,7},{6,4},{7,5},{8,10},{9,11},{10,... | collective-permute-start | bytes 393224 | tf_op jit(solution)/shard_map/ppermute | solution.py:31
  62.4 1.0 %collective-permute-start.24 = (bf16[2,16,2048]{2,1,0:T(8,128)(2,1)S(1)}, bf16[2,16,2048]{2,1,0:T(8,128)(2,1)S(1)}, u32[]{:S(2)}, u32[]{:S(2)}) collective-permute-start(bf16[2,16,2048]{2,1,0:T(8,128)(2,1)S(1)} %get-tuple-element.60), channel_id=1, source_target_pairs={{0,3},{1,2},{2,1},{3,0},{4,7},{5,6},{6,5},{7,4},{8,11},{9,10},{10,... | collective-permute-start | bytes 393224 | tf_op jit(solution)/shard_map/ppermute | solution.py:31
  63.4 1.5 %collective-permute-start.25 = (bf16[2,16,2048]{2,1,0:T(8,128)(2,1)S(1)}, bf16[2,16,2048]{2,1,0:T(8,128)(2,1)S(1)}, u32[]{:S(2)}, u32[]{:S(2)}) collective-permute-start(bf16[2,16,2048]{2,1,0:T(8,128)(2,1)S(1)} %get-tuple-element.61), channel_id=1, source_target_pairs={{0,1},{1,0},{2,3},{3,2},{4,5},{5,4},{6,7},{7,6},{8,9},{9,8},{10,11... | collective-permute-start | bytes 393224 | tf_op jit(solution)/shard_map/ppermute | solution.py:31
  64.9 0.8 %collective-permute-done.28 = bf16[2,16,2048]{2,1,0:T(8,128)(2,1)S(1)} collective-permute-done((bf16[2,16,2048]{2,1,0:T(8,128)(2,1)S(1)}, bf16[2,16,2048]{2,1,0:T(8,128)(2,1)S(1)}, u32[]{:S(2)}, u32[]{:S(2)}) %collective-permute-start.28) | collective-permute-done | bytes 131104 | tf_op jit(solution)/shard_map/ppermute | solution.py:31
  65.7 0.6 collective-permute-start.26
  66.3 0.7 collective-permute-done.30
  67.2 3.4 %collective-permute-start.32 = (bf16[16,2048]{1,0:T(8,128)(2,1)S(1)}, bf16[16,2048]{1,0:T(8,128)(2,1)S(1)}, u32[]{:S(2)}, u32[]{:S(2)}) collective-permute-start(bf16[16,2048]{1,0:T(8,128)(2,1)S(1)} %get-tuple-element.68), channel_id=1, source_target_pairs={{0,12},{1,13},{2,14},{3,15},{4,8},{5,9},{6,10},{7,11},{8,4},{9,5},... | collective-permute-start | bytes 196616 | tf_op jit(solution)/shard_map/ppermute | solution.py:31
  70.7 0.5 collective-permute-start.27
  71.2 2.5 %collective-permute-done.31 = bf16[16,2048]{1,0:T(8,128)(2,1)S(1)} collective-permute-done((bf16[16,2048]{1,0:T(8,128)(2,1)S(1)}, bf16[16,2048]{1,0:T(8,128)(2,1)S(1)}, u32[]{:S(2)}, u32[]{:S(2)}) %collective-permute-start.31) | collective-permute-done | bytes 65568 | tf_op jit(solution)/shard_map/ppermute | solution.py:31
  73.8 1.3 %collective-permute-done.27 = bf16[16,2048]{1,0:T(8,128)(2,1)S(1)} collective-permute-done((bf16[16,2048]{1,0:T(8,128)(2,1)S(1)}, bf16[16,2048]{1,0:T(8,128)(2,1)S(1)}, u32[]{:S(2)}, u32[]{:S(2)}) %collective-permute-start.27) | collective-permute-done | bytes 65568 | tf_op jit(solution)/shard_map/ppermute | solution.py:31
  75.2 1.2 %collective-permute-done.33 = bf16[8,2048]{1,0:T(8,128)(2,1)S(1)} collective-permute-done((bf16[8,2048]{1,0:T(8,128)(2,1)S(1)}, bf16[8,2048]{1,0:T(8,128)(2,1)S(1)}, u32[]{:S(2)}, u32[]{:S(2)}) %collective-permute-start.33) | collective-permute-done | bytes 32800 | tf_op jit(solution)/shard_map/ppermute | solution.py:616
  76.4 0.6 maximum_select_fusion
  (44 shorter events, 1.1 us)
Async XLA Ops:
  2.6 11.4 %collective-permute-start = (bf16[16,4736]{1,0:T(8,128)(2,1)S(1)}, bf16[16,4736]{1,0:T(8,128)(2,1)S(1)}, u32[]{:S(2)}, u32[]{:S(2)}) collective-permute-start(bf16[16,4736]{1,0:T(8,128)(2,1)S(1)} %get-tuple-element.36), channel_id=1, source_target_pairs={{0,8},{1,9},{2,10},{3,11},{4,12},{5,13},{6,14},{7,15},{8,0},{9,1},... | collective-permute-start | bytes 454664 | tf_op jit(solution)/shard_map/ppermute | solution.py:31
  6.7 10.8 %collective-permute-start.3 = (bf16[16,5248]{1,0:T(8,128)(2,1)S(1)}, bf16[16,5248]{1,0:T(8,128)(2,1)S(1)}, u32[]{:S(2)}, u32[]{:S(2)}) collective-permute-start(bf16[16,5248]{1,0:T(8,128)(2,1)S(1)} %get-tuple-element.37), channel_id=1, source_target_pairs={{0,1},{1,0},{2,3},{3,2},{4,5},{5,4},{6,7},{7,6},{8,9},{9,8},{10,11... | collective-permute-start | bytes 503816 | tf_op jit(solution)/shard_map/ppermute | solution.py:31
  8.2 11.4 %collective-permute-start.1 = (bf16[16,5248]{1,0:T(8,128)(2,1)S(1)}, bf16[16,5248]{1,0:T(8,128)(2,1)S(1)}, u32[]{:S(2)}, u32[]{:S(2)}) collective-permute-start(bf16[16,5248]{1,0:T(8,128)(2,1)S(1)} %get-tuple-element.37), channel_id=1, source_target_pairs={{0,2},{1,3},{2,0},{3,1},{4,6},{5,7},{6,4},{7,5},{8,10},{9,11},{10,... | collective-permute-start | bytes 503816 | tf_op jit(solution)/shard_map/ppermute | solution.py:31
  9.7 9.3 %collective-permute-start.5 = (bf16[16,4736]{1,0:T(8,128)(2,1)S(1)}, bf16[16,4736]{1,0:T(8,128)(2,1)S(1)}, u32[]{:S(2)}, u32[]{:S(2)}) collective-permute-start(bf16[16,4736]{1,0:T(8,128)(2,1)S(1)} %get-tuple-element.40), channel_id=1, source_target_pairs={{0,4},{1,5},{2,6},{3,7},{4,0},{5,1},{6,2},{7,3},{8,12},{9,13},{10,... | collective-permute-start | bytes 454664 | tf_op jit(solution)/shard_map/ppermute | solution.py:31
  14.0 22.7 %copy-start = (bf16[8192,256]{1,0:T(8,128)(2,1)S(1)}, bf16[8192,256]{1,0:T(8,128)(2,1)}, u32[]{:S(2)}) copy-start(bf16[8192,256]{1,0:T(8,128)(2,1)} %refs_17_.1) | copy-start | bytes 12582916
  14.0 8.6 %collective-permute-start.7 = (bf16[16,4736]{1,0:T(8,128)(2,1)S(1)}, bf16[16,4736]{1,0:T(8,128)(2,1)S(1)}, u32[]{:S(2)}, u32[]{:S(2)}) collective-permute-start(bf16[16,4736]{1,0:T(8,128)(2,1)S(1)} %get-tuple-element.43), channel_id=1, source_target_pairs={{0,12},{1,13},{2,14},{3,15},{4,8},{5,9},{6,10},{7,11},{8,4},{9,5},... | collective-permute-start | bytes 454664 | tf_op jit(solution)/shard_map/ppermute | solution.py:31
  17.6 7.2 %collective-permute-start.4 = (bf16[16,5248]{1,0:T(8,128)(2,1)S(1)}, bf16[16,5248]{1,0:T(8,128)(2,1)S(1)}, u32[]{:S(2)}, u32[]{:S(2)}) collective-permute-start(bf16[16,5248]{1,0:T(8,128)(2,1)S(1)} %collective-permute-done.3), channel_id=1, source_target_pairs={{0,2},{1,3},{2,0},{3,1},{4,6},{5,7},{6,4},{7,5},{8,10},{9,11},{10,... | collective-permute-start | bytes 503816 | tf_op jit(solution)/shard_map/ppermute | solution.py:31
  19.1 11.8 %collective-permute-start.6 = (bf16[16,5248]{1,0:T(8,128)(2,1)S(1)}, bf16[16,5248]{1,0:T(8,128)(2,1)S(1)}, u32[]{:S(2)}, u32[]{:S(2)}) collective-permute-start(bf16[16,5248]{1,0:T(8,128)(2,1)S(1)} %collective-permute-done.3), channel_id=1, source_target_pairs={{0,4},{1,5},{2,6},{3,7},{4,0},{5,1},{6,2},{7,3},{8,12},{9,13},{10,... | collective-permute-start | bytes 503816 | tf_op jit(solution)/shard_map/ppermute | solution.py:31
  19.1 8.9 %collective-permute-start.10 = (bf16[16,4736]{1,0:T(8,128)(2,1)S(1)}, bf16[16,4736]{1,0:T(8,128)(2,1)S(1)}, u32[]{:S(2)}, u32[]{:S(2)}) collective-permute-start(bf16[16,4736]{1,0:T(8,128)(2,1)S(1)} %collective-permute-done), channel_id=1, source_target_pairs={{0,2},{1,3},{2,0},{3,1},{4,6},{5,7},{6,4},{7,5},{8,10},{9,11},{10,... | collective-permute-start | bytes 454664 | tf_op jit(solution)/shard_map/ppermute | solution.py:31
  19.6 9.9 %collective-permute-start.2 = (bf16[16,4736]{1,0:T(8,128)(2,1)S(1)}, bf16[16,4736]{1,0:T(8,128)(2,1)S(1)}, u32[]{:S(2)}, u32[]{:S(2)}) collective-permute-start(bf16[16,4736]{1,0:T(8,128)(2,1)S(1)} %collective-permute-done), channel_id=1, source_target_pairs={{0,1},{1,0},{2,3},{3,2},{4,5},{5,4},{6,7},{7,6},{8,9},{9,8},{10,11... | collective-permute-start | bytes 454664 | tf_op jit(solution)/shard_map/ppermute | solution.py:31
  22.6 8.9 %collective-permute-start.13 = (bf16[16,4736]{1,0:T(8,128)(2,1)S(1)}, bf16[16,4736]{1,0:T(8,128)(2,1)S(1)}, u32[]{:S(2)}, u32[]{:S(2)}) collective-permute-start(bf16[16,4736]{1,0:T(8,128)(2,1)S(1)} %collective-permute-done.7), channel_id=1, source_target_pairs={{0,2},{1,3},{2,0},{3,1},{4,6},{5,7},{6,4},{7,5},{8,10},{9,11},{10,... | collective-permute-start | bytes 454664 | tf_op jit(solution)/shard_map/ppermute | solution.py:31
  24.8 11.8 %collective-permute-start.9 = (bf16[16,5248]{1,0:T(8,128)(2,1)S(1)}, bf16[16,5248]{1,0:T(8,128)(2,1)S(1)}, u32[]{:S(2)}, u32[]{:S(2)}) collective-permute-start(bf16[16,5248]{1,0:T(8,128)(2,1)S(1)} %collective-permute-done.4), channel_id=1, source_target_pairs={{0,4},{1,5},{2,6},{3,7},{4,0},{5,1},{6,2},{7,3},{8,12},{9,13},{10,... | collective-permute-start | bytes 503816 | tf_op jit(solution)/shard_map/ppermute | solution.py:31
  28.0 8.5 %collective-permute-start.8 = (bf16[16,4736]{1,0:T(8,128)(2,1)S(1)}, bf16[16,4736]{1,0:T(8,128)(2,1)S(1)}, u32[]{:S(2)}, u32[]{:S(2)}) collective-permute-start(bf16[16,4736]{1,0:T(8,128)(2,1)S(1)} %collective-permute-done.5), channel_id=1, source_target_pairs={{0,2},{1,3},{2,0},{3,1},{4,6},{5,7},{6,4},{7,5},{8,10},{9,11},{10,... | collective-permute-start | bytes 454664 | tf_op jit(solution)/shard_map/ppermute | solution.py:31
  29.5 7.0 %collective-permute-start.12 = (bf16[16,4736]{1,0:T(8,128)(2,1)S(1)}, bf16[16,4736]{1,0:T(8,128)(2,1)S(1)}, u32[]{:S(2)}, u32[]{:S(2)}) collective-permute-start(bf16[16,4736]{1,0:T(8,128)(2,1)S(1)} %collective-permute-done.7), channel_id=1, source_target_pairs={{0,1},{1,0},{2,3},{3,2},{4,5},{5,4},{6,7},{7,6},{8,9},{9,8},{10,11... | collective-permute-start | bytes 454664 | tf_op jit(solution)/shard_map/ppermute | solution.py:31
  30.9 5.7 %collective-permute-start.11 = (bf16[16,4736]{1,0:T(8,128)(2,1)S(1)}, bf16[16,4736]{1,0:T(8,128)(2,1)S(1)}, u32[]{:S(2)}, u32[]{:S(2)}) collective-permute-start(bf16[16,4736]{1,0:T(8,128)(2,1)S(1)} %collective-permute-done.2._), channel_id=1, source_target_pairs={{0,2},{1,3},{2,0},{3,1},{4,6},{5,7},{6,4},{7,5},{8,10},{9,11},{10,... | collective-permute-start | bytes 454664 | tf_op jit(solution)/shard_map/ppermute | solution.py:31
  31.5 5.2 %collective-permute-start.14 = (bf16[16,4736]{1,0:T(8,128)(2,1)S(1)}, bf16[16,4736]{1,0:T(8,128)(2,1)S(1)}, u32[]{:S(2)}, u32[]{:S(2)}) collective-permute-start(bf16[16,4736]{1,0:T(8,128)(2,1)S(1)} %collective-permute-done.13), channel_id=1, source_target_pairs={{0,1},{1,0},{2,3},{3,2},{4,5},{5,4},{6,7},{7,6},{8,9},{9,8},{10,11... | collective-permute-start | bytes 454664 | tf_op jit(solution)/shard_map/ppermute | solution.py:31
  36.5 16.3 %copy-start.1 = (f32[4096]{0:T(1024)S(1)}, f32[4096]{0:T(1024)}, u32[]{:S(2)}) copy-start(f32[4096]{0:T(1024)} %param.17) | copy-start | bytes 49156
  38.0 4.7 %collective-permute-start.17 = (bf16[128,256]{1,0:T(8,128)(2,1)S(1)}, bf16[128,256]{1,0:T(8,128)(2,1)S(1)}, u32[]{:S(2)}, u32[]{:S(2)}) collective-permute-start(bf16[128,256]{1,0:T(8,128)(2,1)S(1)} %get-tuple-element.49), channel_id=1, source_target_pairs={{0,4},{1,5},{2,6},{3,7},{4,0},{5,1},{6,2},{7,3},{8,12},{9,13},{10,... | collective-permute-start | bytes 196616 | tf_op jit(solution)/shard_map/ppermute | solution.py:31
  38.1 8.2 %collective-permute-start.15 = (bf16[128,256]{1,0:T(8,128)(2,1)S(1)}, bf16[128,256]{1,0:T(8,128)(2,1)S(1)}, u32[]{:S(2)}, u32[]{:S(2)}) collective-permute-start(bf16[128,256]{1,0:T(8,128)(2,1)S(1)} %get-tuple-element.49), channel_id=1, source_target_pairs={{0,8},{1,9},{2,10},{3,11},{4,12},{5,13},{6,14},{7,15},{8,0},{9,1},... | collective-permute-start | bytes 196616 | tf_op jit(solution)/shard_map/ppermute | solution.py:31
  40.3 6.1 %collective-permute-start.16 = (bf16[128,256]{1,0:T(8,128)(2,1)S(1)}, bf16[128,256]{1,0:T(8,128)(2,1)S(1)}, u32[]{:S(2)}, u32[]{:S(2)}) collective-permute-start(bf16[128,256]{1,0:T(8,128)(2,1)S(1)} %get-tuple-element.49), channel_id=1, source_target_pairs={{0,12},{1,13},{2,14},{3,15},{4,8},{5,9},{6,10},{7,11},{8,4},{9,5},... | collective-permute-start | bytes 196616 | tf_op jit(solution)/shard_map/ppermute | solution.py:31
  42.7 6.5 %collective-permute-start.21 = (bf16[2,128,256]{2,1,0:T(8,128)(2,1)S(1)}, bf16[2,128,256]{2,1,0:T(8,128)(2,1)S(1)}, u32[]{:S(2)}, u32[]{:S(2)}) collective-permute-start(bf16[2,128,256]{2,1,0:T(8,128)(2,1)S(1)} %pad_maximum_fusion.1.refs_0_), channel_id=1, source_target_pairs={{0,1},{1,0},{2,3},{3,2},{4,5},{5,4},{6,7},{7,6},{8,9},{9,8},{10,11... | collective-permute-start | bytes 393224 | tf_op jit(solution)/shard_map/ppermute | solution.py:31
  43.8 7.6 %collective-permute-start.22 = (bf16[2,128,256]{2,1,0:T(8,128)(2,1)S(1)}, bf16[2,128,256]{2,1,0:T(8,128)(2,1)S(1)}, u32[]{:S(2)}, u32[]{:S(2)}) collective-permute-start(bf16[2,128,256]{2,1,0:T(8,128)(2,1)S(1)} %pad_maximum_fusion.1.refs_0_), channel_id=1, source_target_pairs={{0,2},{1,3},{2,0},{3,1},{4,6},{5,7},{6,4},{7,5},{8,10},{9,11},{10,... | collective-permute-start | bytes 393224 | tf_op jit(solution)/shard_map/ppermute | solution.py:31
  45.3 7.6 %collective-permute-start.23 = (bf16[2,128,256]{2,1,0:T(8,128)(2,1)S(1)}, bf16[2,128,256]{2,1,0:T(8,128)(2,1)S(1)}, u32[]{:S(2)}, u32[]{:S(2)}) collective-permute-start(bf16[2,128,256]{2,1,0:T(8,128)(2,1)S(1)} %pad_maximum_fusion.1.refs_0_), channel_id=1, source_target_pairs={{0,3},{1,2},{2,1},{3,0},{4,7},{5,6},{6,5},{7,4},{8,11},{9,10},{10,... | collective-permute-start | bytes 393224 | tf_op jit(solution)/shard_map/ppermute | solution.py:31
  46.4 9.7 %collective-permute-start.18 = (bf16[2,128,256]{2,1,0:T(8,128)(2,1)S(1)}, bf16[2,128,256]{2,1,0:T(8,128)(2,1)S(1)}, u32[]{:S(2)}, u32[]{:S(2)}) collective-permute-start(bf16[2,128,256]{2,1,0:T(8,128)(2,1)S(1)} %pad_maximum_fusion.refs_0_), channel_id=1, source_target_pairs={{0,1},{1,0},{2,3},{3,2},{4,5},{5,4},{6,7},{7,6},{8,9},{9,8},{10,11... | collective-permute-start | bytes 393224 | tf_op jit(solution)/shard_map/ppermute | solution.py:31
  47.8 8.3 %collective-permute-start.19 = (bf16[2,128,256]{2,1,0:T(8,128)(2,1)S(1)}, bf16[2,128,256]{2,1,0:T(8,128)(2,1)S(1)}, u32[]{:S(2)}, u32[]{:S(2)}) collective-permute-start(bf16[2,128,256]{2,1,0:T(8,128)(2,1)S(1)} %pad_maximum_fusion.refs_0_), channel_id=1, source_target_pairs={{0,2},{1,3},{2,0},{3,1},{4,6},{5,7},{6,4},{7,5},{8,10},{9,11},{10,... | collective-permute-start | bytes 393224 | tf_op jit(solution)/shard_map/ppermute | solution.py:31
  49.2 6.9 %collective-permute-start.20 = (bf16[2,128,256]{2,1,0:T(8,128)(2,1)S(1)}, bf16[2,128,256]{2,1,0:T(8,128)(2,1)S(1)}, u32[]{:S(2)}, u32[]{:S(2)}) collective-permute-start(bf16[2,128,256]{2,1,0:T(8,128)(2,1)S(1)} %pad_maximum_fusion.refs_0_), channel_id=1, source_target_pairs={{0,3},{1,2},{2,1},{3,0},{4,7},{5,6},{6,5},{7,4},{8,11},{9,10},{10,... | collective-permute-start | bytes 393224 | tf_op jit(solution)/shard_map/ppermute | solution.py:31
  52.8 3.3 %slice-start = ((s8[6291456]{0:T(1024)(128)(4,1)}), s8[4194304]{0:T(1024)(128)(4,1)S(1)}, s32[]{:S(2)}) async-start(s8[6291456]{0:T(1024)(128)(4,1)} %bitcast.34), calls=%async_computation | async-start | bytes 8388608
  52.8 3.8 %slice-start.1 = ((s8[6291456]{0:T(1024)(128)(4,1)}), s8[2097152]{0:T(1024)(128)(4,1)S(1)}, s32[]{:S(2)}) async-start(s8[6291456]{0:T(1024)(128)(4,1)} %bitcast.34), calls=%async_computation.1 | async-start | bytes 4194304
  58.8 6.9 %collective-permute-start.28 = (bf16[2,16,2048]{2,1,0:T(8,128)(2,1)S(1)}, bf16[2,16,2048]{2,1,0:T(8,128)(2,1)S(1)}, u32[]{:S(2)}, u32[]{:S(2)}) collective-permute-start(bf16[2,16,2048]{2,1,0:T(8,128)(2,1)S(1)} %get-tuple-element.64), channel_id=1, source_target_pairs={{0,3},{1,2},{2,1},{3,0},{4,7},{5,6},{6,5},{7,4},{8,11},{9,10},{10,... | collective-permute-start | bytes 393224 | tf_op jit(solution)/shard_map/ppermute | solution.py:31
  59.9 6.4 %collective-permute-start.29 = (bf16[2,16,2048]{2,1,0:T(8,128)(2,1)S(1)}, bf16[2,16,2048]{2,1,0:T(8,128)(2,1)S(1)}, u32[]{:S(2)}, u32[]{:S(2)}) collective-permute-start(bf16[2,16,2048]{2,1,0:T(8,128)(2,1)S(1)} %get-tuple-element.65), channel_id=1, source_target_pairs={{0,1},{1,0},{2,3},{3,2},{4,5},{5,4},{6,7},{7,6},{8,9},{9,8},{10,11... | collective-permute-start | bytes 393224 | tf_op jit(solution)/shard_map/ppermute | solution.py:31
  61.4 5.6 %collective-permute-start.30 = (bf16[2,16,2048]{2,1,0:T(8,128)(2,1)S(1)}, bf16[2,16,2048]{2,1,0:T(8,128)(2,1)S(1)}, u32[]{:S(2)}, u32[]{:S(2)}) collective-permute-start(bf16[2,16,2048]{2,1,0:T(8,128)(2,1)S(1)} %get-tuple-element.66), channel_id=1, source_target_pairs={{0,2},{1,3},{2,0},{3,1},{4,6},{5,7},{6,4},{7,5},{8,10},{9,11},{10,... | collective-permute-start | bytes 393224 | tf_op jit(solution)/shard_map/ppermute | solution.py:31
  62.4 8.2 %collective-permute-start.24 = (bf16[2,16,2048]{2,1,0:T(8,128)(2,1)S(1)}, bf16[2,16,2048]{2,1,0:T(8,128)(2,1)S(1)}, u32[]{:S(2)}, u32[]{:S(2)}) collective-permute-start(bf16[2,16,2048]{2,1,0:T(8,128)(2,1)S(1)} %get-tuple-element.60), channel_id=1, source_target_pairs={{0,3},{1,2},{2,1},{3,0},{4,7},{5,6},{6,5},{7,4},{8,11},{9,10},{10,... | collective-permute-start | bytes 393224 | tf_op jit(solution)/shard_map/ppermute | solution.py:31
  63.4 7.2 %collective-permute-start.25 = (bf16[2,16,2048]{2,1,0:T(8,128)(2,1)S(1)}, bf16[2,16,2048]{2,1,0:T(8,128)(2,1)S(1)}, u32[]{:S(2)}, u32[]{:S(2)}) collective-permute-start(bf16[2,16,2048]{2,1,0:T(8,128)(2,1)S(1)} %get-tuple-element.61), channel_id=1, source_target_pairs={{0,1},{1,0},{2,3},{3,2},{4,5},{5,4},{6,7},{7,6},{8,9},{9,8},{10,11... | collective-permute-start | bytes 393224 | tf_op jit(solution)/shard_map/ppermute | solution.py:31
  65.7 5.0 %collective-permute-start.26 = (bf16[2,16,2048]{2,1,0:T(8,128)(2,1)S(1)}, bf16[2,16,2048]{2,1,0:T(8,128)(2,1)S(1)}, u32[]{:S(2)}, u32[]{:S(2)}) collective-permute-start(bf16[2,16,2048]{2,1,0:T(8,128)(2,1)S(1)} %get-tuple-element.62), channel_id=1, source_target_pairs={{0,2},{1,3},{2,0},{3,1},{4,6},{5,7},{6,4},{7,5},{8,10},{9,11},{10,... | collective-permute-start | bytes 393224 | tf_op jit(solution)/shard_map/ppermute | solution.py:31
  67.1 6.6 %collective-permute-start.31 = (bf16[16,2048]{1,0:T(8,128)(2,1)S(1)}, bf16[16,2048]{1,0:T(8,128)(2,1)S(1)}, u32[]{:S(2)}, u32[]{:S(2)}) collective-permute-start(bf16[16,2048]{1,0:T(8,128)(2,1)S(1)} %get-tuple-element.67), channel_id=1, source_target_pairs={{0,8},{1,9},{2,10},{3,11},{4,12},{5,13},{6,14},{7,15},{8,0},{9,1},... | collective-permute-start | bytes 196616 | tf_op jit(solution)/shard_map/ppermute | solution.py:31
  67.2 6.6 %collective-permute-start.32 = (bf16[16,2048]{1,0:T(8,128)(2,1)S(1)}, bf16[16,2048]{1,0:T(8,128)(2,1)S(1)}, u32[]{:S(2)}, u32[]{:S(2)}) collective-permute-start(bf16[16,2048]{1,0:T(8,128)(2,1)S(1)} %get-tuple-element.68), channel_id=1, source_target_pairs={{0,12},{1,13},{2,14},{3,15},{4,8},{5,9},{6,10},{7,11},{8,4},{9,5},... | collective-permute-start | bytes 196616 | tf_op jit(solution)/shard_map/ppermute | solution.py:31
  70.7 4.3 %collective-permute-start.27 = (bf16[16,2048]{1,0:T(8,128)(2,1)S(1)}, bf16[16,2048]{1,0:T(8,128)(2,1)S(1)}, u32[]{:S(2)}, u32[]{:S(2)}) collective-permute-start(bf16[16,2048]{1,0:T(8,128)(2,1)S(1)} %slice_bitcast_fusion.2), channel_id=1, source_target_pairs={{0,4},{1,5},{2,6},{3,7},{4,0},{5,1},{6,2},{7,3},{8,12},{9,13},{10,... | collective-permute-start | bytes 196616 | tf_op jit(solution)/shard_map/ppermute | solution.py:31
  75.1 1.3 %collective-permute-start.33 = (bf16[8,2048]{1,0:T(8,128)(2,1)S(1)}, bf16[8,2048]{1,0:T(8,128)(2,1)S(1)}, u32[]{:S(2)}, u32[]{:S(2)}) collective-permute-start(bf16[8,2048]{1,0:T(8,128)(2,1)S(1)} %get-tuple-element.70), channel_id=1, source_target_pairs={{0,16},{16,0},{1,17},{17,1},{2,18},{18,2},{3,19},{19,3},{4,20},{20... | collective-permute-start | bytes 98312 | tf_op jit(solution)/shard_map/ppermute | solution.py:616
